TPU v7x, 32 devices: a whole 2x2x4 slice. The times are simulated.
32 devices in a mesh: grp: 4 (over x, core), blk: 8 (over z, y).
Axes of the slice: x: 2, y: 2, z: 4, core: 2. Of those that a mesh axis runs over, the one named last changes fastest.
Arguments:
- fine_pops: float32 [4, 19, 128, 256], P('grp', None, 'blk'), may hold values from 0.38 to 8.7, as said below
- fine_solid: float32 [4, 128, 256], P('grp', 'blk'), may hold values from 0.05 to 0.6
- coarse_pops: float32 [4, 19, 64, 256], P('grp', None, 'blk'), may hold values from 0.38 to 8.7, as said below
- coarse_solid: float32 [4, 64, 256], P('grp', 'blk'), may hold values from 0.05 to 0.6
- coarse_slot: int32 [4], replicated, may hold values from 0 to 15, as said below
Outputs:
- fine_out: float32 [4, 19, 128, 256], P('grp', None, 'blk')
- coarse_out: float32 [4, 19, 64, 256], P('grp', None, 'blk')
Inputs may be any that keep to these rules, and one draw needn't show every extreme that they name: `fine_pops`: each population is between 0.7 and 1.3 times 20 w_i. `coarse_pops`: each population is between 0.7 and 1.3 times 20 w_i. `coarse_slot`: the 4 entries are distinct, and 15 is one of them.
All inputs are finite; a program needn't handle non-finite values.
Results may differ from a plain program's by a relative error of at most 0.0001.
Values sent between devices are 32-bit elements; how exact they have to be, the bound alone decides.
No kernel may reach another device: no remote copies, remote signals or barrier semaphores. Data moves between devices by JAX's collectives and lax.ppermute only.
A program may use at most 128 MiB of HBM per device.

v0:
```python
import jax
import jax.numpy as jnp
import numpy as np
from jax import lax
from jax.sharding import PartitionSpec as P

BX = 16


lattice_vel = np.array(
    [
        [0, 0, 0],
        [1, 0, 0],
        [-1, 0, 0],
        [0, 1, 0],
        [0, -1, 0],
        [0, 0, 1],
        [0, 0, -1],
        [1, 1, 0],
        [-1, -1, 0],
        [1, -1, 0],
        [-1, 1, 0],
        [1, 0, 1],
        [-1, 0, -1],
        [1, 0, -1],
        [-1, 0, 1],
        [0, 1, 1],
        [0, -1, -1],
        [0, 1, -1],
        [0, -1, 1],
    ]
)
lattice_weight = np.array([1.0 / 3.0] + [1.0 / 18.0] * 6 + [1.0 / 36.0] * 12)
opposite_index = [0, 2, 1, 4, 3, 6, 5, 8, 7, 10, 9, 12, 11, 14, 13, 16, 15, 18, 17]
tau_fine = 0.6
tau_coarse = 0.55


def with_halo(block, sides, width):
    for axis, dim in sides:
        count = lax.axis_size(axis)
        forward = [(i, i + 1) for i in range(count - 1)]
        forward.append((count - 1, 0))
        backward = [(target, source) for source, target in forward]
        low = lax.ppermute(
            lax.slice_in_dim(block, block.shape[dim] - width, None, axis=dim), axis, forward
        )
        high = lax.ppermute(lax.slice_in_dim(block, 0, width, axis=dim), axis, backward)
        block = jnp.concatenate([low, block, high], axis=dim)
    return block


def spread_table(table, populations):
    return jnp.asarray(table, populations.dtype).reshape((19,) + (1,) * (populations.ndim - 1))


def equilibrium(populations):
    density = jnp.sum(populations, axis=0)
    velocity = [
        jnp.sum(spread_table(lattice_vel[:, k], populations) * populations, axis=0) / density
        for k in range(3)
    ]
    projected = spread_table(lattice_vel[:, 0], populations) * velocity[0]
    projected = projected + spread_table(lattice_vel[:, 1], populations) * velocity[1]
    projected = projected + spread_table(lattice_vel[:, 2], populations) * velocity[2]
    speed_sq = velocity[0] * velocity[0] + velocity[1] * velocity[1] + velocity[2] * velocity[2]
    return (
        spread_table(lattice_weight, populations)
        * density
        * (1.0 + 3.0 * projected + 4.5 * projected * projected - 1.5 * speed_sq)
    )


def collide_cells(populations, solid, relax):
    equil = equilibrium(populations)
    mirrored = jnp.stack([populations[j] for j in opposite_index])
    return (
        populations
        - (1.0 - solid) * (populations - equil) / relax
        + solid * (mirrored - populations)
    )


def stream_cells(collided):
    xlength = collided.shape[1]
    zlength = collided.shape[2] // BX
    moved = []
    padded = with_halo(collided, (("blk", 1),), 1)
    for j in range(19):
        offset = 1 - int(lattice_vel[j, 0])
        moved.append(padded[j, offset : offset + xlength])
    rolled = []
    for j in range(19):
        planes = moved[j].reshape(xlength, BX, zlength)
        planes = jnp.roll(planes, (int(lattice_vel[j, 1]), int(lattice_vel[j, 2])), axis=(1, 2))
        rolled.append(planes.reshape(xlength, BX * zlength))
    return jnp.stack(rolled)


def per_device(fine_pops, fine_solid, coarse_pops, coarse_solid, coarse_slot):
    populations = fine_pops[0]
    solid = fine_solid[0]
    for substep in range(2):
        populations = stream_cells(collide_cells(populations, solid, tau_fine))
    xlength = populations.shape[1]
    zlength = populations.shape[2] // BX
    averaged = populations.reshape(19, xlength // 2, 2, BX // 2, 2, zlength // 2, 2).mean(
        axis=(2, 4, 6)
    )
    equil = equilibrium(averaged)
    restricted = (equil + 2.0 * tau_coarse / tau_fine * (averaged - equil)).reshape(
        19, xlength // 2, BX // 2 * (zlength // 2)
    )
    group = lax.axis_index("grp")
    groups = lax.axis_size("grp")
    slot_iota = jnp.arange(groups, dtype=jnp.int32)
    own_code = jnp.sum(jnp.where(slot_iota == group, coarse_slot, 0))
    wanted = group * 4 + jnp.arange(4, dtype=jnp.int32)
    selector = (slot_iota == own_code // 4).astype(jnp.float32)
    outgoing = selector[:, None, None, None] * restricted[None]
    incoming = lax.all_to_all(outgoing, "grp", split_axis=0, concat_axis=0, tiled=True)
    matches = (coarse_slot[None, :] == wanted[:, None]).astype(jnp.float32)
    arrived = jnp.sum(matches[:, :, None, None, None] * incoming[None], axis=1)
    present = jnp.any(coarse_slot[None, :] == wanted[:, None], axis=1)
    coarse = coarse_pops[0].reshape(19, xlength // 2, BX, zlength)
    half_y = BX // 2
    half_z = zlength // 2
    for quadrant in range(4):
        low_y = quadrant // 2 * half_y
        low_z = quadrant % 2 * half_z
        region = coarse[:, :, low_y : low_y + half_y, low_z : low_z + half_z]
        incoming_tile = arrived[quadrant].reshape(19, xlength // 2, half_y, half_z)
        coarse = coarse.at[:, :, low_y : low_y + half_y, low_z : low_z + half_z].set(
            jnp.where(present[quadrant], incoming_tile, region)
        )
    coarse = coarse.reshape(19, xlength // 2, BX * zlength)
    coarse = stream_cells(collide_cells(coarse, coarse_solid[0], tau_coarse))
    return (populations[None], coarse[None])


def solution(mesh):
    placed = (
        P("grp", None, "blk", None),
        P("grp", "blk", None),
        P("grp", None, "blk", None),
        P("grp", "blk", None),
        P(),
    )
    return jax.shard_map(
        per_device,
        mesh=mesh,
        in_specs=placed,
        out_specs=(P("grp", None, "blk", None), P("grp", None, "blk", None)),
        check_vma=False,
    )
```

profile of v0, /device:TPU:0, one launch (start us, length us, event | category | flops | bytes accessed | tf_op | source)
XLA Modules:
  0.0 374.5 jit_solution(4358338910804519490)
XLA Ops:
  18.6 6.1 %collective-permute-start.1 = (f32[19,1,256]{2,1,0:T(1,128)S(1)}, f32[19,1,256]{2,1,0:T(1,128)S(1)}, u32[]{:S(2)}, u32[]{:S(2)}) collective-permute-start(f32[19,1,256]{2,1,0:T(1,128)S(1)} %get-tuple-element.161), channel_id=1, source_target_pairs={{1,0},{2,1},{3,2},{4,3},{5,4},{6,5},{7,6},{0,7},{9,8},{10,9},{11,1... | collective-permute-start | bytes 58376 | tf_op jit(solution)/shard_map/ppermute | solution.py:48
  56.7 2.2 stack.78
  61.9 2.2 stack.68
  64.1 1.6 stack_reshape.172
  65.7 2.2 stack.67
  68.0 1.6 stack_reshape.171
  69.6 2.3 stack.66
  71.8 1.6 stack_reshape.170
  73.4 2.2 stack.65
  75.6 1.6 stack_reshape.169
  77.3 4.7 %collective-permute-start.3 = (f32[19,1,256]{2,1,0:T(1,128)}, f32[19,1,256]{2,1,0:T(1,128)S(1)}, u32[]{:S(2)}, u32[]{:S(2)}) collective-permute-start(f32[19,1,256]{2,1,0:T(1,128)} %get-tuple-element.144), channel_id=1, source_target_pairs={{1,0},{2,1},{3,2},{4,3},{5,4},{6,5},{7,6},{0,7},{9,8},{10,9},{11,1... | collective-permute-start | bytes 58376 | tf_op jit(solution)/shard_map/ppermute | solution.py:48
  122.0 2.0 stack.63
  124.0 2.0 stack.64
  126.0 2.5 constant_dynamic-update-slice_fusion.93
  128.5 2.4 constant_dynamic-update-slice_fusion.92
  130.8 2.3 constant_dynamic-update-slice_fusion.91
  133.1 2.3 constant_dynamic-update-slice_fusion.90
  135.4 2.3 constant_dynamic-update-slice_fusion.89
  137.8 2.3 constant_dynamic-update-slice_fusion.88
  140.1 2.3 constant_dynamic-update-slice_fusion.87
  142.4 2.4 constant_dynamic-update-slice_fusion.86
  144.8 2.3 constant_dynamic-update-slice_fusion.85
  147.1 2.3 constant_dynamic-update-slice_fusion.84
  158.2 8.0 %reduce_sum.357 = f32[19,8,8,8]{3,2,1,0:T(8,128)S(1)} reduce(f32[19,8,2,8,2,8,2]{6,5,4,3,2,1,0:T(8,128)} %constant_dynamic-update-slice_fusion.76, f32[]{:T(128)} %constant.161.clone.1), dimensions={2,4,6}, to_apply=%region_9.10 | reduce | flops 68096 | bytes 350212 | tf_op jit(solution)/shard_map/reduce_sum | solution.py:107
  170.6 3.6 all-to-all-start
  190.3 20.9 %scatter.14 = f32[19,8,16,16]{3,2,1,0:T(8,128)S(1)} dynamic-update-slice(f32[19,8,16,16]{3,2,1,0:T(8,128)S(1)} %reshape_squeeze.200, f32[19,8,8,8]{3,2,1,0:T(8,128)S(1)} %slice_select_fusion.3, s32[]{:T(128)} %constant.169.clone.1, s32[]{:T(128)} %constant.169.clone.1, s32[]{:T(128)} %constant.169.clone.1, s32[]{:T(128)} %constant.169.clone.1) | dynamic-update-slice | bytes 77828 | tf_op jit(solution)/shard_map/scatter | solution.py:133
  212.1 2.8 fusion
  214.9 62.0 %scatter.15 = f32[19,8,16,16]{3,2,1,0:T(8,128)S(1)} dynamic-update-slice(f32[19,8,16,16]{3,2,1,0:T(8,128)S(1)} %scatter.14, f32[19,8,8,8]{3,2,1,0:T(8,128)S(1)} %fusion, s32[]{:T(128)} %constant.169.clone.1, s32[]{:T(128)} %constant.169.clone.1, s32[]{:T(128)} %bitcast.36, s32[]{:T(128)} %bitcast.37) | dynamic-update-slice | bytes 77828 | tf_op jit(solution)/shard_map/scatter | solution.py:133
  279.3 18.8 %scatter.16 = f32[19,8,16,16]{3,2,1,0:T(8,128)S(1)} dynamic-update-slice(f32[19,8,16,16]{3,2,1,0:T(8,128)S(1)} %scatter.15, f32[19,8,8,8]{3,2,1,0:T(8,128)S(1)} %slice_select_fusion.1, s32[]{:T(128)} %constant.169.clone.1, s32[]{:T(128)} %constant.169.clone.1, s32[]{:T(128)} %constant.177.clone.1, s32[]{:T(128)} %constant.169.clone.1) | dynamic-update-slice | bytes 77828 | tf_op jit(solution)/shard_map/scatter | solution.py:133
  299.0 59.0 %scatter.19 = f32[19,8,16,16]{3,2,1,0:T(8,128)S(1)} dynamic-update-slice(f32[19,8,16,16]{3,2,1,0:T(8,128)S(1)} %scatter.16, f32[19,8,8,8]{3,2,1,0:T(8,128)S(1)} %slice_select_fusion, s32[]{:T(128)} %constant.169.clone.1, s32[]{:T(128)} %constant.169.clone.1, s32[]{:T(128)} %constant.177.clone.1, s32[]{:T(128)} %constant.177.clone.1) | dynamic-update-slice | bytes 77828 | tf_op jit(solution)/shard_map/scatter | solution.py:133
  361.9 5.0 %collective-permute-start.5 = (f32[19,1,256]{2,1,0:T(1,128)S(1)}, f32[19,1,256]{2,1,0:T(1,128)S(1)}, u32[]{:S(2)}, u32[]{:S(2)}) collective-permute-start(f32[19,1,256]{2,1,0:T(1,128)S(1)} %get-tuple-element.185), channel_id=1, source_target_pairs={{1,0},{2,1},{3,2},{4,3},{5,4},{6,5},{7,6},{0,7},{9,8},{10,9},{11,1... | collective-permute-start | bytes 58376 | tf_op jit(solution)/shard_map/ppermute | solution.py:48
  366.9 1.7 collective-permute-done.4
  (497 shorter events, 131.2 us)
Async XLA Ops:
  0.6 41.6 %copy-start.26 = (f32[19]{0:T(128)S(1)}, f32[19]{0:T(128)}, u32[]{:S(2)}) copy-start(f32[19]{0:T(128)} %constant.181.clone) | copy-start | bytes 232
  0.6 41.6 %copy-start.28 = (f32[19]{0:T(128)S(1)}, f32[19]{0:T(128)}, u32[]{:S(2)}) copy-start(f32[19]{0:T(128)} %constant.182.clone) | copy-start | bytes 232
  0.7 41.6 %copy-start.30 = (f32[19]{0:T(128)S(1)}, f32[19]{0:T(128)}, u32[]{:S(2)}) copy-start(f32[19]{0:T(128)} %constant.183.clone) | copy-start | bytes 232
  0.7 41.7 %copy-start.32 = (f32[19]{0:T(128)S(1)}, f32[19]{0:T(128)}, u32[]{:S(2)}) copy-start(f32[19]{0:T(128)} %constant.184.clone) | copy-start | bytes 232
  0.7 41.7 %copy-start.13 = (f32[1,16,256]{2,1,0:T(8,128)S(1)}, f32[1,16,256]{2,1,0:T(8,128)}, u32[]{:S(2)}) copy-start(f32[1,16,256]{2,1,0:T(8,128)} %param.42) | copy-start | bytes 49156
  18.6 17.2 %collective-permute-start.1 = (f32[19,1,256]{2,1,0:T(1,128)S(1)}, f32[19,1,256]{2,1,0:T(1,128)S(1)}, u32[]{:S(2)}, u32[]{:S(2)}) collective-permute-start(f32[19,1,256]{2,1,0:T(1,128)S(1)} %get-tuple-element.161), channel_id=1, source_target_pairs={{1,0},{2,1},{3,2},{4,3},{5,4},{6,5},{7,6},{0,7},{9,8},{10,9},{11,1... | collective-permute-start | bytes 58376 | tf_op jit(solution)/shard_map/ppermute | solution.py:48
  24.6 11.1 %collective-permute-start = (f32[19,1,256]{2,1,0:T(1,128)S(1)}, f32[19,1,256]{2,1,0:T(1,128)S(1)}, u32[]{:S(2)}, u32[]{:S(2)}) collective-permute-start(f32[19,1,256]{2,1,0:T(1,128)S(1)} %get-tuple-element.160), channel_id=1, source_target_pairs={{0,1},{1,2},{2,3},{3,4},{4,5},{5,6},{6,7},{7,0},{8,9},{9,10},{10,1... | collective-permute-start | bytes 58376 | tf_op jit(solution)/shard_map/ppermute | solution.py:45
  47.2 34.8 %collective-permute-start.2 = (f32[19,1,256]{2,1,0:T(1,128)}, f32[19,1,256]{2,1,0:T(1,128)}, u32[]{:S(2)}, u32[]{:S(2)}) collective-permute-start(f32[19,1,256]{2,1,0:T(1,128)} %get-tuple-element.145), channel_id=1, source_target_pairs={{0,1},{1,2},{2,3},{3,4},{4,5},{5,6},{6,7},{7,0},{8,9},{9,10},{10,1... | collective-permute-start | bytes 58376 | tf_op jit(solution)/shard_map/ppermute | solution.py:45
  77.3 6.4 %collective-permute-start.3 = (f32[19,1,256]{2,1,0:T(1,128)}, f32[19,1,256]{2,1,0:T(1,128)S(1)}, u32[]{:S(2)}, u32[]{:S(2)}) collective-permute-start(f32[19,1,256]{2,1,0:T(1,128)} %get-tuple-element.144), channel_id=1, source_target_pairs={{1,0},{2,1},{3,2},{4,3},{5,4},{6,5},{7,6},{0,7},{9,8},{10,9},{11,1... | collective-permute-start | bytes 58376 | tf_op jit(solution)/shard_map/ppermute | solution.py:48
  126.0 24.5 %copy-start.4 = (f32[1,8,2,8,2,8,2]{6,5,4,3,2,1,0:T(8,128)S(1)}, f32[1,8,2,8,2,8,2]{6,5,4,3,2,1,0:T(8,128)}, u32[]{:S(2)}) copy-start(f32[1,8,2,8,2,8,2]{6,5,4,3,2,1,0:T(8,128)} %stack.74) | copy-start | bytes 49156
  126.0 25.8 %copy-start.3 = (f32[1,8,2,8,2,8,2]{6,5,4,3,2,1,0:T(8,128)S(1)}, f32[1,8,2,8,2,8,2]{6,5,4,3,2,1,0:T(8,128)}, u32[]{:S(2)}) copy-start(f32[1,8,2,8,2,8,2]{6,5,4,3,2,1,0:T(8,128)} %stack.75) | copy-start | bytes 49156
  126.0 26.9 %copy-start.2 = (f32[1,8,2,8,2,8,2]{6,5,4,3,2,1,0:T(8,128)S(1)}, f32[1,8,2,8,2,8,2]{6,5,4,3,2,1,0:T(8,128)}, u32[]{:S(2)}) copy-start(f32[1,8,2,8,2,8,2]{6,5,4,3,2,1,0:T(8,128)} %stack.76) | copy-start | bytes 49156
  126.0 27.9 %copy-start.1 = (f32[1,8,2,8,2,8,2]{6,5,4,3,2,1,0:T(8,128)S(1)}, f32[1,8,2,8,2,8,2]{6,5,4,3,2,1,0:T(8,128)}, u32[]{:S(2)}) copy-start(f32[1,8,2,8,2,8,2]{6,5,4,3,2,1,0:T(8,128)} %stack.77) | copy-start | bytes 49156
  126.0 29.0 %copy-start = (f32[1,8,2,8,2,8,2]{6,5,4,3,2,1,0:T(8,128)S(1)}, f32[1,8,2,8,2,8,2]{6,5,4,3,2,1,0:T(8,128)}, u32[]{:S(2)}) copy-start(f32[1,8,2,8,2,8,2]{6,5,4,3,2,1,0:T(8,128)} %stack.78) | copy-start | bytes 49156
  150.5 24.3 %copy-start.17 = (f32[1,16,256]{2,1,0:T(8,128)S(1)}, f32[1,16,256]{2,1,0:T(8,128)}, u32[]{:S(2)}) copy-start(f32[1,16,256]{2,1,0:T(8,128)} %stack_reshape.170) | copy-start | bytes 49156
  150.5 24.9 %copy-start.16 = (f32[1,16,256]{2,1,0:T(8,128)S(1)}, f32[1,16,256]{2,1,0:T(8,128)}, u32[]{:S(2)}) copy-start(f32[1,16,256]{2,1,0:T(8,128)} %stack_reshape.171) | copy-start | bytes 49156
  150.5 25.5 %copy-start.15 = (f32[1,16,256]{2,1,0:T(8,128)S(1)}, f32[1,16,256]{2,1,0:T(8,128)}, u32[]{:S(2)}) copy-start(f32[1,16,256]{2,1,0:T(8,128)} %stack_reshape.172) | copy-start | bytes 49156
  150.5 30.1 %copy-start.23 = (f32[1,16,256]{2,1,0:T(8,128)S(1)}, f32[1,16,256]{2,1,0:T(8,128)}, u32[]{:S(2)}) copy-start(f32[1,16,256]{2,1,0:T(8,128)} %stack_reshape.176) | copy-start | bytes 49156
  150.5 30.7 %copy-start.22 = (f32[1,16,256]{2,1,0:T(8,128)S(1)}, f32[1,16,256]{2,1,0:T(8,128)}, u32[]{:S(2)}) copy-start(f32[1,16,256]{2,1,0:T(8,128)} %stack_reshape.177) | copy-start | bytes 49156
  150.5 31.3 %copy-start.21 = (f32[1,16,256]{2,1,0:T(8,128)S(1)}, f32[1,16,256]{2,1,0:T(8,128)}, u32[]{:S(2)}) copy-start(f32[1,16,256]{2,1,0:T(8,128)} %stack_reshape.178) | copy-start | bytes 49156
  150.6 31.9 %copy-start.20 = (f32[1,16,256]{2,1,0:T(8,128)S(1)}, f32[1,16,256]{2,1,0:T(8,128)}, u32[]{:S(2)}) copy-start(f32[1,16,256]{2,1,0:T(8,128)} %stack_reshape.179) | copy-start | bytes 49156
  150.6 32.5 %copy-start.19 = (f32[1,16,256]{2,1,0:T(8,128)S(1)}, f32[1,16,256]{2,1,0:T(8,128)}, u32[]{:S(2)}) copy-start(f32[1,16,256]{2,1,0:T(8,128)} %stack_reshape.180) | copy-start | bytes 49156
  150.6 33.1 %copy-start.14 = (f32[1,16,256]{2,1,0:T(8,128)S(1)}, f32[1,16,256]{2,1,0:T(8,128)}, u32[]{:S(2)}) copy-start(f32[1,16,256]{2,1,0:T(8,128)} %stack_reshape.181) | copy-start | bytes 49156
  158.2 199.8 %copy-start.27 = (f32[19]{0:T(128)S(1)}, f32[19]{0:T(128)}, u32[]{:S(2)}) copy-start(f32[19]{0:T(128)} %constant.181.clone) | copy-start | bytes 232
  158.2 199.8 %copy-start.29 = (f32[19]{0:T(128)S(1)}, f32[19]{0:T(128)}, u32[]{:S(2)}) copy-start(f32[19]{0:T(128)} %constant.182.clone) | copy-start | bytes 232
  158.2 199.8 %copy-start.31 = (f32[19]{0:T(128)S(1)}, f32[19]{0:T(128)}, u32[]{:S(2)}) copy-start(f32[19]{0:T(128)} %constant.183.clone) | copy-start | bytes 232
  166.2 195.3 %copy-start.24 = (f32[1,8,256]{2,1,0:T(8,128)S(1)}, f32[1,8,256]{2,1,0:T(8,128)}, u32[]{:S(2)}) copy-start(f32[1,8,256]{2,1,0:T(8,128)} %param.44) | copy-start | bytes 24580
  166.2 195.3 %copy-start.25 = (f32[8,256]{1,0:T(8,128)S(1)}, f32[8,256]{1,0:T(8,128)}, u32[]{:S(2)}) copy-start(f32[8,256]{1,0:T(8,128)} %subtract_bitcast_fusion.1) | copy-start | bytes 24580
  166.3 195.3 %copy-start.33 = (f32[19]{0:T(128)S(1)}, f32[19]{0:T(128)}, u32[]{:S(2)}) copy-start(f32[19]{0:T(128)} %constant.184.clone) | copy-start | bytes 232
  170.6 15.5 %all-to-all-start = ((f32[4,1,9728]{2,1,0:T(1,128)}), f32[4,1,9728]{2,1,0:T(1,128)S(1)}, u32[]{:S(2)}, u32[]{:S(2)}) async-start(f32[4,1,9728]{2,1,0:T(1,128)} %reshape.628), calls=%async_computation | async-start | bytes 311296 | tf_op jit(solution)/shard_map/all_to_all | solution.py:121
  361.8 6.8 %collective-permute-start.4 = (f32[19,1,256]{2,1,0:T(1,128)S(1)}, f32[19,1,256]{2,1,0:T(1,128)S(1)}, u32[]{:S(2)}, u32[]{:S(2)}) collective-permute-start(f32[19,1,256]{2,1,0:T(1,128)S(1)} %get-tuple-element.186), channel_id=1, source_target_pairs={{0,1},{1,2},{2,3},{3,4},{4,5},{5,6},{6,7},{7,0},{8,9},{9,10},{10,1... | collective-permute-start | bytes 58376 | tf_op jit(solution)/shard_map/ppermute | solution.py:45
  361.9 7.1 %collective-permute-start.5 = (f32[19,1,256]{2,1,0:T(1,128)S(1)}, f32[19,1,256]{2,1,0:T(1,128)S(1)}, u32[]{:S(2)}, u32[]{:S(2)}) collective-permute-start(f32[19,1,256]{2,1,0:T(1,128)S(1)} %get-tuple-element.185), channel_id=1, source_target_pairs={{1,0},{2,1},{3,2},{4,3},{5,4},{6,5},{7,6},{0,7},{9,8},{10,9},{11,1... | collective-permute-start | bytes 58376 | tf_op jit(solution)/shard_map/ppermute | solution.py:48
  (10 other events, 52.4 us)
where the time goes:
time: 378 us; the launch traced here: 375 us
  local copies, waits for them, and re-layouts  299 us (79%)
  other arithmetic  48.6 us (13%)
  starting transfers between devices  19.5 us (5%)
  between operations  5.75 us (2%)
    scatter x4, local copies, waits for them, and re-layouts, per_device(): coarse.at[:, :, low_y:low_y + half_y, low_z:low_z + half_z]  161 us
    unnamed x182, local copies, waits for them, and re-layouts  61.8 us
    another operation x71, local copies, waits for them, and re-layouts, stream_cells(): return jnp.stack(rolled)  49.1 us
    concatenate x60, other arithmetic, stream_cells(): jnp.roll(planes, (int(lattice_vel[j, 1]), int(lattice_vel[j, 2])), axis=(...  16.9 us
    ppermute x3, starting transfers between devices, with_halo(): lax.ppermute(lax.slice_in_dim(block, 0, width, axis=dim), axis, backward)  15.8 us
    another operation x48, local copies, waits for them, and re-layouts, stream_cells(): planes = moved[j].reshape(xlength, BX, zlength)  9.85 us
    reduce_sum x1, other arithmetic, per_device(): populations.reshape(19, xlength // 2, 2, BX // 2, 2, zlength // 2, 2)  8.01 us
  transfers between devices with their start and end apart: 7, of which 2 were waited for; matrix products, arithmetic and copies ran while one was open for 14% of the time, Pallas kernels for 0%

commit v1 on v0

v1 whole, which is shorter than its diff:
```python
import jax
import jax.numpy as jnp
import numpy as np
from jax import lax
from jax.experimental import pallas as pl
from jax.experimental.pallas import tpu as pltpu
from jax.sharding import PartitionSpec as P

VEL = np.array(
    [
        [0, 0, 0],
        [1, 0, 0],
        [-1, 0, 0],
        [0, 1, 0],
        [0, -1, 0],
        [0, 0, 1],
        [0, 0, -1],
        [1, 1, 0],
        [-1, -1, 0],
        [1, -1, 0],
        [-1, 1, 0],
        [1, 0, 1],
        [-1, 0, -1],
        [1, 0, -1],
        [-1, 0, 1],
        [0, 1, 1],
        [0, -1, -1],
        [0, 1, -1],
        [0, -1, 1],
    ]
)
NPOP = 19
BX = 16
TAU_FINE = 0.6
TAU_COARSE = 0.55
RESCALE = 2.0 * TAU_COARSE / TAU_FINE

ROWS, LANES = 8, 128
TILE = (ROWS, LANES)
VMEM = pltpu.VMEM


def row_ids():
    return lax.broadcasted_iota(jnp.int32, TILE, 0)


def lane_ids():
    return lax.broadcasted_iota(jnp.int32, TILE, 1)


def roll_rows(tile, shift):
    return pltpu.roll(tile, shift % ROWS, 0)


def roll_lanes(tile, shift):
    return pltpu.roll(tile, shift % LANES, 1)


def moments(f, scale):
    minus = [f[i] - f[i + 1] for i in range(1, NPOP, 2)]
    plus = [f[i] + f[i + 1] for i in range(1, NPOP, 2)]
    rho = ((f[0] + plus[0]) + (plus[1] + plus[2])) + (
        (plus[3] + plus[4]) + (plus[5] + plus[6])
    ) + (plus[7] + plus[8])
    jx = (minus[0] + minus[3]) + (minus[4] + minus[5]) + minus[6]
    jy = (minus[1] + minus[3]) - (minus[4] - minus[7]) + minus[8]
    jz = (minus[2] + minus[5]) - (minus[6] - minus[7]) - minus[8]
    inverse = 1.5 / rho
    ux, uy, uz = jx * inverse, jy * inverse, jz * inverse
    amount = scale(rho)
    base = amount * (1.0 - (2.0 / 3.0) * (ux * ux + uy * uy + uz * uz))
    directions = [ux, uy, uz, ux + uy, ux - uy, ux + uz, ux - uz, uy + uz, uy - uz]
    base_axis, base_diag = base * (1.0 / 18.0), base * (1.0 / 36.0)
    amount_axis, amount_diag = amount * (1.0 / 9.0), amount * (1.0 / 18.0)
    pairs = []
    for k, along in enumerate(directions):
        odd = (amount_axis if k < 3 else amount_diag) * along
        pairs.append(((base_axis if k < 3 else base_diag) + odd * along, odd))
    return base * (1.0 / 3.0), pairs, plus, minus


def collide(f, solid, tau):
    rate = (1.0 - solid) * (1.0 / tau)
    rest, pairs, plus, minus = moments(f, lambda rho: rate * rho)
    keep = 1.0 - rate
    half = 0.5 * keep
    half_odd = half - solid
    out = [keep * f[0] + rest]
    for (even, odd), p, m in zip(pairs, plus, minus):
        symmetric = half * p + even
        antisymmetric = half_odd * m + odd
        out += [symmetric + antisymmetric, symmetric - antisymmetric]
    return out


def restrict(f):
    rest, pairs, _, _ = moments(f, lambda rho: (1.0 - RESCALE) * rho)
    out = [RESCALE * f[0] + rest]
    for k, (even, odd) in enumerate(pairs):
        out += [RESCALE * f[2 * k + 1] + (even + odd), RESCALE * f[2 * k + 2] + (even - odd)]
    return out


def shift_plane(halves, cy, cz):
    lane = lane_ids()
    if cz:
        edge = lane % BX == (0 if cz > 0 else BX - 1)
        halves = [
            jnp.where(
                edge,
                roll_lanes(v, BX * cy + cz - BX * cz),
                roll_lanes(v, BX * cy + cz),
            )
            for v in halves
        ]
    elif cy:
        halves = [roll_lanes(v, BX * cy) for v in halves]
    if cy:
        carried = lane < BX if cy > 0 else lane >= LANES - BX
        halves = [
            jnp.where(carried, halves[1], halves[0]),
            jnp.where(carried, halves[0], halves[1]),
        ]
    return halves


def shift_ring(tiles, cx):
    if not cx:
        return tiles
    row = row_ids()
    turned = [roll_rows(t, cx) for t in tiles]
    if len(tiles) == 1:
        return turned
    edge = row == (0 if cx > 0 else ROWS - 1)
    n = len(tiles)
    return [jnp.where(edge, turned[(i - cx) % n], turned[i]) for i in range(n)]


def stream_ring(ring):
    out = [[[], []] for _ in ring]
    for i in range(NPOP):
        cx, cy, cz = (int(c) for c in VEL[i])
        moved = [shift_plane([tile[0][i], tile[1][i]], cy, cz) for tile in ring]
        for h in range(2):
            for t, v in enumerate(shift_ring([m[h] for m in moved], cx)):
                out[t][h].append(v)
    return out


def squeeze(halves):
    lane = lane_ids()
    low, high = (v + roll_lanes(v, -1) for v in halves)
    both = jnp.where(lane % 2 == 1, roll_lanes(high, 1), low)
    return both + roll_lanes(both, -BX)


def pair_up(first, second):
    if second is None:
        return first
    return jnp.where(lane_ids() // BX % 2 == 1, roll_lanes(second, BX), first)


def spread(tile, which):
    lane = lane_ids()
    y, z = lane // BX, lane % BX
    source = 2 * BX * (y % 4) + BX * which + 2 * (z % 8) + y // 4
    return jnp.take_along_axis(tile, source, axis=1, mode="promise_in_bounds")


def half_lanes(h):
    return pl.ds(h * LANES, LANES)


def pack_kernel(fine, solid, coarse, coarse_solid, own, high, low, strip, rim, sem):
    planes = fine.shape[2]
    coarse_planes = coarse.shape[2]
    copies = []

    def bring(source, target):
        copies.append(pltpu.make_async_copy(source, target, sem.at[len(copies)]))
        copies[-1].start()

    for first, row in ((0, 0), (planes - 4, 4)):
        bring(fine.at[0, :, pl.ds(first, 4), :], strip.at[pl.ds(0, NPOP), pl.ds(row, 4), :])
        bring(solid.at[0, pl.ds(first, 4), :], strip.at[NPOP, pl.ds(row, 4), :])
    for side, plane in ((0, 0), (1, coarse_planes - 1)):
        bring(coarse.at[0, :, pl.ds(plane, 1), :], rim.at[side, pl.ds(0, NPOP)])
        bring(coarse_solid.at[0, pl.ds(plane, 1), :], rim.at[side, NPOP])
    for copy in copies[:4]:
        copy.wait()
    upper = row_ids() < 4
    for h in range(2):
        at = half_lanes(h)
        s = strip[NPOP, :, at]
        out = collide([strip[i, :, at] for i in range(NPOP)], s, TAU_FINE)
        for i, v in enumerate(out + [s]):
            own[i, h] = v
    for i in range(NPOP + 1):
        first, second = own[i, 0], roll_rows(own[i, 1], 4)
        high[i] = jnp.where(upper, second, first)
        low[i] = jnp.where(upper, first, second)
    for copy in copies[4:]:
        copy.wait()
    for side, message in ((0, low), (1, high)):
        for i in range(NPOP + 1):
            for h in range(2):
                index, row = rim_place(i, h)
                message[index, pl.ds(row, 1), :] = rim[side, i, :, half_lanes(h)]


def rim_place(i, h):
    return NPOP + 1 + (2 * i + h) // ROWS, (2 * i + h) % ROWS


def rim_row(message, i, h):
    index, row = rim_place(i, h)
    return jnp.broadcast_to(message[index, pl.ds(row, 1), :], TILE)


def inner_kernel(fine, solid, slot, inner, packed, chosen, work):
    groups = chosen.shape[1]
    ring = []
    for t in range(2):
        ring.append([])
        for h in range(2):
            rows, at = pl.ds(ROWS * t, ROWS), half_lanes(h)
            f = [fine[0, i, rows, at] for i in range(NPOP)]
            ring[t].append(collide(f, solid[0, rows, at], TAU_FINE))
    ring = stream_ring(ring)
    for t in range(2):
        for h in range(2):
            s = solid[0, pl.ds(ROWS * t, ROWS), half_lanes(h)]
            ring[t][h] = collide(ring[t][h], s, TAU_FINE)
    ring = stream_ring(ring)
    for i in range(NPOP):
        for h in range(2):
            for t in range(2):
                inner[i, h, pl.ds(ROWS * t, ROWS), :] = ring[t][h][i]
                work[i, h, pl.ds(ROWS * t, ROWS), :] = ring[t][h][i]
    mean = []
    for i in range(NPOP):
        halves = [
            work[i, h, pl.ds(0, ROWS, stride=2), :] + work[i, h, pl.ds(1, ROWS, stride=2), :]
            for h in range(2)
        ]
        mean.append(0.125 * squeeze(halves))
    out = restrict(mean) + [None]
    for j in range((NPOP + 1) // 2):
        packed[j] = pair_up(out[2 * j], out[2 * j + 1])
    me = lax.axis_index("grp")
    quadrant = lane_ids() % BX // 8
    for s in range(groups):
        code = slot[me ^ s]
        for h in range(2):
            chosen[h, s] = jnp.where(4 * me + 2 * h + quadrant == code, 1.0, 0.0)


def edge_kernel(own, below, above, edges, packed):
    row = row_ids()
    upper = row < 4
    rings, solids = [], []
    for message, is_low in ((below, True), (above, False)):
        halves = []
        for h in range(2):
            got = []
            for i in range(NPOP + 1):
                other = message[i] if h == 0 else roll_rows(message[i], 4)
                mine = own[i, h]
                got.append(jnp.where(upper, mine, other) if is_low else jnp.where(upper, other, mine))
            halves.append(got)
        rings.append([[half[:NPOP] for half in halves]])
        solids.append([half[NPOP] for half in halves])
    for r in range(2):
        ring = stream_ring(rings[r])
        ring[0] = [collide(ring[0][h], solids[r][h], TAU_FINE) for h in range(2)]
        rings[r] = stream_ring(ring)
    from_above = (row == 1) | (row == ROWS - 1)
    mean = []
    for i in range(NPOP):
        halves = []
        for h in range(2):
            low, high = rings[0][0][h][i], rings[1][0][h][i]
            edges[i, h] = jnp.where(upper, low, high)
            low = low + roll_rows(low, -1)
            high = high + roll_rows(high, -1)
            halves.append(jnp.where(from_above, roll_rows(high, 1), low))
        mean.append(0.125 * squeeze(halves))
    out = restrict(mean) + [None]
    pairs = [pair_up(out[2 * j], out[2 * j + 1]) for j in range((NPOP + 1) // 2)]
    outer = (row < 2) | (row >= 6)
    for j in range(len(pairs) // 2):
        packed[j] = jnp.where(outer, pairs[2 * j], roll_rows(pairs[2 * j + 1], 4))


def write_kernel(inner, edges, out):
    row = row_ids()
    for i in range(NPOP):
        for h in range(2):
            edge = edges[i, h]
            out[0, i, pl.ds(0, ROWS), half_lanes(h)] = jnp.where(
                row < 2, edge, inner[i, h, pl.ds(0, ROWS), :]
            )
            out[0, i, pl.ds(ROWS, ROWS), half_lanes(h)] = jnp.where(
                row >= 6, edge, inner[i, h, pl.ds(ROWS, ROWS), :]
            )


def coarse_kernel(coarse, solid, chosen, *refs):
    packed, out = refs[:-1], refs[-1]
    f = [[], []]
    for i in range(NPOP):
        tiles = [spread(m[i // 2], i % 2) for m in packed]
        for h in range(2):
            v = coarse[0, i, :, half_lanes(h)]
            for s, tile in enumerate(tiles):
                v = jnp.where(chosen[h, s] > 0.5, tile, v)
            f[h].append(v)
    for h in range(2):
        for i, v in enumerate(collide(f[h], solid[0, :, half_lanes(h)], TAU_COARSE)):
            out[i, h] = v


def last_kernel(coarse, solid, chosen, below, above, middle, *refs):
    packed, out = refs[:-1], refs[-1]
    row = row_ids()

    def framed(tile, i, h):
        tile = jnp.where(row == 6, rim_row(below, i, h), tile)
        return jnp.where(row == 1, rim_row(above, i, h), tile)

    f = [[], []]
    for i in range(NPOP):
        tiles = []
        for m in packed:
            tile = m[i // 4]
            tiles.append(spread(roll_rows(tile, 4) if i % 4 >= 2 else tile, i % 2))
        for h in range(2):
            v = framed(coarse[0, i, :, half_lanes(h)], i, h)
            for s, tile in enumerate(tiles):
                v = jnp.where(chosen[h, s] > 0.5, tile, v)
            f[h].append(v)
    ends = [
        collide(f[h], framed(solid[0, :, half_lanes(h)], NPOP, h), TAU_COARSE)
        for h in range(2)
    ]
    outer = (row == 0) | (row == ROWS - 1)
    for i in range(NPOP):
        cx, cy, cz = (int(c) for c in VEL[i])
        halves = []
        for h in range(2):
            v = jnp.where(outer, ends[h][i], middle[i, h])
            if cx > 0:
                v = jnp.where(row == 0, roll_rows(ends[h][i], 2), roll_rows(v, 1))
            elif cx < 0:
                v = jnp.where(row == ROWS - 1, roll_rows(ends[h][i], -2), roll_rows(v, -1))
            halves.append(v)
        for h, v in enumerate(shift_plane(halves, cy, cz)):
            out[0, i, :, half_lanes(h)] = v


def held(array):
    return pltpu.with_memory_space_constraint(array, VMEM)


def in_vmem(*shape):
    return VMEM(shape, jnp.float32)


def call(kernel, args, specs, outs, scratch=(), flops=0, name=None):
    single = not isinstance(outs, (list, tuple))
    outs = [outs] if single else list(outs)
    result = pl.pallas_call(
        kernel,
        in_specs=[pl.BlockSpec(memory_space=s) for s in specs],
        out_specs=[pl.BlockSpec(memory_space=VMEM)] * len(outs),
        out_shape=outs,
        scratch_shapes=list(scratch),
        compiler_params=pltpu.CompilerParams(vmem_limit_bytes=24 << 20),
        cost_estimate=pl.CostEstimate(flops=flops, bytes_accessed=1 << 20, transcendentals=0),
        name=name,
    )(*args)
    return result[0] if single else result


def per_device(fine_pops, fine_solid, coarse_pops, coarse_solid, coarse_slot):
    groups = lax.axis_size("grp")
    blocks = lax.axis_size("blk")
    words = NPOP + 6
    any_, smem = pl.ANY, pltpu.SMEM
    own, high, low = call(
        pack_kernel,
        (fine_pops, fine_solid, coarse_pops, coarse_solid),
        [any_] * 4,
        [in_vmem(NPOP + 1, 2, *TILE), in_vmem(words, *TILE), in_vmem(words, *TILE)],
        [
            in_vmem(NPOP + 1, ROWS, 2 * LANES),
            in_vmem(2, NPOP + 1, 1, 2 * LANES),
            pltpu.SemaphoreType.DMA((8,)),
        ],
        name="pack",
    )
    forward = [(i, (i + 1) % blocks) for i in range(blocks)]
    backward = [(i, (i - 1) % blocks) for i in range(blocks)]
    below = lax.ppermute(high, "blk", forward)
    above = lax.ppermute(low, "blk", backward)

    fine_v, solid_v = held(fine_pops), held(fine_solid)
    coarse_v, coarse_solid_v = held(coarse_pops), held(coarse_solid)
    inner, packed_inner, chosen = call(
        inner_kernel,
        (fine_v, solid_v, coarse_slot),
        [VMEM, VMEM, smem],
        [
            in_vmem(NPOP, 2, 2 * ROWS, LANES),
            in_vmem((NPOP + 1) // 2, *TILE),
            in_vmem(2, groups, *TILE),
        ],
        [in_vmem(NPOP, 2, 2 * ROWS, LANES)],
        name="inner",
    )

    def around(array):
        swaps = [[(i, i ^ s) for i in range(groups)] for s in range(1, groups)]
        return [array] + [lax.ppermute(array, "grp", swap) for swap in swaps]

    inner_parts = around(packed_inner)
    edges, packed_edges = call(
        edge_kernel,
        (held(own), held(below), held(above)),
        [VMEM] * 3,
        [in_vmem(NPOP, 2, *TILE), in_vmem((NPOP + 1) // 4, *TILE)],
        name="edge",
    )
    edge_parts = around(packed_edges)
    fine_out = call(
        write_kernel,
        (held(inner), held(edges)),
        [VMEM] * 2,
        jax.ShapeDtypeStruct(fine_pops.shape, jnp.float32),
        name="write",
    )
    middle = call(
        coarse_kernel,
        (coarse_v, coarse_solid_v, held(chosen), *map(held, inner_parts)),
        [VMEM] * (3 + groups),
        in_vmem(NPOP, 2, *TILE),
        name="coarse",
    )
    coarse_out = call(
        last_kernel,
        (
            coarse_v,
            coarse_solid_v,
            held(chosen),
            held(below),
            held(above),
            held(middle),
            *map(held, edge_parts),
        ),
        [VMEM] * (6 + groups),
        jax.ShapeDtypeStruct(coarse_pops.shape, jnp.float32),
        name="last",
    )
    return fine_out, coarse_out


def solution(mesh):
    placed = (
        P("grp", None, "blk", None),
        P("grp", "blk", None),
        P("grp", None, "blk", None),
        P("grp", "blk", None),
        P(),
    )
    return jax.shard_map(
        per_device,
        mesh=mesh,
        in_specs=placed,
        out_specs=(P("grp", None, "blk", None), P("grp", None, "blk", None)),
        check_vma=False,
    )
```

time: 378 us -> 20.9 us (0.06)
  local copies, waits for them, and re-layouts: 299 us -> 3.3 us
  other arithmetic: 48.6 us -> 0 us
  starting transfers between devices: 19.5 us -> 9.96 us
  between operations: 5.75 us -> 0.69 us
  Pallas kernels: 0 us -> 4.19 us
    scatter x4 -> x0, local copies, waits for them, and re-layouts: 161 us -> none  [per_device(): coarse.at[:, :, low_y:low_y + half_y, low_z:low_z + half_z]]
    another operation x128 -> x0, local copies, waits for them, and re-layouts: 64.4 us -> none  [the longest x71 49.1 us: stream_cells(): return jnp.stack(rolled)]
    unnamed x182 -> x12, local copies, waits for them, and re-layouts: 61.8 us -> 3.3 us
    concatenate x64 -> x0, other arithmetic: 19.8 us -> none  [the longest x60 16.9 us: stream_cells(): jnp.roll(planes, (int(lattice_vel[j, 1]), int(lattice_vel[j, 2])), axis=(...]
    reduce_sum x8 -> x0, other arithmetic: 14 us -> none  [the longest x1 8.01 us: per_device(): populations.reshape(19, xlength // 2, 2, BX // 2, 2, zlength // 2, 2)]
    slice x93 -> x0, local copies, waits for them, and re-layouts: 9.54 us -> none  [the longest x63 5.08 us: stream_cells(): jnp.roll(planes, (int(lattice_vel[j, 1]), int(lattice_vel[j, 2])), axis=(...]
    ppermute x6 -> x8, starting transfers between devices: 15.9 us -> 9.96 us  [the longest x6 3.84 us: around(): return [array] + [lax.ppermute(array, 'grp', swap) for swap in swaps]]
    another operation x3 -> x0, other arithmetic: 4.2 us -> none
  transfers between devices with their start and end apart: 7 -> 8, of which waited for: 2 -> 4; matrix products, arithmetic and copies ran while one was open for 14% -> 0% of each run, Pallas kernels for 0% -> 14%
where the time goes in v1:
time: 20.9 us; the launch traced here: 20.6 us
  starting transfers between devices  9.96 us (48%)
  Pallas kernels  4.19 us (20%)
  local copies, waits for them, and re-layouts  3.3 us (16%)
  waiting for transfers between devices  2.44 us (12%)
  between operations  0.69 us (3%)
    pallas_call x6, Pallas kernels, call(): pl.pallas_call(kernel, in_specs=[pl.BlockSpec(memory_space=s) for s in sp...  4.19 us
    ppermute x6, starting transfers between devices, around(): return [array] + [lax.ppermute(array, 'grp', swap) for swap in swaps]  3.84 us
    unnamed x12, local copies, waits for them, and re-layouts  3.3 us
    ppermute x1, starting transfers between devices, per_device(): above = lax.ppermute(low, 'blk', backward)  3.1 us
    ppermute x1, starting transfers between devices, per_device(): below = lax.ppermute(high, 'blk', forward)  3.02 us
    ppermute x6, waiting for transfers between devices, around(): return [array] + [lax.ppermute(array, 'grp', swap) for swap in swaps]  1.88 us
    ppermute x1, waiting for transfers between devices, per_device(): above = lax.ppermute(low, 'blk', backward)  0.55 us
  transfers between devices with their start and end apart: 8, of which 4 were waited for; matrix products, arithmetic and copies ran while one was open for 0% of the time, Pallas kernels for 14%

profile of v1, /device:TPU:0, one launch (start us, length us, event | category | flops | bytes accessed | tf_op | source)
XLA Modules:
  0.0 20.6 jit_solution(5980943019488031698)
XLA Ops:
  0.6 0.0 copy-start
  0.6 0.9 %copy-done = f32[1,19,8,256]{3,2,1,0:T(8,128)S(1)} copy-done((f32[1,19,8,256]{3,2,1,0:T(8,128)S(1)}, f32[1,19,8,256]{3,2,1,0:T(8,128)}, u32[]{:S(2)}) %copy-start) | copy-done | bytes 155672
  1.5 0.0 copy-start.2
  1.5 1.0 %copy-done.2 = f32[1,19,16,256]{3,2,1,0:T(8,128)S(1)} copy-done((f32[1,19,16,256]{3,2,1,0:T(8,128)S(1)}, f32[1,19,16,256]{3,2,1,0:T(8,128)}, u32[]{:S(2)}) %copy-start.2) | copy-done | bytes 311320
  2.5 0.0 copy-start.3
  2.5 0.7 %copy-done.3 = f32[1,8,256]{2,1,0:T(8,128)S(1)} copy-done((f32[1,8,256]{2,1,0:T(8,128)S(1)}, f32[1,8,256]{2,1,0:T(8,128)}, u32[]{:S(2)}) %copy-start.3) | copy-done | bytes 8216
  3.2 0.7 %copy-done.4 = f32[1,16,256]{2,1,0:T(8,128)S(1)} copy-done((f32[1,16,256]{2,1,0:T(8,128)S(1)}, f32[1,16,256]{2,1,0:T(8,128)}, u32[]{:S(2)}) %copy-start.4) | copy-done | bytes 16408
  3.9 0.2 %pack.1 = (f32[20,2,8,128]{3,2,1,0:T(8,128)S(1)}, f32[25,8,128]{2,1,0:T(8,128)S(1)}, f32[25,8,128]{2,1,0:T(8,128)S(1)}) custom-call(f32[1,19,16,256]{3,2,1,0:T(8,128)S(1)} %copy-done.2, f32[1,16,256]{2,1,0:T(8,128)S(1)} %copy-done.4, f32[1,19,8,256]{3,2,1,0:T(8,128)S(1)} %copy-done, f32[1,8,256]{2,1,0:T(8,128)S(1)} %copy-done.3), custom_call_target="tpu_custom_call" | custom-call | bytes 1048576 | tf_op jit(solution)/shard_map/pack/pallas_call | solution.py:372
  4.1 0.0 copy-start.5
  4.2 3.0 %collective-permute-start = (f32[25,8,128]{2,1,0:T(8,128)S(1)}, f32[25,8,128]{2,1,0:T(8,128)S(1)}, u32[]{:S(2)}, u32[]{:S(2)}) collective-permute-start(f32[25,8,128]{2,1,0:T(8,128)S(1)} %get-tuple-element.12), channel_id=1, source_target_pairs={{0,1},{1,2},{2,3},{3,4},{4,5},{5,6},{6,7},{7,0},{8,9},{9,10},{10,1... | collective-permute-start | bytes 307208 | tf_op jit(solution)/shard_map/ppermute | solution.py:404
  7.2 3.1 %collective-permute-start.1 = (f32[25,8,128]{2,1,0:T(8,128)S(1)}, f32[25,8,128]{2,1,0:T(8,128)S(1)}, u32[]{:S(2)}, u32[]{:S(2)}) collective-permute-start(f32[25,8,128]{2,1,0:T(8,128)S(1)} %get-tuple-element.13), channel_id=1, source_target_pairs={{0,7},{1,0},{2,1},{3,2},{4,3},{5,4},{6,5},{7,6},{8,15},{9,8},{10,9... | collective-permute-start | bytes 307208 | tf_op jit(solution)/shard_map/ppermute | solution.py:405
  10.3 0.0 copy-done.5
  10.3 1.3 %inner.1 = (f32[19,2,16,128]{3,2,1,0:T(8,128)S(1)}, f32[10,8,128]{2,1,0:T(8,128)S(1)}, f32[2,4,8,128]{3,2,1,0:T(8,128)S(1)}) custom-call(f32[1,19,16,256]{3,2,1,0:T(8,128)S(1)} %copy-done.2, f32[1,16,256]{2,1,0:T(8,128)S(1)} %copy-done.4, s32[4]{0:T(128)S(1)} %copy-done.5), custom_call_target="tpu_custom_call" | custom-call | bytes 1048576 | tf_op jit(solution)/shard_map/inner/pallas_call | solution.py:372
  11.6 0.0 collective-permute-start.2
  11.6 1.7 %collective-permute-start.3 = (f32[10,8,128]{2,1,0:T(8,128)S(1)}, f32[10,8,128]{2,1,0:T(8,128)S(1)}, u32[]{:S(2)}, u32[]{:S(2)}) collective-permute-start(f32[10,8,128]{2,1,0:T(8,128)S(1)} %get-tuple-element.16.refs_0_), channel_id=1, source_target_pairs={{0,16},{8,24},{16,0},{24,8},{1,17},{9,25},{17,1},{25,9},{2,18},{10... | collective-permute-start | bytes 122888 | tf_op jit(solution)/shard_map/ppermute | solution.py:424
  13.3 0.2 %collective-permute-start.4 = (f32[10,8,128]{2,1,0:T(8,128)S(1)}, f32[10,8,128]{2,1,0:T(8,128)S(1)}, u32[]{:S(2)}, u32[]{:S(2)}) collective-permute-start(f32[10,8,128]{2,1,0:T(8,128)S(1)} %get-tuple-element.16.refs_0_), channel_id=1, source_target_pairs={{0,24},{8,16},{16,8},{24,0},{1,25},{9,17},{17,9},{25,1},{2,26},{10... | collective-permute-start | bytes 122888 | tf_op jit(solution)/shard_map/ppermute | solution.py:424
  13.5 0.0 collective-permute-done.below
  13.5 0.6 %collective-permute-done.1.above = f32[25,8,128]{2,1,0:T(8,128)S(1)} collective-permute-done((f32[25,8,128]{2,1,0:T(8,128)S(1)}, f32[25,8,128]{2,1,0:T(8,128)S(1)}, u32[]{:S(2)}, u32[]{:S(2)}) %collective-permute-start.1) | collective-permute-done | bytes 102432 | tf_op jit(solution)/shard_map/ppermute | solution.py:405
  14.0 0.7 %edge.1 = (f32[19,2,8,128]{3,2,1,0:T(8,128)S(1)}, f32[5,8,128]{2,1,0:T(8,128)S(1)}) custom-call(f32[20,2,8,128]{3,2,1,0:T(8,128)S(1)} %get-tuple-element.11.own, f32[25,8,128]{2,1,0:T(8,128)S(1)} %collective-permute-done.below, f32[25,8,128]{2,1,0:T(8,128)S(1)} %collective-permute-done.1.above), custom_call_target="tpu_custom_call" | custom-call | bytes 1048576 | tf_op jit(solution)/shard_map/edge/pallas_call | solution.py:372
  14.7 0.1 collective-permute-start.5
  14.8 1.6 %collective-permute-start.6 = (f32[5,8,128]{2,1,0:T(8,128)S(1)}, f32[5,8,128]{2,1,0:T(8,128)S(1)}, u32[]{:S(2)}, u32[]{:S(2)}) collective-permute-start(f32[5,8,128]{2,1,0:T(8,128)S(1)} %get-tuple-element.17.refs_0_), channel_id=1, source_target_pairs={{0,16},{8,24},{16,0},{24,8},{1,17},{9,25},{17,1},{25,9},{2,18},{10... | collective-permute-start | bytes 61448 | tf_op jit(solution)/shard_map/ppermute | solution.py:424
  16.3 0.0 collective-permute-done.2.refs_1_
  16.3 0.3 %collective-permute-start.7 = (f32[5,8,128]{2,1,0:T(8,128)S(1)}, f32[5,8,128]{2,1,0:T(8,128)S(1)}, u32[]{:S(2)}, u32[]{:S(2)}) collective-permute-start(f32[5,8,128]{2,1,0:T(8,128)S(1)} %get-tuple-element.17.refs_0_), channel_id=1, source_target_pairs={{0,24},{8,16},{16,8},{24,0},{1,25},{9,17},{17,9},{25,1},{2,26},{10... | collective-permute-start | bytes 61448 | tf_op jit(solution)/shard_map/ppermute | solution.py:424
  16.6 0.0 collective-permute-done.3.refs_2_
  16.6 0.1 collective-permute-done.4.refs_3_
  16.8 0.0 copy-done.1
  16.8 0.3 %coarse.5.middle = f32[19,2,8,128]{3,2,1,0:T(8,128)S(1)} custom-call(f32[1,19,8,256]{3,2,1,0:T(8,128)S(1)} %copy-done.1, f32[1,8,256]{2,1,0:T(8,128)S(1)} %copy-done.3, f32[2,4,8,128]{3,2,1,0:T(8,128)S(1)} %get-tuple-element.15.chosen, f32[10,8,128]{2,1,0:T(8,128)S(1)} %get-tuple-element.16.refs_0_, f32[10,8,128]{2,1,0:T(8,128)S(1)} %collective-permute-done.2.refs_1_, ...), custom_call_target="tpu_custom_call" | custom-call | bytes 1048576 | tf_op jit(solution)/shard_map/coarse/pallas_call | solution.py:372
  17.1 0.7 %write.1 = f32[1,19,16,256]{3,2,1,0:T(8,128)} custom-call(f32[19,2,16,128]{3,2,1,0:T(8,128)S(1)} %get-tuple-element.10.inner, f32[19,2,8,128]{3,2,1,0:T(8,128)S(1)} %get-tuple-element.14.edges), custom_call_target="tpu_custom_call" | custom-call | bytes 1048576 | tf_op jit(solution)/shard_map/write/pallas_call | solution.py:372
  17.8 0.0 collective-permute-done.5.refs_1_
  17.8 0.8 %collective-permute-done.6.refs_2_ = f32[5,8,128]{2,1,0:T(8,128)S(1)} collective-permute-done((f32[5,8,128]{2,1,0:T(8,128)S(1)}, f32[5,8,128]{2,1,0:T(8,128)S(1)}, u32[]{:S(2)}, u32[]{:S(2)}) %collective-permute-start.6) | collective-permute-done | bytes 20512 | tf_op jit(solution)/shard_map/ppermute | solution.py:424
  18.6 0.9 %collective-permute-done.7.refs_3_ = f32[5,8,128]{2,1,0:T(8,128)S(1)} collective-permute-done((f32[5,8,128]{2,1,0:T(8,128)S(1)}, f32[5,8,128]{2,1,0:T(8,128)S(1)}, u32[]{:S(2)}, u32[]{:S(2)}) %collective-permute-start.7) | collective-permute-done | bytes 20512 | tf_op jit(solution)/shard_map/ppermute | solution.py:424
  19.5 1.0 %last.1 = f32[1,19,8,256]{3,2,1,0:T(8,128)} custom-call(f32[1,19,8,256]{3,2,1,0:T(8,128)S(1)} %copy-done.1, f32[1,8,256]{2,1,0:T(8,128)S(1)} %copy-done.3, f32[2,4,8,128]{3,2,1,0:T(8,128)S(1)} %get-tuple-element.15.chosen, f32[25,8,128]{2,1,0:T(8,128)S(1)} %collective-permute-done.below, f32[25,8,128]{2,1,0:T(8,128)S(1)} %collective-permute-done.1.above, ...), custom_call_target="tpu_custom_call" | custom-call | bytes 1048576 | tf_op jit(solution)/shard_map/last/pallas_call | solution.py:372
  (2 shorter events, 0.0 us)
Async XLA Ops:
  0.6 0.9 %copy-start = (f32[1,19,8,256]{3,2,1,0:T(8,128)S(1)}, f32[1,19,8,256]{3,2,1,0:T(8,128)}, u32[]{:S(2)}) copy-start(f32[1,19,8,256]{3,2,1,0:T(8,128)} %coarse.7) | copy-start | bytes 466948
  1.5 1.0 %copy-start.2 = (f32[1,19,16,256]{3,2,1,0:T(8,128)S(1)}, f32[1,19,16,256]{3,2,1,0:T(8,128)}, u32[]{:S(2)}) copy-start(f32[1,19,16,256]{3,2,1,0:T(8,128)} %fine.3) | copy-start | bytes 933892
  2.5 0.7 %copy-start.3 = (f32[1,8,256]{2,1,0:T(8,128)S(1)}, f32[1,8,256]{2,1,0:T(8,128)}, u32[]{:S(2)}) copy-start(f32[1,8,256]{2,1,0:T(8,128)} %solid.7) | copy-start | bytes 24580
  3.2 0.7 %copy-start.4 = (f32[1,16,256]{2,1,0:T(8,128)S(1)}, f32[1,16,256]{2,1,0:T(8,128)}, u32[]{:S(2)}) copy-start(f32[1,16,256]{2,1,0:T(8,128)} %solid.5) | copy-start | bytes 49156
  4.1 6.1 %copy-start.5 = (s32[4]{0:T(128)S(1)}, s32[4]{0:T(128)}, u32[]{:S(2)}) copy-start(s32[4]{0:T(128)} %slot.1) | copy-start | bytes 52
  4.2 9.3 %collective-permute-start = (f32[25,8,128]{2,1,0:T(8,128)S(1)}, f32[25,8,128]{2,1,0:T(8,128)S(1)}, u32[]{:S(2)}, u32[]{:S(2)}) collective-permute-start(f32[25,8,128]{2,1,0:T(8,128)S(1)} %get-tuple-element.12), channel_id=1, source_target_pairs={{0,1},{1,2},{2,3},{3,4},{4,5},{5,6},{6,7},{7,0},{8,9},{9,10},{10,1... | collective-permute-start | bytes 307208 | tf_op jit(solution)/shard_map/ppermute | solution.py:404
  7.2 6.9 %collective-permute-start.1 = (f32[25,8,128]{2,1,0:T(8,128)S(1)}, f32[25,8,128]{2,1,0:T(8,128)S(1)}, u32[]{:S(2)}, u32[]{:S(2)}) collective-permute-start(f32[25,8,128]{2,1,0:T(8,128)S(1)} %get-tuple-element.13), channel_id=1, source_target_pairs={{0,7},{1,0},{2,1},{3,2},{4,3},{5,4},{6,5},{7,6},{8,15},{9,8},{10,9... | collective-permute-start | bytes 307208 | tf_op jit(solution)/shard_map/ppermute | solution.py:405
  11.6 4.8 %collective-permute-start.2 = (f32[10,8,128]{2,1,0:T(8,128)S(1)}, f32[10,8,128]{2,1,0:T(8,128)S(1)}, u32[]{:S(2)}, u32[]{:S(2)}) collective-permute-start(f32[10,8,128]{2,1,0:T(8,128)S(1)} %get-tuple-element.16.refs_0_), channel_id=1, source_target_pairs={{0,8},{8,0},{16,24},{24,16},{1,9},{9,1},{17,25},{25,17},{2,10},{10... | collective-permute-start | bytes 122888 | tf_op jit(solution)/shard_map/ppermute | solution.py:424
  11.6 5.0 %collective-permute-start.3 = (f32[10,8,128]{2,1,0:T(8,128)S(1)}, f32[10,8,128]{2,1,0:T(8,128)S(1)}, u32[]{:S(2)}, u32[]{:S(2)}) collective-permute-start(f32[10,8,128]{2,1,0:T(8,128)S(1)} %get-tuple-element.16.refs_0_), channel_id=1, source_target_pairs={{0,16},{8,24},{16,0},{24,8},{1,17},{9,25},{17,1},{25,9},{2,18},{10... | collective-permute-start | bytes 122888 | tf_op jit(solution)/shard_map/ppermute | solution.py:424
  13.3 3.5 %collective-permute-start.4 = (f32[10,8,128]{2,1,0:T(8,128)S(1)}, f32[10,8,128]{2,1,0:T(8,128)S(1)}, u32[]{:S(2)}, u32[]{:S(2)}) collective-permute-start(f32[10,8,128]{2,1,0:T(8,128)S(1)} %get-tuple-element.16.refs_0_), channel_id=1, source_target_pairs={{0,24},{8,16},{16,8},{24,0},{1,25},{9,17},{17,9},{25,1},{2,26},{10... | collective-permute-start | bytes 122888 | tf_op jit(solution)/shard_map/ppermute | solution.py:424
  14.0 2.8 %copy-start.1 = (f32[1,19,8,256]{3,2,1,0:T(8,128)S(1)}, f32[1,19,8,256]{3,2,1,0:T(8,128)}, u32[]{:S(2)}) copy-start(f32[1,19,8,256]{3,2,1,0:T(8,128)} %coarse.7) | copy-start | bytes 466948
  14.7 3.1 %collective-permute-start.5 = (f32[5,8,128]{2,1,0:T(8,128)S(1)}, f32[5,8,128]{2,1,0:T(8,128)S(1)}, u32[]{:S(2)}, u32[]{:S(2)}) collective-permute-start(f32[5,8,128]{2,1,0:T(8,128)S(1)} %get-tuple-element.17.refs_0_), channel_id=1, source_target_pairs={{0,8},{8,0},{16,24},{24,16},{1,9},{9,1},{17,25},{25,17},{2,10},{10... | collective-permute-start | bytes 61448 | tf_op jit(solution)/shard_map/ppermute | solution.py:424
  14.8 3.8 %collective-permute-start.6 = (f32[5,8,128]{2,1,0:T(8,128)S(1)}, f32[5,8,128]{2,1,0:T(8,128)S(1)}, u32[]{:S(2)}, u32[]{:S(2)}) collective-permute-start(f32[5,8,128]{2,1,0:T(8,128)S(1)} %get-tuple-element.17.refs_0_), channel_id=1, source_target_pairs={{0,16},{8,24},{16,0},{24,8},{1,17},{9,25},{17,1},{25,9},{2,18},{10... | collective-permute-start | bytes 61448 | tf_op jit(solution)/shard_map/ppermute | solution.py:424
  16.3 3.2 %collective-permute-start.7 = (f32[5,8,128]{2,1,0:T(8,128)S(1)}, f32[5,8,128]{2,1,0:T(8,128)S(1)}, u32[]{:S(2)}, u32[]{:S(2)}) collective-permute-start(f32[5,8,128]{2,1,0:T(8,128)S(1)} %get-tuple-element.17.refs_0_), channel_id=1, source_target_pairs={{0,24},{8,16},{16,8},{24,0},{1,25},{9,17},{17,9},{25,1},{2,26},{10... | collective-permute-start | bytes 61448 | tf_op jit(solution)/shard_map/ppermute | solution.py:424

commit v2 on v1

--- a/solution.py
+++ b/solution.py
@@ -136,21 +136,34 @@
     return [jnp.where(edge, turned[(i - cx) % n], turned[i]) for i in range(n)]
 
 
-def stream_ring(ring):
+def move_in_planes(halves):
+    moved = [
+        shift_plane([halves[0][i], halves[1][i]], int(VEL[i, 1]), int(VEL[i, 2]))
+        for i in range(NPOP)
+    ]
+    return [[moved[i][h] for i in range(NPOP)] for h in range(2)]
+
+
+def move_along(ring):
     out = [[[], []] for _ in ring]
-    for i in range(NPOP):
-        cx, cy, cz = (int(c) for c in VEL[i])
-        moved = [shift_plane([tile[0][i], tile[1][i]], cy, cz) for tile in ring]
-        for h in range(2):
-            for t, v in enumerate(shift_ring([m[h] for m in moved], cx)):
+    for h in range(2):
+        for i in range(NPOP):
+            for t, v in enumerate(shift_ring([tile[h][i] for tile in ring], int(VEL[i, 0]))):
                 out[t][h].append(v)
     return out
 
 
+def merge(mask, first, second):
+    return [
+        [jnp.where(mask, v, w) for v, w in zip(a, b)] for a, b in zip(first, second)
+    ]
+
+
 def squeeze(halves):
-    lane = lane_ids()
-    low, high = (v + roll_lanes(v, -1) for v in halves)
-    both = jnp.where(lane % 2 == 1, roll_lanes(high, 1), low)
+    even = lane_ids() % 2 == 0
+    first = jnp.where(even, halves[0], roll_lanes(halves[1], 1))
+    second = jnp.where(even, roll_lanes(halves[0], -1), halves[1])
+    both = first + second
     return both + roll_lanes(both, -BX)
 
 
@@ -171,67 +184,121 @@
     return pl.ds(h * LANES, LANES)
 
 
+FORWARD = [i for i in range(NPOP) if VEL[i, 0] > 0]
+LEVEL = [i for i in range(NPOP) if VEL[i, 0] == 0]
+BACKWARD = [i for i in range(NPOP) if VEL[i, 0] < 0]
+MOVING = len(FORWARD)
+FIRST_LEVEL = MOVING
+FIRST_PAIR = FIRST_LEVEL + len(LEVEL)
+WORDS = FIRST_PAIR + (MOVING + 1) // 2
+FIRST_RIM = FIRST_LEVEL + 1
+
+
+def pack_message(message, tile, rim, towards, away, up):
+    place = row_ids() % 4
+    spare = place == (0 if up > 0 else 3)
+    near = place >= 2 if up > 0 else place < 2
+    for k, i in enumerate(towards):
+        message[k] = tile(i)
+    for k, i in enumerate(LEVEL):
+        other = roll_rows(tile(NPOP), -up) if k == 0 else rim(k - 1)
+        message[FIRST_LEVEL + k] = tile(i) if other is None else jnp.where(spare, other, tile(i))
+    for k in range((MOVING + 1) // 2):
+        second = away[2 * k + 1] if 2 * k + 1 < MOVING else NPOP
+        message[FIRST_PAIR + k] = jnp.where(near, tile(away[2 * k]), roll_rows(tile(second), -2 * up))
+
+
+def unpack_message(message, towards, away, up):
+    near = row_ids() % 4 >= 2 if up > 0 else row_ids() % 4 < 2
+    found = [None] * (NPOP + 1)
+    for k, i in enumerate(towards):
+        found[i] = message[k]
+    for k, i in enumerate(LEVEL):
+        found[i] = message[FIRST_LEVEL + k]
+    for k in range((MOVING + 1) // 2):
+        tile = message[FIRST_PAIR + k]
+        found[away[2 * k]] = tile
+        found[away[2 * k + 1] if 2 * k + 1 < MOVING else NPOP] = roll_rows(tile, 2 * up)
+    found[NPOP] = jnp.where(near, found[NPOP], roll_rows(message[FIRST_LEVEL], up))
+    return found
+
+
+def rim_row(message, k, h, up):
+    row = (4, 0)[h] if up > 0 else (3, 7)[h]
+    return jnp.broadcast_to(message[FIRST_RIM + k, pl.ds(row, 1), :], TILE)
+
+
 def pack_kernel(fine, solid, coarse, coarse_solid, own, high, low, strip, rim, sem):
     planes = fine.shape[2]
-    coarse_planes = coarse.shape[2]
-    copies = []
-
-    def bring(source, target):
-        copies.append(pltpu.make_async_copy(source, target, sem.at[len(copies)]))
-        copies[-1].start()
-
-    for first, row in ((0, 0), (planes - 4, 4)):
-        bring(fine.at[0, :, pl.ds(first, 4), :], strip.at[pl.ds(0, NPOP), pl.ds(row, 4), :])
-        bring(solid.at[0, pl.ds(first, 4), :], strip.at[NPOP, pl.ds(row, 4), :])
-    for side, plane in ((0, 0), (1, coarse_planes - 1)):
-        bring(coarse.at[0, :, pl.ds(plane, 1), :], rim.at[side, pl.ds(0, NPOP)])
-        bring(coarse_solid.at[0, pl.ds(plane, 1), :], rim.at[side, NPOP])
-    for copy in copies[:4]:
-        copy.wait()
-    upper = row_ids() < 4
+    last = coarse.shape[2] - 1
+
+    def bring(source, target, which):
+        pltpu.make_async_copy(source, target, sem.at[which]).start()
+
+    def arrive(target, which):
+        pltpu.make_async_copy(target, target, sem.at[which]).wait()
+
+    ends = ((0, 0), (planes - 4, 4))
+    for h in range(2):
+        at = half_lanes(h)
+        for first, row in ends:
+            bring(fine.at[0, :, pl.ds(first, 4), at], strip.at[pl.ds(0, NPOP), pl.ds(row, 4), at], 0)
+    for first, row in ends:
+        bring(solid.at[0, pl.ds(first, 4), :], strip.at[NPOP, pl.ds(row, 4), :], 0)
+    for plane, h, row in ((last, 1, 0), (last, 0, 4), (0, 0, 3), (0, 1, 7)):
+        target = rim.at[pl.ds(0, NPOP), pl.ds(row, 1), :]
+        bring(coarse.at[0, :, pl.ds(plane, 1), half_lanes(h)], target, 1)
+        bring(coarse_solid.at[0, pl.ds(plane, 1), half_lanes(h)], rim.at[NPOP, pl.ds(row, 1), :], 1)
+    arrive(strip, 0)
     for h in range(2):
         at = half_lanes(h)
         s = strip[NPOP, :, at]
         out = collide([strip[i, :, at] for i in range(NPOP)], s, TAU_FINE)
         for i, v in enumerate(out + [s]):
             own[i, h] = v
-    for i in range(NPOP + 1):
-        first, second = own[i, 0], roll_rows(own[i, 1], 4)
-        high[i] = jnp.where(upper, second, first)
-        low[i] = jnp.where(upper, first, second)
-    for copy in copies[4:]:
-        copy.wait()
-    for side, message in ((0, low), (1, high)):
-        for i in range(NPOP + 1):
-            for h in range(2):
-                index, row = rim_place(i, h)
-                message[index, pl.ds(row, 1), :] = rim[side, i, :, half_lanes(h)]
-
-
-def rim_place(i, h):
-    return NPOP + 1 + (2 * i + h) // ROWS, (2 * i + h) % ROWS
-
-
-def rim_row(message, i, h):
-    index, row = rim_place(i, h)
-    return jnp.broadcast_to(message[index, pl.ds(row, 1), :], TILE)
-
-
-def inner_kernel(fine, solid, slot, inner, packed, chosen, work):
+    arrive(rim.at[:, pl.ds(0, 4), :], 1)
+    s = rim[NPOP]
+    ends = collide([rim[i] for i in range(NPOP)], s, TAU_COARSE) + [s]
+    upper = row_ids() < 4
+
+    def ending(i):
+        return jnp.where(upper, roll_rows(own[i, 1], 4), own[i, 0])
+
+    def beginning(i):
+        return jnp.where(upper, own[i, 0], roll_rows(own[i, 1], 4))
+
+    def rim_of(towards):
+        return lambda k: ends[(towards + [NPOP])[k]] if k <= MOVING else None
+
+    pack_message(high, ending, rim_of(FORWARD), FORWARD, BACKWARD, 1)
+    pack_message(low, beginning, rim_of(BACKWARD), BACKWARD, FORWARD, -1)
+
+
+def inner_kernel(fine, solid, own, slot, inner, packed, chosen, moved, work):
     groups = chosen.shape[1]
-    ring = []
-    for t in range(2):
-        ring.append([])
-        for h in range(2):
-            rows, at = pl.ds(ROWS * t, ROWS), half_lanes(h)
-            f = [fine[0, i, rows, at] for i in range(NPOP)]
-            ring[t].append(collide(f, solid[0, rows, at], TAU_FINE))
-    ring = stream_ring(ring)
+    upper = row_ids() < 4
+
+    def middle(ref, h, *i):
+        at = half_lanes(h)
+        return jnp.where(upper, ref[(0, *i, pl.ds(ROWS, ROWS), at)], ref[(0, *i, pl.ds(0, ROWS), at)])
+
+    outer = move_in_planes([[own[i, h] for i in range(NPOP)] for h in range(2)])
+    center = move_in_planes(
+        [
+            collide([middle(fine, h, i) for i in range(NPOP)], middle(solid, h), TAU_FINE)
+            for h in range(2)
+        ]
+    )
+    for i in range(NPOP):
+        for h in range(2):
+            moved[i, h] = outer[h][i]
+    ring = move_along([merge(upper, outer, center), merge(upper, center, outer)])
     for t in range(2):
         for h in range(2):
             s = solid[0, pl.ds(ROWS * t, ROWS), half_lanes(h)]
             ring[t][h] = collide(ring[t][h], s, TAU_FINE)
-    ring = stream_ring(ring)
+        ring[t] = move_in_planes(ring[t])
+    ring = move_along(ring)
     for i in range(NPOP):
         for h in range(2):
             for t in range(2):
@@ -248,48 +315,52 @@
     for j in range((NPOP + 1) // 2):
         packed[j] = pair_up(out[2 * j], out[2 * j + 1])
     me = lax.axis_index("grp")
-    quadrant = lane_ids() % BX // 8
-    for s in range(groups):
-        code = slot[me ^ s]
-        for h in range(2):
-            chosen[h, s] = jnp.where(4 * me + 2 * h + quadrant == code, 1.0, 0.0)
-
-
-def edge_kernel(own, below, above, edges, packed):
+    codes = slot[...].reshape(1, groups)
+    group_ids = lax.broadcasted_iota(jnp.int32, codes.shape, 1)
+    quadrant = 4 * me + lane_ids() % BX // 8
+    for s, other in enumerate(peers(groups)):
+        code = jnp.sum(jnp.where(group_ids == me ^ other, codes, 0), axis=1, keepdims=True)
+        for h in range(2):
+            chosen[h, s] = jnp.where(quadrant + 2 * h == code, 1.0, 0.0)
+
+
+def edge_kernel(own, moved, below, above, edges, packed):
     row = row_ids()
     upper = row < 4
-    rings, solids = [], []
-    for message, is_low in ((below, True), (above, False)):
-        halves = []
-        for h in range(2):
-            got = []
-            for i in range(NPOP + 1):
-                other = message[i] if h == 0 else roll_rows(message[i], 4)
-                mine = own[i, h]
-                got.append(jnp.where(upper, mine, other) if is_low else jnp.where(upper, other, mine))
-            halves.append(got)
-        rings.append([[half[:NPOP] for half in halves]])
-        solids.append([half[NPOP] for half in halves])
-    for r in range(2):
-        ring = stream_ring(rings[r])
-        ring[0] = [collide(ring[0][h], solids[r][h], TAU_FINE) for h in range(2)]
-        rings[r] = stream_ring(ring)
-    from_above = (row == 1) | (row == ROWS - 1)
+    below = unpack_message(below, FORWARD, BACKWARD, 1)
+    above = unpack_message(above, BACKWARD, FORWARD, -1)
+    halos = [
+        [jnp.where(upper, a, b) for a, b in zip(above, below)],
+        [roll_rows(jnp.where(upper, b, a), 4) for a, b in zip(above, below)],
+    ]
+    solids = [(own[NPOP, h], halos[h][NPOP]) for h in range(2)]
+    halos = move_in_planes([half[:NPOP] for half in halos])
+    mine = [[moved[i, h] for i in range(NPOP)] for h in range(2)]
+    low, high = (
+        move_along([ring])[0] for ring in (merge(upper, mine, halos), merge(upper, halos, mine))
+    )
+    low = [collide(low[h], jnp.where(upper, *solids[h]), TAU_FINE) for h in range(2)]
+    high = [collide(high[h], jnp.where(upper, *solids[h][::-1]), TAU_FINE) for h in range(2)]
+    low, high = (move_along([ring])[0] for ring in (low, high))
+    high = [[roll_rows(v, 4) for v in half] for half in high]
+    both = move_in_planes(merge((row < 2) | (row >= 6), low, high))
+    sums = [[v + roll_rows(v, -1) for v in half] + [None] for half in both]
+    odd = row % 2 == 1
     mean = []
-    for i in range(NPOP):
-        halves = []
-        for h in range(2):
-            low, high = rings[0][0][h][i], rings[1][0][h][i]
-            edges[i, h] = jnp.where(upper, low, high)
-            low = low + roll_rows(low, -1)
-            high = high + roll_rows(high, -1)
-            halves.append(jnp.where(from_above, roll_rows(high, 1), low))
-        mean.append(0.125 * squeeze(halves))
-    out = restrict(mean) + [None]
-    pairs = [pair_up(out[2 * j], out[2 * j + 1]) for j in range((NPOP + 1) // 2)]
-    outer = (row < 2) | (row >= 6)
+    for i in range(0, NPOP, 2):
+        pair = [half[i] if half[i + 1] is None else jnp.where(odd, roll_rows(half[i + 1], 1), half[i]) for half in sums]
+        pair = 0.125 * squeeze(pair)
+        mean += [pair, roll_rows(pair, -1)]
+    out = restrict(mean[:NPOP]) + [None]
+    pairs = [
+        out[i] if out[i + 1] is None else jnp.where(odd, roll_rows(out[i + 1], 1), out[i])
+        for i in range(0, NPOP, 2)
+    ]
     for j in range(len(pairs) // 2):
-        packed[j] = jnp.where(outer, pairs[2 * j], roll_rows(pairs[2 * j + 1], 4))
+        packed[j] = pair_up(pairs[2 * j], pairs[2 * j + 1])
+    for i in range(NPOP):
+        for h in range(2):
+            edges[i, h] = both[h][i]
 
 
 def write_kernel(inner, edges, out):
@@ -301,7 +372,7 @@
                 row < 2, edge, inner[i, h, pl.ds(0, ROWS), :]
             )
             out[0, i, pl.ds(ROWS, ROWS), half_lanes(h)] = jnp.where(
-                row >= 6, edge, inner[i, h, pl.ds(ROWS, ROWS), :]
+                row >= 6, roll_rows(edge, 4), inner[i, h, pl.ds(ROWS, ROWS), :]
             )
 
 
@@ -323,43 +394,63 @@
 def last_kernel(coarse, solid, chosen, below, above, middle, *refs):
     packed, out = refs[:-1], refs[-1]
     row = row_ids()
-
-    def framed(tile, i, h):
-        tile = jnp.where(row == 6, rim_row(below, i, h), tile)
-        return jnp.where(row == 1, rim_row(above, i, h), tile)
-
-    f = [[], []]
-    for i in range(NPOP):
-        tiles = []
-        for m in packed:
-            tile = m[i // 4]
-            tiles.append(spread(roll_rows(tile, 4) if i % 4 >= 2 else tile, i % 2))
-        for h in range(2):
-            v = framed(coarse[0, i, :, half_lanes(h)], i, h)
-            for s, tile in enumerate(tiles):
-                v = jnp.where(chosen[h, s] > 0.5, tile, v)
-            f[h].append(v)
-    ends = [
-        collide(f[h], framed(solid[0, :, half_lanes(h)], NPOP, h), TAU_COARSE)
-        for h in range(2)
-    ]
-    outer = (row == 0) | (row == ROWS - 1)
+    masks = [[chosen[h, s] > 0.5 for s in range(len(packed))] for h in range(2)]
+    pasted = []
+    for h in range(2):
+        total = chosen[h, 0]
+        for s in range(1, len(packed)):
+            total = total + chosen[h, s]
+        pasted.append(total > 0.5)
+    f = [[None] * NPOP, [None] * NPOP]
+    for j in range((NPOP + 1) // 4):
+        for which in range(2):
+            tiles = [spread(m[j], which) for m in packed]
+            for h in range(2):
+                chosen_tile = tiles[0]
+                for s in range(1, len(packed)):
+                    chosen_tile = jnp.where(masks[h][s], tiles[s], chosen_tile)
+                for i in (4 * j + 2 * which, 4 * j + 2 * which + 1):
+                    if i < NPOP:
+                        tile = roll_rows(chosen_tile, -(i % 2))
+                        here = coarse[0, i, :, half_lanes(h)]
+                        here = jnp.where(row == 2, roll_rows(here, 3), here)
+                        f[h][i] = jnp.where(pasted[h], tile, here)
+    ends = []
+    for h in range(2):
+        s = solid[0, :, half_lanes(h)]
+        s = jnp.where(row == 2, roll_rows(s, 3), s)
+        s = jnp.where(row == 6, rim_row(below, MOVING, h, 1), s)
+        s = jnp.where(row == 4, rim_row(above, MOVING, h, -1), s)
+        ends.append(collide(f[h], s, TAU_COARSE))
     for i in range(NPOP):
         cx, cy, cz = (int(c) for c in VEL[i])
         halves = []
         for h in range(2):
-            v = jnp.where(outer, ends[h][i], middle[i, h])
+            v = jnp.where(row == 0, ends[h][i], middle[i, h])
+            v = jnp.where(row == ROWS - 1, roll_rows(ends[h][i], 5), v)
             if cx > 0:
-                v = jnp.where(row == 0, roll_rows(ends[h][i], 2), roll_rows(v, 1))
+                rim = rim_row(below, FORWARD.index(i), h, 1)
+                rim = jnp.where(pasted[h], roll_rows(ends[h][i], 2), rim)
+                v = jnp.where(row == 0, rim, roll_rows(v, 1))
             elif cx < 0:
-                v = jnp.where(row == ROWS - 1, roll_rows(ends[h][i], -2), roll_rows(v, -1))
+                rim = rim_row(above, BACKWARD.index(i), h, -1)
+                rim = jnp.where(pasted[h], roll_rows(ends[h][i], 3), rim)
+                v = jnp.where(row == ROWS - 1, rim, roll_rows(v, -1))
             halves.append(v)
         for h, v in enumerate(shift_plane(halves, cy, cz)):
             out[0, i, :, half_lanes(h)] = v
 
 
+def peers(groups):
+    return [0, *range(1, groups)]
+
+
 def held(array):
     return pltpu.with_memory_space_constraint(array, VMEM)
+
+
+def left(array):
+    return pltpu.with_memory_space_constraint(array, pltpu.HBM)
 
 
 def in_vmem(*shape):
@@ -385,17 +476,15 @@
 def per_device(fine_pops, fine_solid, coarse_pops, coarse_solid, coarse_slot):
     groups = lax.axis_size("grp")
     blocks = lax.axis_size("blk")
-    words = NPOP + 6
-    any_, smem = pl.ANY, pltpu.SMEM
     own, high, low = call(
         pack_kernel,
-        (fine_pops, fine_solid, coarse_pops, coarse_solid),
-        [any_] * 4,
-        [in_vmem(NPOP + 1, 2, *TILE), in_vmem(words, *TILE), in_vmem(words, *TILE)],
+        tuple(map(left, (fine_pops, fine_solid, coarse_pops, coarse_solid))),
+        [pl.ANY] * 4,
+        [in_vmem(NPOP + 1, 2, *TILE), in_vmem(WORDS, *TILE), in_vmem(WORDS, *TILE)],
         [
             in_vmem(NPOP + 1, ROWS, 2 * LANES),
-            in_vmem(2, NPOP + 1, 1, 2 * LANES),
-            pltpu.SemaphoreType.DMA((8,)),
+            in_vmem(NPOP + 1, *TILE),
+            pltpu.SemaphoreType.DMA((2,)),
         ],
         name="pack",
     )
@@ -406,28 +495,29 @@
 
     fine_v, solid_v = held(fine_pops), held(fine_solid)
     coarse_v, coarse_solid_v = held(coarse_pops), held(coarse_solid)
-    inner, packed_inner, chosen = call(
+    inner, packed_inner, chosen, moved = call(
         inner_kernel,
-        (fine_v, solid_v, coarse_slot),
-        [VMEM, VMEM, smem],
+        (fine_v, solid_v, held(own), held(coarse_slot)),
+        [VMEM] * 4,
         [
             in_vmem(NPOP, 2, 2 * ROWS, LANES),
             in_vmem((NPOP + 1) // 2, *TILE),
             in_vmem(2, groups, *TILE),
+            in_vmem(NPOP, 2, *TILE),
         ],
         [in_vmem(NPOP, 2, 2 * ROWS, LANES)],
         name="inner",
     )
 
     def around(array):
-        swaps = [[(i, i ^ s) for i in range(groups)] for s in range(1, groups)]
+        swaps = [[(i, i ^ s) for i in range(groups)] for s in peers(groups)[1:]]
         return [array] + [lax.ppermute(array, "grp", swap) for swap in swaps]
 
     inner_parts = around(packed_inner)
     edges, packed_edges = call(
         edge_kernel,
-        (held(own), held(below), held(above)),
-        [VMEM] * 3,
+        (held(own), held(moved), held(below), held(above)),
+        [VMEM] * 4,
         [in_vmem(NPOP, 2, *TILE), in_vmem((NPOP + 1) // 4, *TILE)],
         name="edge",
     )

time: 20.9 us -> 17 us (0.81)
  local copies, waits for them, and re-layouts: 3.3 us -> 0.02 us
  waiting for transfers between devices: 2.44 us -> 2.1 us
    unnamed x12 -> x10, local copies, waits for them, and re-layouts: 3.3 us -> 0.02 us
    ppermute x1, waiting for transfers between devices: 0.55 us -> 0.15 us  [per_device(): above = lax.ppermute(low, 'blk', backward)]
  transfers between devices with their start and end apart: 8 -> 8, of which waited for: 4 -> 3; matrix products, arithmetic and copies ran while one was open for 0% -> 0% of each run, Pallas kernels for 14% -> 13%
where the time goes in v2:
time: 17 us; the launch traced here: 16.8 us
  starting transfers between devices  9.9 us (58%)
  Pallas kernels  4.12 us (24%)
  waiting for transfers between devices  2.1 us (12%)
  between operations  0.68 us (4%)
    pallas_call x6, Pallas kernels, call(): pl.pallas_call(kernel, in_specs=[pl.BlockSpec(memory_space=s) for s in sp...  4.12 us
    ppermute x6, starting transfers between devices, around(): return [array] + [lax.ppermute(array, 'grp', swap) for swap in swaps]  3.77 us
    ppermute x1, starting transfers between devices, per_device(): above = lax.ppermute(low, 'blk', backward)  3.11 us
    ppermute x1, starting transfers between devices, per_device(): below = lax.ppermute(high, 'blk', forward)  3.02 us
    ppermute x6, waiting for transfers between devices, around(): return [array] + [lax.ppermute(array, 'grp', swap) for swap in swaps]  1.95 us
  transfers between devices with their start and end apart: 8, of which 3 were waited for; matrix products, arithmetic and copies ran while one was open for 0% of the time, Pallas kernels for 13%

profile of v2, /device:TPU:0, one launch (start us, length us, event | category | flops | bytes accessed | tf_op | source)
XLA Modules:
  0.0 16.8 jit_solution(16388003758556423841)
XLA Ops:
  0.6 0.0 copy-start.1
  0.6 0.0 copy-start.3
  0.6 1.0 %pack.1 = (f32[20,2,8,128]{3,2,1,0:T(8,128)S(1)}, f32[17,8,128]{2,1,0:T(8,128)S(1)}, f32[17,8,128]{2,1,0:T(8,128)S(1)}) custom-call(f32[1,19,16,256]{3,2,1,0:T(8,128)} %fine.3, f32[1,16,256]{2,1,0:T(8,128)} %solid.5, f32[1,19,8,256]{3,2,1,0:T(8,128)} %coarse.7, f32[1,8,256]{2,1,0:T(8,128)} %solid.7), custom_call_target="tpu_custom_call" | custom-call | bytes 1048576 | tf_op jit(solution)/shard_map/pack/pallas_call | solution.py:463
  1.6 3.0 %collective-permute-start = (f32[17,8,128]{2,1,0:T(8,128)S(1)}, f32[17,8,128]{2,1,0:T(8,128)S(1)}, u32[]{:S(2)}, u32[]{:S(2)}) collective-permute-start(f32[17,8,128]{2,1,0:T(8,128)S(1)} %get-tuple-element.14), channel_id=1, source_target_pairs={{0,1},{1,2},{2,3},{3,4},{4,5},{5,6},{6,7},{7,0},{8,9},{9,10},{10,1... | collective-permute-start | bytes 208904 | tf_op jit(solution)/shard_map/ppermute | solution.py:493
  4.7 0.0 copy-start.4
  4.7 3.1 %collective-permute-start.1 = (f32[17,8,128]{2,1,0:T(8,128)S(1)}, f32[17,8,128]{2,1,0:T(8,128)S(1)}, u32[]{:S(2)}, u32[]{:S(2)}) collective-permute-start(f32[17,8,128]{2,1,0:T(8,128)S(1)} %get-tuple-element.15), channel_id=1, source_target_pairs={{0,7},{1,0},{2,1},{3,2},{4,3},{5,4},{6,5},{7,6},{8,15},{9,8},{10,9... | collective-permute-start | bytes 208904 | tf_op jit(solution)/shard_map/ppermute | solution.py:494
  7.8 0.0 copy-done.1
  7.8 0.0 copy-done.3
  7.8 0.0 copy-done.4
  7.8 0.6 %inner.1 = (f32[19,2,16,128]{3,2,1,0:T(8,128)S(1)}, f32[10,8,128]{2,1,0:T(8,128)S(1)}, f32[2,4,8,128]{3,2,1,0:T(8,128)S(1)}, f32[19,2,8,128]{3,2,1,0:T(8,128)S(1)}) custom-call(f32[1,19,16,256]{3,2,1,0:T(8,128)S(1)} %copy-done.1, f32[1,16,256]{2,1,0:T(8,128)S(1)} %copy-done.3, f32[20,2,8,128]{3,2,1,0:T(8,128)S(1)} %get-tuple-element.11.own, s32[4]{0:T(128)S(1)} %copy-done.4), custom_call_target="tpu_custom_call" | custom-call | bytes 1048576 | tf_op jit(solution)/shard_map/inner/pallas_call | solution.py:463
  8.4 0.7 %collective-permute-start.4 = (f32[10,8,128]{2,1,0:T(8,128)S(1)}, f32[10,8,128]{2,1,0:T(8,128)S(1)}, u32[]{:S(2)}, u32[]{:S(2)}) collective-permute-start(f32[10,8,128]{2,1,0:T(8,128)S(1)} %get-tuple-element.18.refs_0_), channel_id=1, source_target_pairs={{0,24},{8,16},{16,8},{24,0},{1,25},{9,17},{17,9},{25,1},{2,26},{10... | collective-permute-start | bytes 122888 | tf_op jit(solution)/shard_map/ppermute | solution.py:514
  9.1 1.0 %collective-permute-start.3 = (f32[10,8,128]{2,1,0:T(8,128)S(1)}, f32[10,8,128]{2,1,0:T(8,128)S(1)}, u32[]{:S(2)}, u32[]{:S(2)}) collective-permute-start(f32[10,8,128]{2,1,0:T(8,128)S(1)} %get-tuple-element.18.refs_0_), channel_id=1, source_target_pairs={{0,16},{8,24},{16,0},{24,8},{1,17},{9,25},{17,1},{25,9},{2,18},{10... | collective-permute-start | bytes 122888 | tf_op jit(solution)/shard_map/ppermute | solution.py:514
  10.1 0.2 %collective-permute-start.2 = (f32[10,8,128]{2,1,0:T(8,128)S(1)}, f32[10,8,128]{2,1,0:T(8,128)S(1)}, u32[]{:S(2)}, u32[]{:S(2)}) collective-permute-start(f32[10,8,128]{2,1,0:T(8,128)S(1)} %get-tuple-element.18.refs_0_), channel_id=1, source_target_pairs={{0,8},{8,0},{16,24},{24,16},{1,9},{9,1},{17,25},{25,17},{2,10},{10... | collective-permute-start | bytes 122888 | tf_op jit(solution)/shard_map/ppermute | solution.py:514
  10.3 0.0 collective-permute-done.below
  10.3 0.1 collective-permute-done.1.above
  10.5 0.0 copy-start
  10.5 0.0 copy-start.2
  10.5 0.5 %edge.1 = (f32[19,2,8,128]{3,2,1,0:T(8,128)S(1)}, f32[5,8,128]{2,1,0:T(8,128)S(1)}) custom-call(f32[20,2,8,128]{3,2,1,0:T(8,128)S(1)} %get-tuple-element.11.own, f32[19,2,8,128]{3,2,1,0:T(8,128)S(1)} %get-tuple-element.13.moved, f32[17,8,128]{2,1,0:T(8,128)S(1)} %collective-permute-done.below, f32[17,8,128]{2,1,0:T(8,128)S(1)} %collective-permute-done.1.above), custom_call_target="tpu_custom_call" | custom-call | bytes 1048576 | tf_op jit(solution)/shard_map/edge/pallas_call | solution.py:463
  11.0 1.1 %collective-permute-start.7 = (f32[5,8,128]{2,1,0:T(8,128)S(1)}, f32[5,8,128]{2,1,0:T(8,128)S(1)}, u32[]{:S(2)}, u32[]{:S(2)}) collective-permute-start(f32[5,8,128]{2,1,0:T(8,128)S(1)} %get-tuple-element.19.refs_0_), channel_id=1, source_target_pairs={{0,24},{8,16},{16,8},{24,0},{1,25},{9,17},{17,9},{25,1},{2,26},{10... | collective-permute-start | bytes 61448 | tf_op jit(solution)/shard_map/ppermute | solution.py:514
  12.1 0.7 %collective-permute-start.6 = (f32[5,8,128]{2,1,0:T(8,128)S(1)}, f32[5,8,128]{2,1,0:T(8,128)S(1)}, u32[]{:S(2)}, u32[]{:S(2)}) collective-permute-start(f32[5,8,128]{2,1,0:T(8,128)S(1)} %get-tuple-element.19.refs_0_), channel_id=1, source_target_pairs={{0,16},{8,24},{16,0},{24,8},{1,17},{9,25},{17,1},{25,9},{2,18},{10... | collective-permute-start | bytes 61448 | tf_op jit(solution)/shard_map/ppermute | solution.py:514
  12.8 0.0 collective-permute-done.4.refs_3_
  12.8 0.1 collective-permute-start.5
  12.9 0.6 %collective-permute-done.3.refs_2_ = f32[10,8,128]{2,1,0:T(8,128)S(1)} collective-permute-done((f32[10,8,128]{2,1,0:T(8,128)S(1)}, f32[10,8,128]{2,1,0:T(8,128)S(1)}, u32[]{:S(2)}, u32[]{:S(2)}) %collective-permute-start.3) | collective-permute-done | bytes 40992 | tf_op jit(solution)/shard_map/ppermute | solution.py:514
  13.5 0.0 collective-permute-done.2.refs_1_
  13.5 0.0 copy-done
  13.5 0.0 copy-done.2
  13.5 0.3 %coarse.5.middle = f32[19,2,8,128]{3,2,1,0:T(8,128)S(1)} custom-call(f32[1,19,8,256]{3,2,1,0:T(8,128)S(1)} %copy-done, f32[1,8,256]{2,1,0:T(8,128)S(1)} %copy-done.2, f32[2,4,8,128]{3,2,1,0:T(8,128)S(1)} %get-tuple-element.17.chosen, f32[10,8,128]{2,1,0:T(8,128)S(1)} %get-tuple-element.18.refs_0_, f32[10,8,128]{2,1,0:T(8,128)S(1)} %collective-permute-done.2.refs_1_, ...), custom_call_target="tpu_custom_call" | custom-call | bytes 1048576 | tf_op jit(solution)/shard_map/coarse/pallas_call | solution.py:463
  13.7 0.8 %write.1 = f32[1,19,16,256]{3,2,1,0:T(8,128)} custom-call(f32[19,2,16,128]{3,2,1,0:T(8,128)S(1)} %get-tuple-element.12.inner, f32[19,2,8,128]{3,2,1,0:T(8,128)S(1)} %get-tuple-element.16.edges), custom_call_target="tpu_custom_call" | custom-call | bytes 1048576 | tf_op jit(solution)/shard_map/write/pallas_call | solution.py:463
  14.5 0.0 collective-permute-done.7.refs_3_
  14.5 1.3 %collective-permute-done.6.refs_2_ = f32[5,8,128]{2,1,0:T(8,128)S(1)} collective-permute-done((f32[5,8,128]{2,1,0:T(8,128)S(1)}, f32[5,8,128]{2,1,0:T(8,128)S(1)}, u32[]{:S(2)}, u32[]{:S(2)}) %collective-permute-start.6) | collective-permute-done | bytes 20512 | tf_op jit(solution)/shard_map/ppermute | solution.py:514
  15.9 0.0 collective-permute-done.5.refs_1_
  15.9 1.0 %last.1 = f32[1,19,8,256]{3,2,1,0:T(8,128)} custom-call(f32[1,19,8,256]{3,2,1,0:T(8,128)S(1)} %copy-done, f32[1,8,256]{2,1,0:T(8,128)S(1)} %copy-done.2, f32[2,4,8,128]{3,2,1,0:T(8,128)S(1)} %get-tuple-element.17.chosen, f32[17,8,128]{2,1,0:T(8,128)S(1)} %collective-permute-done.below, f32[17,8,128]{2,1,0:T(8,128)S(1)} %collective-permute-done.1.above, ...), custom_call_target="tpu_custom_call" | custom-call | bytes 1048576 | tf_op jit(solution)/shard_map/last/pallas_call | solution.py:463
Async XLA Ops:
  0.6 7.1 %copy-start.1 = (f32[1,19,16,256]{3,2,1,0:T(8,128)S(1)}, f32[1,19,16,256]{3,2,1,0:T(8,128)}, u32[]{:S(2)}) copy-start(f32[1,19,16,256]{3,2,1,0:T(8,128)} %fine.3) | copy-start | bytes 933892
  0.6 7.1 %copy-start.3 = (f32[1,16,256]{2,1,0:T(8,128)S(1)}, f32[1,16,256]{2,1,0:T(8,128)}, u32[]{:S(2)}) copy-start(f32[1,16,256]{2,1,0:T(8,128)} %solid.5) | copy-start | bytes 49156
  1.6 8.7 %collective-permute-start = (f32[17,8,128]{2,1,0:T(8,128)S(1)}, f32[17,8,128]{2,1,0:T(8,128)S(1)}, u32[]{:S(2)}, u32[]{:S(2)}) collective-permute-start(f32[17,8,128]{2,1,0:T(8,128)S(1)} %get-tuple-element.14), channel_id=1, source_target_pairs={{0,1},{1,2},{2,3},{3,4},{4,5},{5,6},{6,7},{7,0},{8,9},{9,10},{10,1... | collective-permute-start | bytes 208904 | tf_op jit(solution)/shard_map/ppermute | solution.py:493
  4.7 3.1 %copy-start.4 = (s32[4]{0:T(128)S(1)}, s32[4]{0:T(128)}, u32[]{:S(2)}) copy-start(s32[4]{0:T(128)} %slot.1) | copy-start | bytes 52
  4.7 5.8 %collective-permute-start.1 = (f32[17,8,128]{2,1,0:T(8,128)S(1)}, f32[17,8,128]{2,1,0:T(8,128)S(1)}, u32[]{:S(2)}, u32[]{:S(2)}) collective-permute-start(f32[17,8,128]{2,1,0:T(8,128)S(1)} %get-tuple-element.15), channel_id=1, source_target_pairs={{0,7},{1,0},{2,1},{3,2},{4,3},{5,4},{6,5},{7,6},{8,15},{9,8},{10,9... | collective-permute-start | bytes 208904 | tf_op jit(solution)/shard_map/ppermute | solution.py:494
  8.4 4.4 %collective-permute-start.4 = (f32[10,8,128]{2,1,0:T(8,128)S(1)}, f32[10,8,128]{2,1,0:T(8,128)S(1)}, u32[]{:S(2)}, u32[]{:S(2)}) collective-permute-start(f32[10,8,128]{2,1,0:T(8,128)S(1)} %get-tuple-element.18.refs_0_), channel_id=1, source_target_pairs={{0,24},{8,16},{16,8},{24,0},{1,25},{9,17},{17,9},{25,1},{2,26},{10... | collective-permute-start | bytes 122888 | tf_op jit(solution)/shard_map/ppermute | solution.py:514
  9.1 4.4 %collective-permute-start.3 = (f32[10,8,128]{2,1,0:T(8,128)S(1)}, f32[10,8,128]{2,1,0:T(8,128)S(1)}, u32[]{:S(2)}, u32[]{:S(2)}) collective-permute-start(f32[10,8,128]{2,1,0:T(8,128)S(1)} %get-tuple-element.18.refs_0_), channel_id=1, source_target_pairs={{0,16},{8,24},{16,0},{24,8},{1,17},{9,25},{17,1},{25,9},{2,18},{10... | collective-permute-start | bytes 122888 | tf_op jit(solution)/shard_map/ppermute | solution.py:514
  10.1 3.4 %collective-permute-start.2 = (f32[10,8,128]{2,1,0:T(8,128)S(1)}, f32[10,8,128]{2,1,0:T(8,128)S(1)}, u32[]{:S(2)}, u32[]{:S(2)}) collective-permute-start(f32[10,8,128]{2,1,0:T(8,128)S(1)} %get-tuple-element.18.refs_0_), channel_id=1, source_target_pairs={{0,8},{8,0},{16,24},{24,16},{1,9},{9,1},{17,25},{25,17},{2,10},{10... | collective-permute-start | bytes 122888 | tf_op jit(solution)/shard_map/ppermute | solution.py:514
  10.5 3.0 %copy-start = (f32[1,19,8,256]{3,2,1,0:T(8,128)S(1)}, f32[1,19,8,256]{3,2,1,0:T(8,128)}, u32[]{:S(2)}) copy-start(f32[1,19,8,256]{3,2,1,0:T(8,128)} %coarse.7) | copy-start | bytes 466948
  10.5 3.0 %copy-start.2 = (f32[1,8,256]{2,1,0:T(8,128)S(1)}, f32[1,8,256]{2,1,0:T(8,128)}, u32[]{:S(2)}) copy-start(f32[1,8,256]{2,1,0:T(8,128)} %solid.7) | copy-start | bytes 24580
  11.0 3.5 %collective-permute-start.7 = (f32[5,8,128]{2,1,0:T(8,128)S(1)}, f32[5,8,128]{2,1,0:T(8,128)S(1)}, u32[]{:S(2)}, u32[]{:S(2)}) collective-permute-start(f32[5,8,128]{2,1,0:T(8,128)S(1)} %get-tuple-element.19.refs_0_), channel_id=1, source_target_pairs={{0,24},{8,16},{16,8},{24,0},{1,25},{9,17},{17,9},{25,1},{2,26},{10... | collective-permute-start | bytes 61448 | tf_op jit(solution)/shard_map/ppermute | solution.py:514
  12.1 3.8 %collective-permute-start.6 = (f32[5,8,128]{2,1,0:T(8,128)S(1)}, f32[5,8,128]{2,1,0:T(8,128)S(1)}, u32[]{:S(2)}, u32[]{:S(2)}) collective-permute-start(f32[5,8,128]{2,1,0:T(8,128)S(1)} %get-tuple-element.19.refs_0_), channel_id=1, source_target_pairs={{0,16},{8,24},{16,0},{24,8},{1,17},{9,25},{17,1},{25,9},{2,18},{10... | collective-permute-start | bytes 61448 | tf_op jit(solution)/shard_map/ppermute | solution.py:514
  12.8 3.0 %collective-permute-start.5 = (f32[5,8,128]{2,1,0:T(8,128)S(1)}, f32[5,8,128]{2,1,0:T(8,128)S(1)}, u32[]{:S(2)}, u32[]{:S(2)}) collective-permute-start(f32[5,8,128]{2,1,0:T(8,128)S(1)} %get-tuple-element.19.refs_0_), channel_id=1, source_target_pairs={{0,8},{8,0},{16,24},{24,16},{1,9},{9,1},{17,25},{25,17},{2,10},{10... | collective-permute-start | bytes 61448 | tf_op jit(solution)/shard_map/ppermute | solution.py:514

commit v3 on v2

--- a/solution.py
+++ b/solution.py
@@ -318,13 +318,13 @@
     codes = slot[...].reshape(1, groups)
     group_ids = lax.broadcasted_iota(jnp.int32, codes.shape, 1)
     quadrant = 4 * me + lane_ids() % BX // 8
-    for s, other in enumerate(peers(groups)):
-        code = jnp.sum(jnp.where(group_ids == me ^ other, codes, 0), axis=1, keepdims=True)
+    for s in range(groups):
+        code = jnp.sum(jnp.where(group_ids == me ^ s, codes, 0), axis=1, keepdims=True)
         for h in range(2):
             chosen[h, s] = jnp.where(quadrant + 2 * h == code, 1.0, 0.0)
 
 
-def edge_kernel(own, moved, below, above, edges, packed):
+def edge_kernel(own, moved, below, above, coarse, coarse_solid, edges, packed):
     row = row_ids()
     upper = row < 4
     below = unpack_message(below, FORWARD, BACKWARD, 1)
@@ -376,23 +376,27 @@
             )
 
 
-def coarse_kernel(coarse, solid, chosen, *refs):
+def split_kernel(after, tiles, first, second):
+    half = first.shape[0]
+    first[...] = tiles[pl.ds(0, half)]
+    second[...] = tiles[pl.ds(half, half)]
+
+
+def paste_kernel(coarse, chosen, *refs):
     packed, out = refs[:-1], refs[-1]
-    f = [[], []]
+    groups = [1, *range(0, chosen.shape[1], 2)]
     for i in range(NPOP):
         tiles = [spread(m[i // 2], i % 2) for m in packed]
         for h in range(2):
             v = coarse[0, i, :, half_lanes(h)]
-            for s, tile in enumerate(tiles):
+            for s, tile in zip(groups, tiles):
                 v = jnp.where(chosen[h, s] > 0.5, tile, v)
-            f[h].append(v)
-    for h in range(2):
-        for i, v in enumerate(collide(f[h], solid[0, :, half_lanes(h)], TAU_COARSE)):
             out[i, h] = v
 
 
-def last_kernel(coarse, solid, chosen, below, above, middle, *refs):
-    packed, out = refs[:-1], refs[-1]
+def last_kernel(coarse, solid, chosen, below, above, base, *refs):
+    groups = chosen.shape[1]
+    packed, relayed, out = refs[:groups], refs[groups:-1], refs[-1]
     row = row_ids()
     masks = [[chosen[h, s] > 0.5 for s in range(len(packed))] for h in range(2)]
     pasted = []
@@ -415,6 +419,16 @@
                         here = coarse[0, i, :, half_lanes(h)]
                         here = jnp.where(row == 2, roll_rows(here, 3), here)
                         f[h][i] = jnp.where(pasted[h], tile, here)
+    middle = [[], []]
+    for i in range(NPOP):
+        half, at = divmod(i // 2, relayed[0].shape[0])
+        tiles = [spread(part[at], i % 2) for part in relayed[half::2]]
+        for h in range(2):
+            v = base[i, h]
+            for s, tile in enumerate(tiles):
+                v = jnp.where(masks[h][2 * s + 3], tile, v)
+            middle[h].append(v)
+    middle = [collide(middle[h], solid[0, :, half_lanes(h)], TAU_COARSE) for h in range(2)]
     ends = []
     for h in range(2):
         s = solid[0, :, half_lanes(h)]
@@ -426,7 +440,7 @@
         cx, cy, cz = (int(c) for c in VEL[i])
         halves = []
         for h in range(2):
-            v = jnp.where(row == 0, ends[h][i], middle[i, h])
+            v = jnp.where(row == 0, ends[h][i], middle[h][i])
             v = jnp.where(row == ROWS - 1, roll_rows(ends[h][i], 5), v)
             if cx > 0:
                 rim = rim_row(below, FORWARD.index(i), h, 1)
@@ -441,8 +455,9 @@
             out[0, i, :, half_lanes(h)] = v
 
 
-def peers(groups):
-    return [0, *range(1, groups)]
+def exchange(array, distance):
+    groups = lax.axis_size("grp")
+    return lax.ppermute(array, "grp", [(i, i ^ distance) for i in range(groups)])
 
 
 def held(array):
@@ -509,19 +524,16 @@
         name="inner",
     )
 
-    def around(array):
-        swaps = [[(i, i ^ s) for i in range(groups)] for s in peers(groups)[1:]]
-        return [array] + [lax.ppermute(array, "grp", swap) for swap in swaps]
-
-    inner_parts = around(packed_inner)
+    across = [exchange(packed_inner, s) for s in range(2, groups, 2)]
+    beside = exchange(packed_inner, 1)
     edges, packed_edges = call(
         edge_kernel,
-        (held(own), held(moved), held(below), held(above)),
-        [VMEM] * 4,
+        (held(own), held(moved), held(below), held(above), coarse_v, coarse_solid_v),
+        [VMEM] * 6,
         [in_vmem(NPOP, 2, *TILE), in_vmem((NPOP + 1) // 4, *TILE)],
         name="edge",
     )
-    edge_parts = around(packed_edges)
+    edge_parts = [packed_edges] + [exchange(packed_edges, s) for s in range(1, groups)]
     fine_out = call(
         write_kernel,
         (held(inner), held(edges)),
@@ -529,12 +541,23 @@
         jax.ShapeDtypeStruct(fine_pops.shape, jnp.float32),
         name="write",
     )
-    middle = call(
-        coarse_kernel,
-        (coarse_v, coarse_solid_v, held(chosen), *map(held, inner_parts)),
-        [VMEM] * (3 + groups),
+    relayed = []
+    for part in across:
+        halves = call(
+            split_kernel,
+            (held(edges), held(part)),
+            [VMEM] * 2,
+            [in_vmem(part.shape[0] // 2, *TILE)] * 2,
+            name="split",
+        )
+        relayed += [exchange(half, 1) for half in halves]
+    inner_parts = [beside, packed_inner, *across]
+    base = call(
+        paste_kernel,
+        (coarse_v, held(chosen), *map(held, inner_parts)),
+        [VMEM] * (2 + len(inner_parts)),
         in_vmem(NPOP, 2, *TILE),
-        name="coarse",
+        name="paste",
     )
     coarse_out = call(
         last_kernel,
@@ -544,10 +567,11 @@
             held(chosen),
             held(below),
             held(above),
-            held(middle),
+            held(base),
             *map(held, edge_parts),
+            *map(held, relayed),
         ),
-        [VMEM] * (6 + groups),
+        [VMEM] * (6 + len(edge_parts) + len(relayed)),
         jax.ShapeDtypeStruct(coarse_pops.shape, jnp.float32),
         name="last",
     )

time: 17 us -> 16.1 us (0.947)
  waiting for transfers between devices: 2.1 us -> 0.99 us
  starting transfers between devices: 9.9 us -> 10.2 us
    ppermute x6 -> x7, waiting for transfers between devices: 1.95 us -> 0.58 us  [exchange(): lax.ppermute(array, 'grp', [(i, i ^ distance) for i in range(groups)])]
    ppermute x6 -> x7, starting transfers between devices: 3.77 us -> 4.06 us  [exchange(): lax.ppermute(array, 'grp', [(i, i ^ distance) for i in range(groups)])]
    ppermute x1, waiting for transfers between devices: 0.15 us -> 0.41 us  [per_device(): above = lax.ppermute(low, 'blk', backward)]
    pallas_call x6 -> x7, Pallas kernels: 4.12 us -> 4.09 us  [call(): pl.pallas_call(kernel, in_specs=[pl.BlockSpec(memory_space=s) for s in sp...]
  transfers between devices with their start and end apart: 8 -> 9, of which waited for: 3 -> 2; matrix products, arithmetic and copies ran while one was open for 0% -> 0% of each run, Pallas kernels for 13% -> 13%
where the time goes in v3:
time: 16.1 us; the launch traced here: 16 us
  starting transfers between devices  10.2 us (63%)
  Pallas kernels  4.09 us (25%)
  waiting for transfers between devices  0.99 us (6%)
  between operations  0.69 us (4%)
    pallas_call x7, Pallas kernels, call(): pl.pallas_call(kernel, in_specs=[pl.BlockSpec(memory_space=s) for s in sp...  4.09 us
    ppermute x7, starting transfers between devices, exchange(): lax.ppermute(array, 'grp', [(i, i ^ distance) for i in range(groups)])  4.06 us
    ppermute x1, starting transfers between devices, per_device(): above = lax.ppermute(low, 'blk', backward)  3.11 us
    ppermute x1, starting transfers between devices, per_device(): below = lax.ppermute(high, 'blk', forward)  3.02 us
    ppermute x7, waiting for transfers between devices, exchange(): lax.ppermute(array, 'grp', [(i, i ^ distance) for i in range(groups)])  0.58 us
    ppermute x1, waiting for transfers between devices, per_device(): above = lax.ppermute(low, 'blk', backward)  0.41 us
  transfers between devices with their start and end apart: 9, of which 2 were waited for; matrix products, arithmetic and copies ran while one was open for 0% of the time, Pallas kernels for 13%

profile of v3, /device:TPU:0, one launch (start us, length us, event | category | flops | bytes accessed | tf_op | source)
XLA Modules:
  0.0 16.0 jit_solution(11393684962634715174)
XLA Ops:
  0.6 0.0 copy-start.1
  0.6 0.0 copy-start.3
  0.6 1.0 %pack.1 = (f32[20,2,8,128]{3,2,1,0:T(8,128)S(1)}, f32[17,8,128]{2,1,0:T(8,128)S(1)}, f32[17,8,128]{2,1,0:T(8,128)S(1)}) custom-call(f32[1,19,16,256]{3,2,1,0:T(8,128)} %fine.3, f32[1,16,256]{2,1,0:T(8,128)} %solid.4, f32[1,19,8,256]{3,2,1,0:T(8,128)} %coarse.7, f32[1,8,256]{2,1,0:T(8,128)} %solid.5), custom_call_target="tpu_custom_call" | custom-call | bytes 1048576 | tf_op jit(solution)/shard_map/pack/pallas_call | solution.py:478
  1.6 3.0 %collective-permute-start = (f32[17,8,128]{2,1,0:T(8,128)S(1)}, f32[17,8,128]{2,1,0:T(8,128)S(1)}, u32[]{:S(2)}, u32[]{:S(2)}) collective-permute-start(f32[17,8,128]{2,1,0:T(8,128)S(1)} %get-tuple-element.16), channel_id=1, source_target_pairs={{0,1},{1,2},{2,3},{3,4},{4,5},{5,6},{6,7},{7,0},{8,9},{9,10},{10,1... | collective-permute-start | bytes 208904 | tf_op jit(solution)/shard_map/ppermute | solution.py:508
  4.7 3.1 %collective-permute-start.1 = (f32[17,8,128]{2,1,0:T(8,128)S(1)}, f32[17,8,128]{2,1,0:T(8,128)S(1)}, u32[]{:S(2)}, u32[]{:S(2)}) collective-permute-start(f32[17,8,128]{2,1,0:T(8,128)S(1)} %get-tuple-element.17), channel_id=1, source_target_pairs={{0,7},{1,0},{2,1},{3,2},{4,3},{5,4},{6,5},{7,6},{8,15},{9,8},{10,9... | collective-permute-start | bytes 208904 | tf_op jit(solution)/shard_map/ppermute | solution.py:509
  7.8 0.0 copy-done.1
  7.8 0.0 copy-done.3
  7.8 0.0 copy-done.4
  7.8 0.0 copy-start.2
  7.8 0.6 %inner.1 = (f32[19,2,16,128]{3,2,1,0:T(8,128)S(1)}, f32[10,8,128]{2,1,0:T(8,128)S(1)}, f32[2,4,8,128]{3,2,1,0:T(8,128)S(1)}, f32[19,2,8,128]{3,2,1,0:T(8,128)S(1)}) custom-call(f32[1,19,16,256]{3,2,1,0:T(8,128)S(1)} %copy-done.1, f32[1,16,256]{2,1,0:T(8,128)S(1)} %copy-done.3, f32[20,2,8,128]{3,2,1,0:T(8,128)S(1)} %get-tuple-element.13.own, s32[4]{0:T(128)S(1)} %copy-done.4), custom_call_target="tpu_custom_call" | custom-call | bytes 1048576 | tf_op jit(solution)/shard_map/inner/pallas_call | solution.py:478
  8.4 1.6 %collective-permute-start.3 = (f32[10,8,128]{2,1,0:T(8,128)S(1)}, f32[10,8,128]{2,1,0:T(8,128)S(1)}, u32[]{:S(2)}, u32[]{:S(2)}) collective-permute-start(f32[10,8,128]{2,1,0:T(8,128)S(1)} %get-tuple-element.20.refs_1_), channel_id=1, source_target_pairs={{0,16},{8,24},{16,0},{24,8},{1,17},{9,25},{17,1},{25,9},{2,18},{10... | collective-permute-start | bytes 122888 | tf_op jit(solution)/shard_map/ppermute | solution.py:460
  10.0 0.0 collective-permute-start.2
  10.1 0.0 collective-permute-done.below
  10.1 0.4 %collective-permute-done.1.above = f32[17,8,128]{2,1,0:T(8,128)S(1)} collective-permute-done((f32[17,8,128]{2,1,0:T(8,128)S(1)}, f32[17,8,128]{2,1,0:T(8,128)S(1)}, u32[]{:S(2)}, u32[]{:S(2)}) %collective-permute-start.1) | collective-permute-done | bytes 69664 | tf_op jit(solution)/shard_map/ppermute | solution.py:509
  10.5 0.0 copy-done
  10.5 0.0 copy-done.2
  10.5 0.5 %edge.1 = (f32[19,2,8,128]{3,2,1,0:T(8,128)S(1)}, f32[5,8,128]{2,1,0:T(8,128)S(1)}) custom-call(f32[20,2,8,128]{3,2,1,0:T(8,128)S(1)} %get-tuple-element.13.own, f32[19,2,8,128]{3,2,1,0:T(8,128)S(1)} %get-tuple-element.15.moved, f32[17,8,128]{2,1,0:T(8,128)S(1)} %collective-permute-done.below, f32[17,8,128]{2,1,0:T(8,128)S(1)} %collective-permute-done.1.above, ...), custom_call_target="tpu_custom_call" | custom-call | bytes 1048576 | tf_op jit(solution)/shard_map/edge/pallas_call | solution.py:478
  11.0 0.2 %collective-permute-start.6 = (f32[5,8,128]{2,1,0:T(8,128)S(1)}, f32[5,8,128]{2,1,0:T(8,128)S(1)}, u32[]{:S(2)}, u32[]{:S(2)}) collective-permute-start(f32[5,8,128]{2,1,0:T(8,128)S(1)} %get-tuple-element.21.refs_0_), channel_id=1, source_target_pairs={{0,24},{8,16},{16,8},{24,0},{1,25},{9,17},{17,9},{25,1},{2,26},{10... | collective-permute-start | bytes 61448 | tf_op jit(solution)/shard_map/ppermute | solution.py:460
  11.2 1.6 %collective-permute-start.5 = (f32[5,8,128]{2,1,0:T(8,128)S(1)}, f32[5,8,128]{2,1,0:T(8,128)S(1)}, u32[]{:S(2)}, u32[]{:S(2)}) collective-permute-start(f32[5,8,128]{2,1,0:T(8,128)S(1)} %get-tuple-element.21.refs_0_), channel_id=1, source_target_pairs={{0,16},{8,24},{16,0},{24,8},{1,17},{9,25},{17,1},{25,9},{2,18},{10... | collective-permute-start | bytes 61448 | tf_op jit(solution)/shard_map/ppermute | solution.py:460
  12.8 0.1 collective-permute-start.4
  12.9 0.0 collective-permute-done.3.refs_2_.tiles
  12.9 0.4 %collective-permute-start.7 = (f32[5,8,128]{2,1,0:T(8,128)S(1)}, f32[5,8,128]{2,1,0:T(8,128)S(1)}, u32[]{:S(2)}, u32[]{:S(2)}) collective-permute-start(f32[5,8,128]{2,1,0:T(8,128)S(1)} %get-tuple-element.22), channel_id=1, source_target_pairs={{0,8},{8,0},{16,24},{24,16},{1,9},{9,1},{17,25},{25,17},{2,10},{10... | collective-permute-start | bytes 61448 | tf_op jit(solution)/shard_map/ppermute | solution.py:460
  13.3 0.0 collective-permute-done.2.refs_0_
  13.3 0.2 %collective-permute-start.8 = (f32[5,8,128]{2,1,0:T(8,128)S(1)}, f32[5,8,128]{2,1,0:T(8,128)S(1)}, u32[]{:S(2)}, u32[]{:S(2)}) collective-permute-start(f32[5,8,128]{2,1,0:T(8,128)S(1)} %get-tuple-element.23), channel_id=1, source_target_pairs={{0,8},{8,0},{16,24},{24,16},{1,9},{9,1},{17,25},{25,17},{2,10},{10... | collective-permute-start | bytes 61448 | tf_op jit(solution)/shard_map/ppermute | solution.py:460
  13.4 0.2 %paste.1.base = f32[19,2,8,128]{3,2,1,0:T(8,128)S(1)} custom-call(f32[1,19,8,256]{3,2,1,0:T(8,128)S(1)} %copy-done, f32[2,4,8,128]{3,2,1,0:T(8,128)S(1)} %get-tuple-element.19.chosen, f32[10,8,128]{2,1,0:T(8,128)S(1)} %collective-permute-done.2.refs_0_, f32[10,8,128]{2,1,0:T(8,128)S(1)} %get-tuple-element.20.refs_1_, ...), custom_call_target="tpu_custom_call" | custom-call | bytes 1048576 | tf_op jit(solution)/shard_map/paste/pallas_call | solution.py:478
  13.6 0.8 %write.1 = f32[1,19,16,256]{3,2,1,0:T(8,128)} custom-call(f32[19,2,16,128]{3,2,1,0:T(8,128)S(1)} %get-tuple-element.14.inner, f32[19,2,8,128]{3,2,1,0:T(8,128)S(1)} %get-tuple-element.18.edges.after), custom_call_target="tpu_custom_call" | custom-call | bytes 1048576 | tf_op jit(solution)/shard_map/write/pallas_call | solution.py:478
  14.4 0.0 collective-permute-done.6.refs_3_
  14.4 0.6 %collective-permute-done.5.refs_2_ = f32[5,8,128]{2,1,0:T(8,128)S(1)} collective-permute-done((f32[5,8,128]{2,1,0:T(8,128)S(1)}, f32[5,8,128]{2,1,0:T(8,128)S(1)}, u32[]{:S(2)}, u32[]{:S(2)}) %collective-permute-start.5) | collective-permute-done | bytes 20512 | tf_op jit(solution)/shard_map/ppermute | solution.py:460
  15.0 0.0 collective-permute-done.4.refs_1_
  15.0 0.0 collective-permute-done.7.refs_4_
  15.0 0.0 collective-permute-done.8.refs_5_
  15.0 1.0 %last.1 = f32[1,19,8,256]{3,2,1,0:T(8,128)} custom-call(f32[1,19,8,256]{3,2,1,0:T(8,128)S(1)} %copy-done, f32[1,8,256]{2,1,0:T(8,128)S(1)} %copy-done.2, f32[2,4,8,128]{3,2,1,0:T(8,128)S(1)} %get-tuple-element.19.chosen, f32[17,8,128]{2,1,0:T(8,128)S(1)} %collective-permute-done.below, f32[17,8,128]{2,1,0:T(8,128)S(1)} %collective-permute-done.1.above, ...), custom_call_target="tpu_custom_call" | custom-call | bytes 1048576 | tf_op jit(solution)/shard_map/last/pallas_call | solution.py:478
  (3 shorter events, 0.0 us)
Async XLA Ops:
  0.6 7.1 %copy-start.1 = (f32[1,19,16,256]{3,2,1,0:T(8,128)S(1)}, f32[1,19,16,256]{3,2,1,0:T(8,128)}, u32[]{:S(2)}) copy-start(f32[1,19,16,256]{3,2,1,0:T(8,128)} %fine.3) | copy-start | bytes 933892
  0.6 7.1 %copy-start.3 = (f32[1,16,256]{2,1,0:T(8,128)S(1)}, f32[1,16,256]{2,1,0:T(8,128)}, u32[]{:S(2)}) copy-start(f32[1,16,256]{2,1,0:T(8,128)} %solid.4) | copy-start | bytes 49156
  1.6 8.4 %collective-permute-start = (f32[17,8,128]{2,1,0:T(8,128)S(1)}, f32[17,8,128]{2,1,0:T(8,128)S(1)}, u32[]{:S(2)}, u32[]{:S(2)}) collective-permute-start(f32[17,8,128]{2,1,0:T(8,128)S(1)} %get-tuple-element.16), channel_id=1, source_target_pairs={{0,1},{1,2},{2,3},{3,4},{4,5},{5,6},{6,7},{7,0},{8,9},{9,10},{10,1... | collective-permute-start | bytes 208904 | tf_op jit(solution)/shard_map/ppermute | solution.py:508
  4.7 3.1 %copy-start.4 = (s32[4]{0:T(128)S(1)}, s32[4]{0:T(128)}, u32[]{:S(2)}) copy-start(s32[4]{0:T(128)} %slot.1) | copy-start | bytes 52
  4.7 5.8 %collective-permute-start.1 = (f32[17,8,128]{2,1,0:T(8,128)S(1)}, f32[17,8,128]{2,1,0:T(8,128)S(1)}, u32[]{:S(2)}, u32[]{:S(2)}) collective-permute-start(f32[17,8,128]{2,1,0:T(8,128)S(1)} %get-tuple-element.17), channel_id=1, source_target_pairs={{0,7},{1,0},{2,1},{3,2},{4,3},{5,4},{6,5},{7,6},{8,15},{9,8},{10,9... | collective-permute-start | bytes 208904 | tf_op jit(solution)/shard_map/ppermute | solution.py:509
  7.8 2.7 %copy-start = (f32[1,19,8,256]{3,2,1,0:T(8,128)S(1)}, f32[1,19,8,256]{3,2,1,0:T(8,128)}, u32[]{:S(2)}) copy-start(f32[1,19,8,256]{3,2,1,0:T(8,128)} %coarse.7) | copy-start | bytes 466948
  7.8 2.7 %copy-start.2 = (f32[1,8,256]{2,1,0:T(8,128)S(1)}, f32[1,8,256]{2,1,0:T(8,128)}, u32[]{:S(2)}) copy-start(f32[1,8,256]{2,1,0:T(8,128)} %solid.5) | copy-start | bytes 24580
  8.4 4.5 %collective-permute-start.3 = (f32[10,8,128]{2,1,0:T(8,128)S(1)}, f32[10,8,128]{2,1,0:T(8,128)S(1)}, u32[]{:S(2)}, u32[]{:S(2)}) collective-permute-start(f32[10,8,128]{2,1,0:T(8,128)S(1)} %get-tuple-element.20.refs_1_), channel_id=1, source_target_pairs={{0,16},{8,24},{16,0},{24,8},{1,17},{9,25},{17,1},{25,9},{2,18},{10... | collective-permute-start | bytes 122888 | tf_op jit(solution)/shard_map/ppermute | solution.py:460
  10.0 3.2 %collective-permute-start.2 = (f32[10,8,128]{2,1,0:T(8,128)S(1)}, f32[10,8,128]{2,1,0:T(8,128)S(1)}, u32[]{:S(2)}, u32[]{:S(2)}) collective-permute-start(f32[10,8,128]{2,1,0:T(8,128)S(1)} %get-tuple-element.20.refs_1_), channel_id=1, source_target_pairs={{0,8},{8,0},{16,24},{24,16},{1,9},{9,1},{17,25},{25,17},{2,10},{10... | collective-permute-start | bytes 122888 | tf_op jit(solution)/shard_map/ppermute | solution.py:460
  11.0 3.4 %collective-permute-start.6 = (f32[5,8,128]{2,1,0:T(8,128)S(1)}, f32[5,8,128]{2,1,0:T(8,128)S(1)}, u32[]{:S(2)}, u32[]{:S(2)}) collective-permute-start(f32[5,8,128]{2,1,0:T(8,128)S(1)} %get-tuple-element.21.refs_0_), channel_id=1, source_target_pairs={{0,24},{8,16},{16,8},{24,0},{1,25},{9,17},{17,9},{25,1},{2,26},{10... | collective-permute-start | bytes 61448 | tf_op jit(solution)/shard_map/ppermute | solution.py:460
  11.2 3.8 %collective-permute-start.5 = (f32[5,8,128]{2,1,0:T(8,128)S(1)}, f32[5,8,128]{2,1,0:T(8,128)S(1)}, u32[]{:S(2)}, u32[]{:S(2)}) collective-permute-start(f32[5,8,128]{2,1,0:T(8,128)S(1)} %get-tuple-element.21.refs_0_), channel_id=1, source_target_pairs={{0,16},{8,24},{16,0},{24,8},{1,17},{9,25},{17,1},{25,9},{2,18},{10... | collective-permute-start | bytes 61448 | tf_op jit(solution)/shard_map/ppermute | solution.py:460
  12.8 2.2 %collective-permute-start.4 = (f32[5,8,128]{2,1,0:T(8,128)S(1)}, f32[5,8,128]{2,1,0:T(8,128)S(1)}, u32[]{:S(2)}, u32[]{:S(2)}) collective-permute-start(f32[5,8,128]{2,1,0:T(8,128)S(1)} %get-tuple-element.21.refs_0_), channel_id=1, source_target_pairs={{0,8},{8,0},{16,24},{24,16},{1,9},{9,1},{17,25},{25,17},{2,10},{10... | collective-permute-start | bytes 61448 | tf_op jit(solution)/shard_map/ppermute | solution.py:460
  12.9 2.1 %collective-permute-start.7 = (f32[5,8,128]{2,1,0:T(8,128)S(1)}, f32[5,8,128]{2,1,0:T(8,128)S(1)}, u32[]{:S(2)}, u32[]{:S(2)}) collective-permute-start(f32[5,8,128]{2,1,0:T(8,128)S(1)} %get-tuple-element.22), channel_id=1, source_target_pairs={{0,8},{8,0},{16,24},{24,16},{1,9},{9,1},{17,25},{25,17},{2,10},{10... | collective-permute-start | bytes 61448 | tf_op jit(solution)/shard_map/ppermute | solution.py:460
  13.3 1.7 %collective-permute-start.8 = (f32[5,8,128]{2,1,0:T(8,128)S(1)}, f32[5,8,128]{2,1,0:T(8,128)S(1)}, u32[]{:S(2)}, u32[]{:S(2)}) collective-permute-start(f32[5,8,128]{2,1,0:T(8,128)S(1)} %get-tuple-element.23), channel_id=1, source_target_pairs={{0,8},{8,0},{16,24},{24,16},{1,9},{9,1},{17,25},{25,17},{2,10},{10... | collective-permute-start | bytes 61448 | tf_op jit(solution)/shard_map/ppermute | solution.py:460

commit v4 on v3

--- a/solution.py
+++ b/solution.py
@@ -188,47 +188,85 @@
 LEVEL = [i for i in range(NPOP) if VEL[i, 0] == 0]
 BACKWARD = [i for i in range(NPOP) if VEL[i, 0] < 0]
 MOVING = len(FORWARD)
-FIRST_LEVEL = MOVING
-FIRST_PAIR = FIRST_LEVEL + len(LEVEL)
-WORDS = FIRST_PAIR + (MOVING + 1) // 2
-FIRST_RIM = FIRST_LEVEL + 1
-
-
-def pack_message(message, tile, rim, towards, away, up):
-    place = row_ids() % 4
-    spare = place == (0 if up > 0 else 3)
-    near = place >= 2 if up > 0 else place < 2
-    for k, i in enumerate(towards):
-        message[k] = tile(i)
-    for k, i in enumerate(LEVEL):
-        other = roll_rows(tile(NPOP), -up) if k == 0 else rim(k - 1)
-        message[FIRST_LEVEL + k] = tile(i) if other is None else jnp.where(spare, other, tile(i))
-    for k in range((MOVING + 1) // 2):
-        second = away[2 * k + 1] if 2 * k + 1 < MOVING else NPOP
-        message[FIRST_PAIR + k] = jnp.where(near, tile(away[2 * k]), roll_rows(tile(second), -2 * up))
-
-
-def unpack_message(message, towards, away, up):
-    near = row_ids() % 4 >= 2 if up > 0 else row_ids() % 4 < 2
-    found = [None] * (NPOP + 1)
-    for k, i in enumerate(towards):
-        found[i] = message[k]
-    for k, i in enumerate(LEVEL):
-        found[i] = message[FIRST_LEVEL + k]
-    for k in range((MOVING + 1) // 2):
-        tile = message[FIRST_PAIR + k]
-        found[away[2 * k]] = tile
-        found[away[2 * k + 1] if 2 * k + 1 < MOVING else NPOP] = roll_rows(tile, 2 * up)
-    found[NPOP] = jnp.where(near, found[NPOP], roll_rows(message[FIRST_LEVEL], up))
-    return found
+
+PAIRS = (len(LEVEL) + 1) // 2
+FIRST_RIM = MOVING + PAIRS
+WORDS = FIRST_RIM + (MOVING + 1 + 3) // 4
+
+
+def pick(*choices):
+    row = row_ids()
+    out = choices[-1][-1]
+    for rows, tile in choices[-2::-1]:
+        mask = row == rows[0]
+        for r in rows[1:]:
+            mask = mask | (row == r)
+        out = jnp.where(mask, tile, out)
+    return out
+
+
+def pack_message(message, first, second, rim, up):
+    for k, i in enumerate(FORWARD if up else BACKWARD):
+        f, s = [first(i, h) for h in range(2)], [second(i, h) for h in range(2)]
+        if up:
+            message[k] = pick(
+                ((7, 0), roll_rows(f[0], 1)),
+                ((1, 2), roll_rows(f[1], 3)),
+                ((3, 4), roll_rows(s[0], -2)),
+                (s[1],),
+            )
+        else:
+            message[k] = pick(
+                ((3, 4), roll_rows(f[0], 3)),
+                ((5, 6), roll_rows(f[1], 5)),
+                ((7, 0), roll_rows(s[0], -2)),
+                (s[1],),
+            )
+    for k in range(PAIRS):
+        shared = []
+        for i in (LEVEL + [NPOP])[2 * k : 2 * k + 2]:
+            f = [first(i, h) for h in range(2)]
+            s = [second(i, h) for h in range(2)] if i < NPOP else f
+            if up:
+                shared.append(
+                    pick(
+                        ((7,), f[0]),
+                        ((1,), roll_rows(f[1], 2)),
+                        ((3,), roll_rows(s[0], -3)),
+                        (roll_rows(s[1], -1),),
+                    )
+                )
+            else:
+                shared.append(
+                    pick(
+                        ((4,), roll_rows(f[0], 4)),
+                        ((6,), roll_rows(f[1], -2)),
+                        ((0,), roll_rows(s[0], -1)),
+                        (roll_rows(s[1], 1),),
+                    )
+                )
+        own_rows = (1, 3, 5, 7) if up else (0, 2, 4, 6)
+        message[MOVING + k] = pick((own_rows, shared[0]), (roll_rows(shared[1], 1),))
+    for j in range(WORDS - FIRST_RIM):
+        tile = None
+        for k, v in enumerate(rim[4 * j : 4 * j + 4]):
+            v = roll_rows(v, k if up else -k)
+            at = k if up else 3 - k
+            tile = v if tile is None else jnp.where(row_ids() % 4 == at, v, tile)
+        message[FIRST_RIM + j] = tile
+
+
+def shared_tile(message, i):
+    k = (LEVEL + [NPOP]).index(i)
+    return roll_rows(message[MOVING + k // 2], -(k % 2))
 
 
 def rim_row(message, k, h, up):
-    row = (4, 0)[h] if up > 0 else (3, 7)[h]
-    return jnp.broadcast_to(message[FIRST_RIM + k, pl.ds(row, 1), :], TILE)
-
-
-def pack_kernel(fine, solid, coarse, coarse_solid, own, high, low, strip, rim, sem):
+    row = 4 * (1 - h) + k % 4 if up else 4 * h + 3 - k % 4
+    return jnp.broadcast_to(message[FIRST_RIM + k // 4, pl.ds(row, 1), :], TILE)
+
+
+def pack_kernel(fine, solid, coarse, coarse_solid, slot, moved, second, high, low, slot_out, strip, rim, sem):
     planes = fine.shape[2]
     last = coarse.shape[2] - 1
 
@@ -249,49 +287,48 @@
         target = rim.at[pl.ds(0, NPOP), pl.ds(row, 1), :]
         bring(coarse.at[0, :, pl.ds(plane, 1), half_lanes(h)], target, 1)
         bring(coarse_solid.at[0, pl.ds(plane, 1), half_lanes(h)], rim.at[NPOP, pl.ds(row, 1), :], 1)
+    bring(slot, slot_out, 2)
     arrive(strip, 0)
-    for h in range(2):
-        at = half_lanes(h)
-        s = strip[NPOP, :, at]
-        out = collide([strip[i, :, at] for i in range(NPOP)], s, TAU_FINE)
-        for i, v in enumerate(out + [s]):
-            own[i, h] = v
+    solids = [strip[NPOP, :, half_lanes(h)] for h in range(2)]
+    once = move_in_planes(
+        [collide([strip[i, :, half_lanes(h)] for i in range(NPOP)], solids[h], TAU_FINE) for h in range(2)]
+    )
+    arrive(slot_out, 2)
     arrive(rim.at[:, pl.ds(0, 4), :], 1)
     s = rim[NPOP]
-    ends = collide([rim[i] for i in range(NPOP)], s, TAU_COARSE) + [s]
-    upper = row_ids() < 4
-
-    def ending(i):
-        return jnp.where(upper, roll_rows(own[i, 1], 4), own[i, 0])
-
-    def beginning(i):
-        return jnp.where(upper, own[i, 0], roll_rows(own[i, 1], 4))
-
-    def rim_of(towards):
-        return lambda k: ends[(towards + [NPOP])[k]] if k <= MOVING else None
-
-    pack_message(high, ending, rim_of(FORWARD), FORWARD, BACKWARD, 1)
-    pack_message(low, beginning, rim_of(BACKWARD), BACKWARD, FORWARD, -1)
-
-
-def inner_kernel(fine, solid, own, slot, inner, packed, chosen, moved, work):
-    groups = chosen.shape[1]
+    outer = collide([rim[i] for i in range(NPOP)], s, TAU_COARSE) + [s]
+    ring = move_along([once])[0]
+    twice = [collide(ring[h], solids[h], TAU_FINE) for h in range(2)]
+    for h in range(2):
+        for i in range(NPOP):
+            moved[i, h] = once[h][i]
+            second[i, h] = twice[h][i]
+        moved[NPOP, h] = solids[h]
+
+    def first_of(i, h):
+        return moved[i, h]
+
+    def second_of(i, h):
+        return second[i, h]
+
+    pack_message(high, first_of, second_of, [outer[i] for i in FORWARD + [NPOP]], True)
+    pack_message(low, first_of, second_of, [outer[i] for i in BACKWARD + [NPOP]], False)
+
+
+def inner_steps(fine, solid, moved, inner, packed, work):
     upper = row_ids() < 4
 
     def middle(ref, h, *i):
         at = half_lanes(h)
         return jnp.where(upper, ref[(0, *i, pl.ds(ROWS, ROWS), at)], ref[(0, *i, pl.ds(0, ROWS), at)])
 
-    outer = move_in_planes([[own[i, h] for i in range(NPOP)] for h in range(2)])
+    outer = [[moved[i, h] for i in range(NPOP)] for h in range(2)]
     center = move_in_planes(
         [
             collide([middle(fine, h, i) for i in range(NPOP)], middle(solid, h), TAU_FINE)
             for h in range(2)
         ]
     )
-    for i in range(NPOP):
-        for h in range(2):
-            moved[i, h] = outer[h][i]
     ring = move_along([merge(upper, outer, center), merge(upper, center, outer)])
     for t in range(2):
         for h in range(2):
@@ -314,6 +351,22 @@
     out = restrict(mean) + [None]
     for j in range((NPOP + 1) // 2):
         packed[j] = pair_up(out[2 * j], out[2 * j + 1])
+
+
+def starts_early():
+    return lax.axis_index("blk") == 0
+
+
+def early_kernel(fine, solid, moved, low, inner, packed, low_out, work):
+    low_out[...] = low[...]
+
+    @pl.when(starts_early())
+    def _():
+        inner_steps(fine, solid, moved, inner, packed, work)
+
+
+def inner_kernel(fine, solid, moved, early_inner, early_packed, slot, inner, packed, chosen, work):
+    groups = chosen.shape[1]
     me = lax.axis_index("grp")
     codes = slot[...].reshape(1, groups)
     group_ids = lax.broadcasted_iota(jnp.int32, codes.shape, 1)
@@ -323,27 +376,70 @@
         for h in range(2):
             chosen[h, s] = jnp.where(quadrant + 2 * h == code, 1.0, 0.0)
 
-
-def edge_kernel(own, moved, below, above, coarse, coarse_solid, edges, packed):
+    @pl.when(starts_early())
+    def _():
+        inner[...] = early_inner[...]
+        packed[...] = early_packed[...]
+
+    @pl.when(jnp.logical_not(starts_early()))
+    def _():
+        inner_steps(fine, solid, moved, inner, packed, work)
+
+
+def edge_kernel(moved, second, below, above, coarse, coarse_solid, edges, packed):
     row = row_ids()
-    upper = row < 4
-    below = unpack_message(below, FORWARD, BACKWARD, 1)
-    above = unpack_message(above, BACKWARD, FORWARD, -1)
-    halos = [
-        [jnp.where(upper, a, b) for a, b in zip(above, below)],
-        [roll_rows(jnp.where(upper, b, a), 4) for a, b in zip(above, below)],
-    ]
-    solids = [(own[NPOP, h], halos[h][NPOP]) for h in range(2)]
-    halos = move_in_planes([half[:NPOP] for half in halos])
-    mine = [[moved[i, h] for i in range(NPOP)] for h in range(2)]
-    low, high = (
-        move_along([ring])[0] for ring in (merge(upper, mine, halos), merge(upper, halos, mine))
-    )
-    low = [collide(low[h], jnp.where(upper, *solids[h]), TAU_FINE) for h in range(2)]
-    high = [collide(high[h], jnp.where(upper, *solids[h][::-1]), TAU_FINE) for h in range(2)]
-    low, high = (move_along([ring])[0] for ring in (low, high))
-    high = [[roll_rows(v, 4) for v in half] for half in high]
-    both = move_in_planes(merge((row < 2) | (row >= 6), low, high))
+
+    def middle(i):
+        v = [moved[i, h] for h in range(2)]
+        if i in FORWARD:
+            return pick(
+                ((3, 4), roll_rows(v[0], -3)),
+                ((5, 6), roll_rows(v[1], -1)),
+                (below[FORWARD.index(i)],),
+            )
+        if i in BACKWARD:
+            return pick(
+                ((7, 0), roll_rows(v[0], -1)),
+                ((1, 2), roll_rows(v[1], 1)),
+                (above[BACKWARD.index(i)],),
+            )
+        return pick(
+            ((0,), v[0]),
+            ((2,), roll_rows(v[1], 2)),
+            ((3,), roll_rows(v[0], 4)),
+            ((5,), roll_rows(v[1], -2)),
+            ((1, 7), shared_tile(below, i)),
+            (shared_tile(above, i),),
+        )
+
+    twice = collide([middle(i) for i in range(NPOP)], middle(NPOP), TAU_FINE)
+    both = [[], []]
+    for h in range(2):
+        for i in range(NPOP):
+            cx = int(VEL[i, 0])
+            v, mine = roll_rows(twice[i], cx - 2 * h), second[i, h]
+            if cx > 0:
+                v = pick(
+                    ((0, 1, 4, 5), v),
+                    ((2, 3), roll_rows(mine, -3)),
+                    (roll_rows(below[FORWARD.index(i)], 3 - 2 * h),),
+                )
+            elif cx < 0:
+                v = pick(
+                    ((2, 3, 6, 7), v),
+                    ((0, 1), roll_rows(mine, -1)),
+                    (roll_rows(above[BACKWARD.index(i)], -3 - 2 * h),),
+                )
+            else:
+                v = pick(
+                    ((0, 3, 4, 7), v),
+                    ((1,), mine),
+                    ((2,), roll_rows(mine, 4)),
+                    ((6,), roll_rows(shared_tile(below, i), 3 - 2 * h)),
+                    (roll_rows(shared_tile(above, i), -3 - 2 * h),),
+                )
+            both[h].append(v)
+    both = move_in_planes(both)
     sums = [[v + roll_rows(v, -1) for v in half] + [None] for half in both]
     odd = row % 2 == 1
     mean = []
@@ -358,6 +454,7 @@
     ]
     for j in range(len(pairs) // 2):
         packed[j] = pair_up(pairs[2 * j], pairs[2 * j + 1])
+    packed[len(pairs) // 2] = jnp.zeros(TILE, jnp.float32)
     for i in range(NPOP):
         for h in range(2):
             edges[i, h] = both[h][i]
@@ -382,7 +479,7 @@
     second[...] = tiles[pl.ds(half, half)]
 
 
-def paste_kernel(coarse, chosen, *refs):
+def paste_kernel(after, coarse, chosen, *refs):
     packed, out = refs[:-1], refs[-1]
     groups = [1, *range(0, chosen.shape[1], 2)]
     for i in range(NPOP):
@@ -398,11 +495,11 @@
     groups = chosen.shape[1]
     packed, relayed, out = refs[:groups], refs[groups:-1], refs[-1]
     row = row_ids()
-    masks = [[chosen[h, s] > 0.5 for s in range(len(packed))] for h in range(2)]
+    masks = [[chosen[h, s] > 0.5 for s in others(groups)] for h in range(2)]
     pasted = []
     for h in range(2):
         total = chosen[h, 0]
-        for s in range(1, len(packed)):
+        for s in range(1, groups):
             total = total + chosen[h, s]
         pasted.append(total > 0.5)
     f = [[None] * NPOP, [None] * NPOP]
@@ -411,8 +508,8 @@
             tiles = [spread(m[j], which) for m in packed]
             for h in range(2):
                 chosen_tile = tiles[0]
-                for s in range(1, len(packed)):
-                    chosen_tile = jnp.where(masks[h][s], tiles[s], chosen_tile)
+                for mask, tile in zip(masks[h], tiles[1:]):
+                    chosen_tile = jnp.where(mask, tile, chosen_tile)
                 for i in (4 * j + 2 * which, 4 * j + 2 * which + 1):
                     if i < NPOP:
                         tile = roll_rows(chosen_tile, -(i % 2))
@@ -426,15 +523,15 @@
         for h in range(2):
             v = base[i, h]
             for s, tile in enumerate(tiles):
-                v = jnp.where(masks[h][2 * s + 3], tile, v)
+                v = jnp.where(chosen[h, 2 * s + 3] > 0.5, tile, v)
             middle[h].append(v)
     middle = [collide(middle[h], solid[0, :, half_lanes(h)], TAU_COARSE) for h in range(2)]
     ends = []
     for h in range(2):
         s = solid[0, :, half_lanes(h)]
         s = jnp.where(row == 2, roll_rows(s, 3), s)
-        s = jnp.where(row == 6, rim_row(below, MOVING, h, 1), s)
-        s = jnp.where(row == 4, rim_row(above, MOVING, h, -1), s)
+        s = jnp.where(row == 6, rim_row(below, MOVING, h, True), s)
+        s = jnp.where(row == 4, rim_row(above, MOVING, h, False), s)
         ends.append(collide(f[h], s, TAU_COARSE))
     for i in range(NPOP):
         cx, cy, cz = (int(c) for c in VEL[i])
@@ -443,16 +540,20 @@
             v = jnp.where(row == 0, ends[h][i], middle[h][i])
             v = jnp.where(row == ROWS - 1, roll_rows(ends[h][i], 5), v)
             if cx > 0:
-                rim = rim_row(below, FORWARD.index(i), h, 1)
+                rim = rim_row(below, FORWARD.index(i), h, True)
                 rim = jnp.where(pasted[h], roll_rows(ends[h][i], 2), rim)
                 v = jnp.where(row == 0, rim, roll_rows(v, 1))
             elif cx < 0:
-                rim = rim_row(above, BACKWARD.index(i), h, -1)
+                rim = rim_row(above, BACKWARD.index(i), h, False)
                 rim = jnp.where(pasted[h], roll_rows(ends[h][i], 3), rim)
                 v = jnp.where(row == ROWS - 1, rim, roll_rows(v, -1))
             halves.append(v)
         for h, v in enumerate(shift_plane(halves, cy, cz)):
             out[0, i, :, half_lanes(h)] = v
+
+
+def others(groups):
+    return range(1, groups)
 
 
 def exchange(array, distance):
@@ -491,36 +592,45 @@
 def per_device(fine_pops, fine_solid, coarse_pops, coarse_solid, coarse_slot):
     groups = lax.axis_size("grp")
     blocks = lax.axis_size("blk")
-    own, high, low = call(
+    moved, second, high, low, slot = call(
         pack_kernel,
-        tuple(map(left, (fine_pops, fine_solid, coarse_pops, coarse_solid))),
-        [pl.ANY] * 4,
-        [in_vmem(NPOP + 1, 2, *TILE), in_vmem(WORDS, *TILE), in_vmem(WORDS, *TILE)],
+        tuple(map(left, (fine_pops, fine_solid, coarse_pops, coarse_solid, coarse_slot))),
+        [pl.ANY] * 5,
+        [
+            in_vmem(NPOP + 1, 2, *TILE),
+            in_vmem(NPOP, 2, *TILE),
+            in_vmem(WORDS, *TILE),
+            in_vmem(WORDS, *TILE),
+            VMEM((groups,), jnp.int32),
+        ],
         [
             in_vmem(NPOP + 1, ROWS, 2 * LANES),
             in_vmem(NPOP + 1, *TILE),
-            pltpu.SemaphoreType.DMA((2,)),
+            pltpu.SemaphoreType.DMA((3,)),
         ],
         name="pack",
+    )
+    fine_v, solid_v = held(fine_pops), held(fine_solid)
+    coarse_v, coarse_solid_v = held(coarse_pops), held(coarse_solid)
+    inner_shapes = [in_vmem(NPOP, 2, 2 * ROWS, LANES), in_vmem((NPOP + 1) // 2, *TILE)]
+    early_inner, early_packed, low = call(
+        early_kernel,
+        (fine_v, solid_v, held(moved), held(low)),
+        [VMEM] * 4,
+        [*inner_shapes, in_vmem(WORDS, *TILE)],
+        inner_shapes[:1],
+        name="early",
     )
     forward = [(i, (i + 1) % blocks) for i in range(blocks)]
     backward = [(i, (i - 1) % blocks) for i in range(blocks)]
     below = lax.ppermute(high, "blk", forward)
     above = lax.ppermute(low, "blk", backward)
-
-    fine_v, solid_v = held(fine_pops), held(fine_solid)
-    coarse_v, coarse_solid_v = held(coarse_pops), held(coarse_solid)
-    inner, packed_inner, chosen, moved = call(
+    inner, packed_inner, chosen = call(
         inner_kernel,
-        (fine_v, solid_v, held(own), held(coarse_slot)),
-        [VMEM] * 4,
-        [
-            in_vmem(NPOP, 2, 2 * ROWS, LANES),
-            in_vmem((NPOP + 1) // 2, *TILE),
-            in_vmem(2, groups, *TILE),
-            in_vmem(NPOP, 2, *TILE),
-        ],
-        [in_vmem(NPOP, 2, 2 * ROWS, LANES)],
+        (fine_v, solid_v, held(moved), held(early_inner), held(early_packed), held(slot)),
+        [VMEM] * 6,
+        [*inner_shapes, in_vmem(2, groups, *TILE)],
+        inner_shapes[:1],
         name="inner",
     )
 
@@ -528,12 +638,12 @@
     beside = exchange(packed_inner, 1)
     edges, packed_edges = call(
         edge_kernel,
-        (held(own), held(moved), held(below), held(above), coarse_v, coarse_solid_v),
+        (held(moved), held(second), held(below), held(above), coarse_v, coarse_solid_v),
         [VMEM] * 6,
-        [in_vmem(NPOP, 2, *TILE), in_vmem((NPOP + 1) // 4, *TILE)],
+        [in_vmem(NPOP, 2, *TILE), in_vmem((NPOP + 1) // 4 + 1, *TILE)],
         name="edge",
     )
-    edge_parts = [packed_edges] + [exchange(packed_edges, s) for s in range(1, groups)]
+    edge_parts = [packed_edges] + [exchange(packed_edges, s) for s in others(groups)]
     fine_out = call(
         write_kernel,
         (held(inner), held(edges)),
@@ -541,24 +651,24 @@
         jax.ShapeDtypeStruct(fine_pops.shape, jnp.float32),
         name="write",
     )
+    inner_parts = [beside, packed_inner, *across]
+    base = call(
+        paste_kernel,
+        (held(edges), coarse_v, held(chosen), *map(held, inner_parts)),
+        [VMEM] * (3 + len(inner_parts)),
+        in_vmem(NPOP, 2, *TILE),
+        name="paste",
+    )
     relayed = []
     for part in across:
         halves = call(
             split_kernel,
-            (held(edges), held(part)),
+            (held(base), held(part)),
             [VMEM] * 2,
             [in_vmem(part.shape[0] // 2, *TILE)] * 2,
             name="split",
         )
         relayed += [exchange(half, 1) for half in halves]
-    inner_parts = [beside, packed_inner, *across]
-    base = call(
-        paste_kernel,
-        (coarse_v, held(chosen), *map(held, inner_parts)),
-        [VMEM] * (2 + len(inner_parts)),
-        in_vmem(NPOP, 2, *TILE),
-        name="paste",
-    )
     coarse_out = call(
         last_kernel,
         (

time: 16.1 us -> 15.7 us (0.975)
  starting transfers between devices: 10.2 us -> 9.69 us
    ppermute x1, starting transfers between devices: 3.11 us -> 2.51 us  [per_device(): above = lax.ppermute(low, 'blk', backward)]
    ppermute x1, waiting for transfers between devices: 0.41 us -> 0.14 us  [per_device(): above = lax.ppermute(low, 'blk', backward)]
    ppermute x1, waiting for transfers between devices: 0.01 us -> 0.21 us  [per_device(): below = lax.ppermute(high, 'blk', forward)]
    pallas_call x7 -> x8, Pallas kernels: 4.09 us -> 4.25 us  [call(): pl.pallas_call(kernel, in_specs=[pl.BlockSpec(memory_space=s) for s in sp...]
  transfers between devices with their start and end apart: 9 -> 9, of which waited for: 2 -> 4; matrix products, arithmetic and copies ran while one was open for 0% -> 0% of each run, Pallas kernels for 13% -> 13%
where the time goes in v4:
time: 15.7 us; the launch traced here: 15.6 us
  starting transfers between devices  9.69 us (62%)
  Pallas kernels  4.25 us (27%)
  waiting for transfers between devices  0.96 us (6%)
  between operations  0.69 us (4%)
    pallas_call x8, Pallas kernels, call(): pl.pallas_call(kernel, in_specs=[pl.BlockSpec(memory_space=s) for s in sp...  4.25 us
    ppermute x7, starting transfers between devices, exchange(): lax.ppermute(array, 'grp', [(i, i ^ distance) for i in range(groups)])  4.16 us
    ppermute x1, starting transfers between devices, per_device(): below = lax.ppermute(high, 'blk', forward)  3.02 us
    ppermute x1, starting transfers between devices, per_device(): above = lax.ppermute(low, 'blk', backward)  2.51 us
    ppermute x7, waiting for transfers between devices, exchange(): lax.ppermute(array, 'grp', [(i, i ^ distance) for i in range(groups)])  0.61 us
  transfers between devices with their start and end apart: 9, of which 4 were waited for; matrix products, arithmetic and copies ran while one was open for 0% of the time, Pallas kernels for 13%

profile of v4, /device:TPU:0, one launch (start us, length us, event | category | flops | bytes accessed | tf_op | source)
XLA Modules:
  0.0 15.6 jit_solution(10992584614661701927)
XLA Ops:
  0.6 0.0 copy-start
  0.6 0.0 copy-start.2
  0.6 1.2 %pack.1 = (f32[20,2,8,128]{3,2,1,0:T(8,128)S(1)}, f32[19,2,8,128]{3,2,1,0:T(8,128)S(1)}, f32[12,8,128]{2,1,0:T(8,128)S(1)}, f32[12,8,128]{2,1,0:T(8,128)S(1)}, s32[4]{0:T(128)S(1)}) custom-call(f32[1,19,16,256]{3,2,1,0:T(8,128)} %fine.5, f32[1,16,256]{2,1,0:T(8,128)} %solid.6, f32[1,19,8,256]{3,2,1,0:T(8,128)} %coarse.7, f32[1,8,256]{2,1,0:T(8,128)} %solid.7, ...), custom_call_target="tpu_custom_call" | custom-call | bytes 1048576 | tf_op jit(solution)/shard_map/pack/pallas_call | solution.py:579
  1.8 3.0 %collective-permute-start = (f32[12,8,128]{2,1,0:T(8,128)S(1)}, f32[12,8,128]{2,1,0:T(8,128)S(1)}, u32[]{:S(2)}, u32[]{:S(2)}) collective-permute-start(f32[12,8,128]{2,1,0:T(8,128)S(1)} %get-tuple-element.24), channel_id=1, source_target_pairs={{0,1},{1,2},{2,3},{3,4},{4,5},{5,6},{6,7},{7,0},{8,9},{9,10},{10,1... | collective-permute-start | bytes 147464 | tf_op jit(solution)/shard_map/ppermute | solution.py:626
  4.8 0.0 copy-done
  4.9 0.0 copy-done.2
  4.9 0.6 %early.1 = (f32[19,2,16,128]{3,2,1,0:T(8,128)S(1)}, f32[10,8,128]{2,1,0:T(8,128)S(1)}, f32[12,8,128]{2,1,0:T(8,128)S(1)}) custom-call(f32[1,19,16,256]{3,2,1,0:T(8,128)S(1)} %copy-done, f32[1,16,256]{2,1,0:T(8,128)S(1)} %copy-done.2, f32[20,2,8,128]{3,2,1,0:T(8,128)S(1)} %get-tuple-element.17.moved, f32[12,8,128]{2,1,0:T(8,128)S(1)} %get-tuple-element.18.low), custom_call_target="tpu_custom_call" | custom-call | bytes 1048576 | tf_op jit(solution)/shard_map/early/pallas_call | solution.py:579
  5.5 2.5 %collective-permute-start.1 = (f32[12,8,128]{2,1,0:T(8,128)S(1)}, f32[12,8,128]{2,1,0:T(8,128)S(1)}, u32[]{:S(2)}, u32[]{:S(2)}) collective-permute-start(f32[12,8,128]{2,1,0:T(8,128)S(1)} %get-tuple-element.25), channel_id=1, source_target_pairs={{0,7},{1,0},{2,1},{3,2},{4,3},{5,4},{6,5},{7,6},{8,15},{9,8},{10,9... | collective-permute-start | bytes 147464 | tf_op jit(solution)/shard_map/ppermute | solution.py:627
  8.0 0.0 copy-start.1
  8.0 0.1 inner.1
  8.1 1.7 %collective-permute-start.3 = (f32[10,8,128]{2,1,0:T(8,128)S(1)}, f32[10,8,128]{2,1,0:T(8,128)S(1)}, u32[]{:S(2)}, u32[]{:S(2)}) collective-permute-start(f32[10,8,128]{2,1,0:T(8,128)S(1)} %get-tuple-element.28.refs_1_), channel_id=1, source_target_pairs={{0,16},{8,24},{16,0},{24,8},{1,17},{9,25},{17,1},{25,9},{2,18},{10... | collective-permute-start | bytes 122888 | tf_op jit(solution)/shard_map/ppermute | solution.py:561
  9.8 0.0 collective-permute-start.2
  9.8 0.2 %collective-permute-done.below = f32[12,8,128]{2,1,0:T(8,128)S(1)} collective-permute-done((f32[12,8,128]{2,1,0:T(8,128)S(1)}, f32[12,8,128]{2,1,0:T(8,128)S(1)}, u32[]{:S(2)}, u32[]{:S(2)}) %collective-permute-start) | collective-permute-done | bytes 49184 | tf_op jit(solution)/shard_map/ppermute | solution.py:626
  10.0 0.1 collective-permute-done.1.above
  10.2 0.0 copy-done.1
  10.2 0.0 copy-done.3
  10.2 0.4 %edge.1 = (f32[19,2,8,128]{3,2,1,0:T(8,128)S(1)}, f32[6,8,128]{2,1,0:T(8,128)S(1)}) custom-call(f32[20,2,8,128]{3,2,1,0:T(8,128)S(1)} %get-tuple-element.17.moved, f32[19,2,8,128]{3,2,1,0:T(8,128)S(1)} %get-tuple-element.23.second, f32[12,8,128]{2,1,0:T(8,128)S(1)} %collective-permute-done.below, f32[12,8,128]{2,1,0:T(8,128)S(1)} %collective-permute-done.1.above, ...), custom_call_target="tpu_custom_call" | custom-call | bytes 1048576 | tf_op jit(solution)/shard_map/edge/pallas_call | solution.py:579
  10.6 0.2 %collective-permute-start.6 = (f32[6,8,128]{2,1,0:T(8,128)S(1)}, f32[6,8,128]{2,1,0:T(8,128)S(1)}, u32[]{:S(2)}, u32[]{:S(2)}) collective-permute-start(f32[6,8,128]{2,1,0:T(8,128)S(1)} %get-tuple-element.29.refs_0_), channel_id=1, source_target_pairs={{0,24},{8,16},{16,8},{24,0},{1,25},{9,17},{17,9},{25,1},{2,26},{10... | collective-permute-start | bytes 73736 | tf_op jit(solution)/shard_map/ppermute | solution.py:561
  10.8 1.6 %collective-permute-start.5 = (f32[6,8,128]{2,1,0:T(8,128)S(1)}, f32[6,8,128]{2,1,0:T(8,128)S(1)}, u32[]{:S(2)}, u32[]{:S(2)}) collective-permute-start(f32[6,8,128]{2,1,0:T(8,128)S(1)} %get-tuple-element.29.refs_0_), channel_id=1, source_target_pairs={{0,16},{8,24},{16,0},{24,8},{1,17},{9,25},{17,1},{25,9},{2,18},{10... | collective-permute-start | bytes 73736 | tf_op jit(solution)/shard_map/ppermute | solution.py:561
  12.4 0.1 collective-permute-start.4
  12.4 0.0 collective-permute-done.3.refs_2_.tiles
  12.4 0.0 collective-permute-done.2.refs_0_
  12.4 0.2 %paste.1.after.base = f32[19,2,8,128]{3,2,1,0:T(8,128)S(1)} custom-call(f32[19,2,8,128]{3,2,1,0:T(8,128)S(1)} %get-tuple-element.26.edges.after, f32[1,19,8,256]{3,2,1,0:T(8,128)S(1)} %copy-done.1, f32[2,4,8,128]{3,2,1,0:T(8,128)S(1)} %get-tuple-element.27.chosen, f32[10,8,128]{2,1,0:T(8,128)S(1)} %collective-permute-done.2.refs_0_, ...), custom_call_target="tpu_custom_call" | custom-call | bytes 1048576 | tf_op jit(solution)/shard_map/paste/pallas_call | solution.py:579
  12.6 0.5 %collective-permute-start.7 = (f32[5,8,128]{2,1,0:T(8,128)S(1)}, f32[5,8,128]{2,1,0:T(8,128)S(1)}, u32[]{:S(2)}, u32[]{:S(2)}) collective-permute-start(f32[5,8,128]{2,1,0:T(8,128)S(1)} %get-tuple-element.30), channel_id=1, source_target_pairs={{0,8},{8,0},{16,24},{24,16},{1,9},{9,1},{17,25},{25,17},{2,10},{10... | collective-permute-start | bytes 61448 | tf_op jit(solution)/shard_map/ppermute | solution.py:561
  13.2 0.1 collective-permute-start.8
  13.2 0.8 %write.1 = f32[1,19,16,256]{3,2,1,0:T(8,128)} custom-call(f32[19,2,16,128]{3,2,1,0:T(8,128)S(1)} %get-tuple-element.22.inner, f32[19,2,8,128]{3,2,1,0:T(8,128)S(1)} %get-tuple-element.26.edges.after), custom_call_target="tpu_custom_call" | custom-call | bytes 1048576 | tf_op jit(solution)/shard_map/write/pallas_call | solution.py:579
  14.0 0.0 collective-permute-done.7.refs_4_
  14.0 0.3 %collective-permute-done.8.refs_5_ = f32[5,8,128]{2,1,0:T(8,128)S(1)} collective-permute-done((f32[5,8,128]{2,1,0:T(8,128)S(1)}, f32[5,8,128]{2,1,0:T(8,128)S(1)}, u32[]{:S(2)}, u32[]{:S(2)}) %collective-permute-start.8) | collective-permute-done | bytes 20512 | tf_op jit(solution)/shard_map/ppermute | solution.py:561
  14.3 0.0 collective-permute-done.6.refs_3_
  14.3 0.2 %collective-permute-done.5.refs_2_ = f32[6,8,128]{2,1,0:T(8,128)S(1)} collective-permute-done((f32[6,8,128]{2,1,0:T(8,128)S(1)}, f32[6,8,128]{2,1,0:T(8,128)S(1)}, u32[]{:S(2)}, u32[]{:S(2)}) %collective-permute-start.5) | collective-permute-done | bytes 24608 | tf_op jit(solution)/shard_map/ppermute | solution.py:561
  14.6 0.0 collective-permute-done.4.refs_1_
  14.6 1.0 %last.1 = f32[1,19,8,256]{3,2,1,0:T(8,128)} custom-call(f32[1,19,8,256]{3,2,1,0:T(8,128)S(1)} %copy-done.1, f32[1,8,256]{2,1,0:T(8,128)S(1)} %copy-done.3, f32[2,4,8,128]{3,2,1,0:T(8,128)S(1)} %get-tuple-element.27.chosen, f32[12,8,128]{2,1,0:T(8,128)S(1)} %collective-permute-done.below, f32[12,8,128]{2,1,0:T(8,128)S(1)} %collective-permute-done.1.above, ...), custom_call_target="tpu_custom_call" | custom-call | bytes 1048576 | tf_op jit(solution)/shard_map/last/pallas_call | solution.py:579
  (2 shorter events, 0.0 us)
Async XLA Ops:
  0.6 4.2 %copy-start = (f32[1,19,16,256]{3,2,1,0:T(8,128)S(1)}, f32[1,19,16,256]{3,2,1,0:T(8,128)}, u32[]{:S(2)}) copy-start(f32[1,19,16,256]{3,2,1,0:T(8,128)} %fine.5) | copy-start | bytes 933892
  0.6 4.2 %copy-start.2 = (f32[1,16,256]{2,1,0:T(8,128)S(1)}, f32[1,16,256]{2,1,0:T(8,128)}, u32[]{:S(2)}) copy-start(f32[1,16,256]{2,1,0:T(8,128)} %solid.6) | copy-start | bytes 49156
  1.8 8.2 %collective-permute-start = (f32[12,8,128]{2,1,0:T(8,128)S(1)}, f32[12,8,128]{2,1,0:T(8,128)S(1)}, u32[]{:S(2)}, u32[]{:S(2)}) collective-permute-start(f32[12,8,128]{2,1,0:T(8,128)S(1)} %get-tuple-element.24), channel_id=1, source_target_pairs={{0,1},{1,2},{2,3},{3,4},{4,5},{5,6},{6,7},{7,0},{8,9},{9,10},{10,1... | collective-permute-start | bytes 147464 | tf_op jit(solution)/shard_map/ppermute | solution.py:626
  5.5 4.7 %collective-permute-start.1 = (f32[12,8,128]{2,1,0:T(8,128)S(1)}, f32[12,8,128]{2,1,0:T(8,128)S(1)}, u32[]{:S(2)}, u32[]{:S(2)}) collective-permute-start(f32[12,8,128]{2,1,0:T(8,128)S(1)} %get-tuple-element.25), channel_id=1, source_target_pairs={{0,7},{1,0},{2,1},{3,2},{4,3},{5,4},{6,5},{7,6},{8,15},{9,8},{10,9... | collective-permute-start | bytes 147464 | tf_op jit(solution)/shard_map/ppermute | solution.py:627
  8.0 2.2 %copy-start.1 = (f32[1,19,8,256]{3,2,1,0:T(8,128)S(1)}, f32[1,19,8,256]{3,2,1,0:T(8,128)}, u32[]{:S(2)}) copy-start(f32[1,19,8,256]{3,2,1,0:T(8,128)} %coarse.7) | copy-start | bytes 466948
  8.0 2.2 %copy-start.3 = (f32[1,8,256]{2,1,0:T(8,128)S(1)}, f32[1,8,256]{2,1,0:T(8,128)}, u32[]{:S(2)}) copy-start(f32[1,8,256]{2,1,0:T(8,128)} %solid.7) | copy-start | bytes 24580
  8.1 4.3 %collective-permute-start.3 = (f32[10,8,128]{2,1,0:T(8,128)S(1)}, f32[10,8,128]{2,1,0:T(8,128)S(1)}, u32[]{:S(2)}, u32[]{:S(2)}) collective-permute-start(f32[10,8,128]{2,1,0:T(8,128)S(1)} %get-tuple-element.28.refs_1_), channel_id=1, source_target_pairs={{0,16},{8,24},{16,0},{24,8},{1,17},{9,25},{17,1},{25,9},{2,18},{10... | collective-permute-start | bytes 122888 | tf_op jit(solution)/shard_map/ppermute | solution.py:561
  9.8 2.6 %collective-permute-start.2 = (f32[10,8,128]{2,1,0:T(8,128)S(1)}, f32[10,8,128]{2,1,0:T(8,128)S(1)}, u32[]{:S(2)}, u32[]{:S(2)}) collective-permute-start(f32[10,8,128]{2,1,0:T(8,128)S(1)} %get-tuple-element.28.refs_1_), channel_id=1, source_target_pairs={{0,8},{8,0},{16,24},{24,16},{1,9},{9,1},{17,25},{25,17},{2,10},{10... | collective-permute-start | bytes 122888 | tf_op jit(solution)/shard_map/ppermute | solution.py:561
  10.6 3.8 %collective-permute-start.6 = (f32[6,8,128]{2,1,0:T(8,128)S(1)}, f32[6,8,128]{2,1,0:T(8,128)S(1)}, u32[]{:S(2)}, u32[]{:S(2)}) collective-permute-start(f32[6,8,128]{2,1,0:T(8,128)S(1)} %get-tuple-element.29.refs_0_), channel_id=1, source_target_pairs={{0,24},{8,16},{16,8},{24,0},{1,25},{9,17},{17,9},{25,1},{2,26},{10... | collective-permute-start | bytes 73736 | tf_op jit(solution)/shard_map/ppermute | solution.py:561
  10.8 3.8 %collective-permute-start.5 = (f32[6,8,128]{2,1,0:T(8,128)S(1)}, f32[6,8,128]{2,1,0:T(8,128)S(1)}, u32[]{:S(2)}, u32[]{:S(2)}) collective-permute-start(f32[6,8,128]{2,1,0:T(8,128)S(1)} %get-tuple-element.29.refs_0_), channel_id=1, source_target_pairs={{0,16},{8,24},{16,0},{24,8},{1,17},{9,25},{17,1},{25,9},{2,18},{10... | collective-permute-start | bytes 73736 | tf_op jit(solution)/shard_map/ppermute | solution.py:561
  12.4 2.2 %collective-permute-start.4 = (f32[6,8,128]{2,1,0:T(8,128)S(1)}, f32[6,8,128]{2,1,0:T(8,128)S(1)}, u32[]{:S(2)}, u32[]{:S(2)}) collective-permute-start(f32[6,8,128]{2,1,0:T(8,128)S(1)} %get-tuple-element.29.refs_0_), channel_id=1, source_target_pairs={{0,8},{8,0},{16,24},{24,16},{1,9},{9,1},{17,25},{25,17},{2,10},{10... | collective-permute-start | bytes 73736 | tf_op jit(solution)/shard_map/ppermute | solution.py:561
  12.6 1.4 %collective-permute-start.7 = (f32[5,8,128]{2,1,0:T(8,128)S(1)}, f32[5,8,128]{2,1,0:T(8,128)S(1)}, u32[]{:S(2)}, u32[]{:S(2)}) collective-permute-start(f32[5,8,128]{2,1,0:T(8,128)S(1)} %get-tuple-element.30), channel_id=1, source_target_pairs={{0,8},{8,0},{16,24},{24,16},{1,9},{9,1},{17,25},{25,17},{2,10},{10... | collective-permute-start | bytes 61448 | tf_op jit(solution)/shard_map/ppermute | solution.py:561
  13.2 1.2 %collective-permute-start.8 = (f32[5,8,128]{2,1,0:T(8,128)S(1)}, f32[5,8,128]{2,1,0:T(8,128)S(1)}, u32[]{:S(2)}, u32[]{:S(2)}) collective-permute-start(f32[5,8,128]{2,1,0:T(8,128)S(1)} %get-tuple-element.31), channel_id=1, source_target_pairs={{0,8},{8,0},{16,24},{24,16},{1,9},{9,1},{17,25},{25,17},{2,10},{10... | collective-permute-start | bytes 61448 | tf_op jit(solution)/shard_map/ppermute | solution.py:561

commit v5 on v4

--- a/solution.py
+++ b/solution.py
@@ -159,25 +159,49 @@
     ]
 
 
-def squeeze(halves):
-    even = lane_ids() % 2 == 0
-    first = jnp.where(even, halves[0], roll_lanes(halves[1], 1))
-    second = jnp.where(even, roll_lanes(halves[0], -1), halves[1])
-    both = first + second
-    return both + roll_lanes(both, -BX)
+def means():
+    shape = (2 * LANES, LANES)
+    fine = lax.broadcasted_iota(jnp.int32, shape, 0)
+    place = lax.broadcasted_iota(jnp.int32, shape, 1)
+    same = (fine // (2 * BX) == place // BX) & (fine % BX // 2 == place % 8)
+    return jnp.where(same, 0.125, 0.0).astype(jnp.bfloat16)
+
+
+def squeeze(planes, matrix):
+    cells = jnp.concatenate([jnp.concatenate(halves, axis=1) for halves in planes], axis=0)
+    found = None
+    for _ in range(3):
+        part = cells.astype(jnp.bfloat16)
+        product = jnp.dot(part, matrix, preferred_element_type=jnp.float32)
+        found = product if found is None else found + product
+        cells = cells - part.astype(jnp.float32)
+    return [found[ROWS * k : ROWS * (k + 1)] for k in range(len(planes))]
+
+
+def lower():
+    return lane_ids() % BX < 8
 
 
 def pair_up(first, second):
-    if second is None:
-        return first
-    return jnp.where(lane_ids() // BX % 2 == 1, roll_lanes(second, BX), first)
-
-
-def spread(tile, which):
-    lane = lane_ids()
-    y, z = lane // BX, lane % BX
-    source = 2 * BX * (y % 4) + BX * which + 2 * (z % 8) + y // 4
-    return jnp.take_along_axis(tile, source, axis=1, mode="promise_in_bounds")
+    return first if second is None else jnp.where(lower(), first, second)
+
+
+def spread(first, second, which):
+    if which:
+        return jnp.where(lower(), roll_lanes(first, -8), second)
+    return jnp.where(lower(), first, roll_lanes(second, 8))
+
+
+def filled(chosen, h, sources):
+    low, high = (sum(chosen[2 * h + z, s] for s in sources) for z in range(2))
+    return jnp.where(lower(), low, high) > 0.5
+
+
+def choose(chosen, quadrant, tiles):
+    (_, out), *rest = tiles
+    for s, tile in rest:
+        out = jnp.where(chosen[quadrant, s] > 0.5, tile, out)
+    return out
 
 
 def half_lanes(h):
@@ -277,16 +301,14 @@
         pltpu.make_async_copy(target, target, sem.at[which]).wait()
 
     ends = ((0, 0), (planes - 4, 4))
-    for h in range(2):
-        at = half_lanes(h)
+    for half in (pl.ds(0, 10), pl.ds(10, 9)):
         for first, row in ends:
-            bring(fine.at[0, :, pl.ds(first, 4), at], strip.at[pl.ds(0, NPOP), pl.ds(row, 4), at], 0)
+            bring(fine.at[0, half, pl.ds(first, 4), :], strip.at[half, pl.ds(row, 4), :], 0)
     for first, row in ends:
         bring(solid.at[0, pl.ds(first, 4), :], strip.at[NPOP, pl.ds(row, 4), :], 0)
-    for plane, h, row in ((last, 1, 0), (last, 0, 4), (0, 0, 3), (0, 1, 7)):
-        target = rim.at[pl.ds(0, NPOP), pl.ds(row, 1), :]
-        bring(coarse.at[0, :, pl.ds(plane, 1), half_lanes(h)], target, 1)
-        bring(coarse_solid.at[0, pl.ds(plane, 1), half_lanes(h)], rim.at[NPOP, pl.ds(row, 1), :], 1)
+    for plane, row in ((last, 0), (0, 3)):
+        bring(coarse.at[0, :, pl.ds(plane, 1), :], rim.at[pl.ds(0, NPOP), pl.ds(row, 1), :], 1)
+        bring(coarse_solid.at[0, pl.ds(plane, 1), :], rim.at[NPOP, pl.ds(row, 1), :], 1)
     bring(slot, slot_out, 2)
     arrive(strip, 0)
     solids = [strip[NPOP, :, half_lanes(h)] for h in range(2)]
@@ -294,9 +316,14 @@
         [collide([strip[i, :, half_lanes(h)] for i in range(NPOP)], solids[h], TAU_FINE) for h in range(2)]
     )
     arrive(slot_out, 2)
-    arrive(rim.at[:, pl.ds(0, 4), :], 1)
-    s = rim[NPOP]
-    outer = collide([rim[i] for i in range(NPOP)], s, TAU_COARSE) + [s]
+    arrive(rim.at[:, pl.ds(0, 2), :], 1)
+
+    def rim_tile(i):
+        v = [rim[i, :, half_lanes(h)] for h in range(2)]
+        return pick(((0,), v[1]), ((3,), v[0]), ((4,), roll_rows(v[0], 4)), (roll_rows(v[1], 4),))
+
+    s = rim_tile(NPOP)
+    outer = collide([rim_tile(i) for i in range(NPOP)], s, TAU_COARSE) + [s]
     ring = move_along([once])[0]
     twice = [collide(ring[h], solids[h], TAU_FINE) for h in range(2)]
     for h in range(2):
@@ -312,6 +339,7 @@
         return second[i, h]
 
     pack_message(high, first_of, second_of, [outer[i] for i in FORWARD + [NPOP]], True)
+    high[WORDS] = jnp.zeros(TILE, jnp.float32)
     pack_message(low, first_of, second_of, [outer[i] for i in BACKWARD + [NPOP]], False)
 
 
@@ -341,14 +369,14 @@
             for t in range(2):
                 inner[i, h, pl.ds(ROWS * t, ROWS), :] = ring[t][h][i]
                 work[i, h, pl.ds(ROWS * t, ROWS), :] = ring[t][h][i]
-    mean = []
-    for i in range(NPOP):
-        halves = [
+    sums = [
+        [
             work[i, h, pl.ds(0, ROWS, stride=2), :] + work[i, h, pl.ds(1, ROWS, stride=2), :]
             for h in range(2)
         ]
-        mean.append(0.125 * squeeze(halves))
-    out = restrict(mean) + [None]
+        for i in range(NPOP)
+    ]
+    out = restrict(squeeze(sums, means())) + [None]
     for j in range((NPOP + 1) // 2):
         packed[j] = pair_up(out[2 * j], out[2 * j + 1])
 
@@ -365,16 +393,16 @@
         inner_steps(fine, solid, moved, inner, packed, work)
 
 
-def inner_kernel(fine, solid, moved, early_inner, early_packed, slot, inner, packed, chosen, work):
+def inner_kernel(fine, solid, moved, early_inner, early_packed, slot, inner, packed, padded, chosen, matrix, work):
     groups = chosen.shape[1]
+    matrix[...] = means()
     me = lax.axis_index("grp")
     codes = slot[...].reshape(1, groups)
     group_ids = lax.broadcasted_iota(jnp.int32, codes.shape, 1)
-    quadrant = 4 * me + lane_ids() % BX // 8
     for s in range(groups):
         code = jnp.sum(jnp.where(group_ids == me ^ s, codes, 0), axis=1, keepdims=True)
-        for h in range(2):
-            chosen[h, s] = jnp.where(quadrant + 2 * h == code, 1.0, 0.0)
+        for q in range(4):
+            chosen[q, s] = jnp.where(lane_ids() * 0 + (4 * me + q) == code, 1.0, 0.0)
 
     @pl.when(starts_early())
     def _():
@@ -385,8 +413,12 @@
     def _():
         inner_steps(fine, solid, moved, inner, packed, work)
 
-
-def edge_kernel(moved, second, below, above, coarse, coarse_solid, edges, packed):
+    size = packed.shape[0]
+    padded[pl.ds(0, size)] = packed[...]
+    padded[size] = jnp.zeros(TILE, jnp.float32)
+
+
+def edge_kernel(moved, second, below, above, matrix, coarse, coarse_solid, edges, packed):
     row = row_ids()
 
     def middle(i):
@@ -442,10 +474,12 @@
     both = move_in_planes(both)
     sums = [[v + roll_rows(v, -1) for v in half] + [None] for half in both]
     odd = row % 2 == 1
+    pairs = [
+        [half[i] if half[i + 1] is None else jnp.where(odd, roll_rows(half[i + 1], 1), half[i]) for half in sums]
+        for i in range(0, NPOP, 2)
+    ]
     mean = []
-    for i in range(0, NPOP, 2):
-        pair = [half[i] if half[i + 1] is None else jnp.where(odd, roll_rows(half[i + 1], 1), half[i]) for half in sums]
-        pair = 0.125 * squeeze(pair)
+    for pair in squeeze(pairs, matrix[...]):
         mean += [pair, roll_rows(pair, -1)]
     out = restrict(mean[:NPOP]) + [None]
     pairs = [
@@ -479,77 +513,117 @@
     second[...] = tiles[pl.ds(half, half)]
 
 
-def paste_kernel(after, coarse, chosen, *refs):
-    packed, out = refs[:-1], refs[-1]
-    groups = [1, *range(0, chosen.shape[1], 2)]
-    for i in range(NPOP):
-        tiles = [spread(m[i // 2], i % 2) for m in packed]
+def paste_inner(chosen, sources, tile, base, out):
+    masks = [filled(chosen, h, sources) for h in range(2)]
+    for j in range((NPOP + 1) // 2):
+        tiles = [(s, tile(s, j)) for s in sources]
         for h in range(2):
-            v = coarse[0, i, :, half_lanes(h)]
-            for s, tile in zip(groups, tiles):
-                v = jnp.where(chosen[h, s] > 0.5, tile, v)
-            out[i, h] = v
-
-
-def last_kernel(coarse, solid, chosen, below, above, base, *refs):
-    groups = chosen.shape[1]
-    packed, relayed, out = refs[:groups], refs[groups:-1], refs[-1]
-    row = row_ids()
-    masks = [[chosen[h, s] > 0.5 for s in others(groups)] for h in range(2)]
-    pasted = []
+            low, high = (choose(chosen, 2 * h + z, tiles) for z in range(2))
+            for i in range(2 * j, min(2 * j + 2, NPOP)):
+                out(i, h, jnp.where(masks[h], spread(low, high, i % 2), base(i, h)))
+
+
+def paste_kernel(after, coarse, solid, chosen, below, above, *refs):
+    *packed, out, ends = refs
+    sources = [1, *range(0, chosen.shape[1], 2)]
+    parts = dict(zip(sources, packed))
+
+    def write(i, h, tile):
+        out[i, h] = tile
+
+    paste_inner(
+        chosen, sources, lambda s, j: parts[s][j], lambda i, h: coarse[0, i, :, half_lanes(h)], write
+    )
+    for i in range(NPOP + 1):
+        v = [coarse[0, i, :, half_lanes(h)] if i < NPOP else solid[0, :, half_lanes(h)] for h in range(2)]
+        tile = pick(((0,), v[0]), ((1,), roll_rows(v[1], 1)), ((2,), roll_rows(v[0], 3)), (roll_rows(v[1], 4),))
+        if i == NPOP:
+            tile = pick(
+                ((4,), rim_row(above, MOVING, 0, False)),
+                ((5,), rim_row(above, MOVING, 1, False)),
+                ((6,), rim_row(below, MOVING, 0, True)),
+                ((7,), rim_row(below, MOVING, 1, True)),
+                (tile,),
+            )
+        ends[i] = tile
+
+
+def coarse_kernel(after, base, solid, chosen, *refs):
+    relayed, out = refs[:-1], refs[-1]
+    sources = [2 * k + 3 for k in range(len(relayed) // 2)]
+    f = [[None] * NPOP, [None] * NPOP]
+
+    def write(i, h, tile):
+        f[h][i] = tile
+
+    def tile(s, j):
+        half, at = divmod(j, relayed[0].shape[0])
+        return relayed[s - 3 + half][at]
+
+    paste_inner(chosen, sources, tile, lambda i, h: base[i, h], write)
+    f = move_in_planes([collide(f[h], solid[0, :, half_lanes(h)], TAU_COARSE) for h in range(2)])
     for h in range(2):
-        total = chosen[h, 0]
-        for s in range(1, groups):
-            total = total + chosen[h, s]
-        pasted.append(total > 0.5)
-    f = [[None] * NPOP, [None] * NPOP]
+        for i in range(NPOP):
+            out[i, h] = f[h][i]
+
+
+CHUNKS = (0, 3, 6, 9, 12, 15, 17, NPOP)
+
+
+def last_kernel(chosen, below, above, base, middle, *refs):
+    *packed, result, out, sem = refs
+    sources = [0, *others(len(packed))]
+    row, lane = row_ids(), lane_ids()
+    odd = row % 2 == 1
+    pasted = [filled(chosen, h, sources) for h in range(2)]
+    pasted = (odd & pasted[1]) | (~odd & pasted[0])
+    f = []
     for j in range((NPOP + 1) // 4):
+        tiles = [(s, part[j]) for s, part in zip(sources, packed)]
+        quadrants = [choose(chosen, q, tiles) for q in range(4)]
         for which in range(2):
-            tiles = [spread(m[j], which) for m in packed]
-            for h in range(2):
-                chosen_tile = tiles[0]
-                for mask, tile in zip(masks[h], tiles[1:]):
-                    chosen_tile = jnp.where(mask, tile, chosen_tile)
-                for i in (4 * j + 2 * which, 4 * j + 2 * which + 1):
-                    if i < NPOP:
-                        tile = roll_rows(chosen_tile, -(i % 2))
-                        here = coarse[0, i, :, half_lanes(h)]
-                        here = jnp.where(row == 2, roll_rows(here, 3), here)
-                        f[h][i] = jnp.where(pasted[h], tile, here)
-    middle = [[], []]
-    for i in range(NPOP):
-        half, at = divmod(i // 2, relayed[0].shape[0])
-        tiles = [spread(part[at], i % 2) for part in relayed[half::2]]
-        for h in range(2):
-            v = base[i, h]
-            for s, tile in enumerate(tiles):
-                v = jnp.where(chosen[h, 2 * s + 3] > 0.5, tile, v)
-            middle[h].append(v)
-    middle = [collide(middle[h], solid[0, :, half_lanes(h)], TAU_COARSE) for h in range(2)]
-    ends = []
-    for h in range(2):
-        s = solid[0, :, half_lanes(h)]
-        s = jnp.where(row == 2, roll_rows(s, 3), s)
-        s = jnp.where(row == 6, rim_row(below, MOVING, h, True), s)
-        s = jnp.where(row == 4, rim_row(above, MOVING, h, False), s)
-        ends.append(collide(f[h], s, TAU_COARSE))
+            v = [spread(quadrants[2 * h], quadrants[2 * h + 1], which) for h in range(2)]
+            f.append(jnp.where(odd, roll_rows(v[1], 1), v[0]))
+            f.append(jnp.where(odd, v[1], roll_rows(v[0], -1)))
+    f = [jnp.where(pasted, f[i], base[i]) for i in range(NPOP)]
+    f = collide(f, base[NPOP], TAU_COARSE)
+    copied = 0
     for i in range(NPOP):
         cx, cy, cz = (int(c) for c in VEL[i])
-        halves = []
+        v = f[i]
+        if cx:
+            k = (FORWARD if cx > 0 else BACKWARD).index(i)
+            rim = [rim_row(below if cx > 0 else above, k, h, cx > 0) for h in range(2)]
+            at = row >= 6 if cx > 0 else (row == 4) | (row == 5)
+            v = jnp.where(at & ~pasted, jnp.where(odd, rim[1], rim[0]), v)
+        if cz:
+            edge = lane % BX == (0 if cz > 0 else BX - 1)
+            v = jnp.where(
+                edge, roll_lanes(v, BX * cy + cz - BX * cz), roll_lanes(v, BX * cy + cz)
+            )
+        elif cy:
+            v = roll_lanes(v, BX * cy)
+        if cy:
+            carried = lane < BX if cy > 0 else lane >= LANES - BX
+            v = jnp.where(carried, jnp.where(odd, roll_rows(v, 1), roll_rows(v, -1)), v)
         for h in range(2):
-            v = jnp.where(row == 0, ends[h][i], middle[h][i])
-            v = jnp.where(row == ROWS - 1, roll_rows(ends[h][i], 5), v)
+            inside = middle[i, h]
             if cx > 0:
-                rim = rim_row(below, FORWARD.index(i), h, True)
-                rim = jnp.where(pasted[h], roll_rows(ends[h][i], 2), rim)
-                v = jnp.where(row == 0, rim, roll_rows(v, 1))
+                tile = pick(
+                    ((0,), roll_rows(v, 2 - h)), ((1,), roll_rows(v, 1 - h)), (roll_rows(inside, 1),)
+                )
             elif cx < 0:
-                rim = rim_row(above, BACKWARD.index(i), h, False)
-                rim = jnp.where(pasted[h], roll_rows(ends[h][i], 3), rim)
-                v = jnp.where(row == ROWS - 1, rim, roll_rows(v, -1))
-            halves.append(v)
-        for h, v in enumerate(shift_plane(halves, cy, cz)):
-            out[0, i, :, half_lanes(h)] = v
+                tile = pick(
+                    ((7,), roll_rows(v, 3 - h)), ((6,), roll_rows(v, 4 - h)), (roll_rows(inside, -1),)
+                )
+            else:
+                tile = pick(((0,), roll_rows(v, -h)), ((7,), roll_rows(v, 5 - h)), (inside,))
+            out[0, i, :, half_lanes(h)] = tile
+        if i + 1 in CHUNKS:
+            some = pl.ds(copied, i + 1 - copied)
+            pltpu.make_async_copy(out.at[0, some], result.at[0, some], sem).start()
+            copied = i + 1
+    pltpu.make_async_copy(out, result, sem).wait()
 
 
 def others(groups):
@@ -573,17 +647,17 @@
     return VMEM(shape, jnp.float32)
 
 
-def call(kernel, args, specs, outs, scratch=(), flops=0, name=None):
+def call(kernel, args, specs, outs, scratch=(), flops=0, name=None, out_space=VMEM):
     single = not isinstance(outs, (list, tuple))
     outs = [outs] if single else list(outs)
     result = pl.pallas_call(
         kernel,
         in_specs=[pl.BlockSpec(memory_space=s) for s in specs],
-        out_specs=[pl.BlockSpec(memory_space=VMEM)] * len(outs),
+        out_specs=[pl.BlockSpec(memory_space=out_space)] * len(outs),
         out_shape=outs,
         scratch_shapes=list(scratch),
         compiler_params=pltpu.CompilerParams(vmem_limit_bytes=24 << 20),
-        cost_estimate=pl.CostEstimate(flops=flops, bytes_accessed=1 << 20, transcendentals=0),
+        cost_estimate=pl.CostEstimate(flops=flops, bytes_accessed=1, transcendentals=0),
         name=name,
     )(*args)
     return result[0] if single else result
@@ -599,13 +673,13 @@
         [
             in_vmem(NPOP + 1, 2, *TILE),
             in_vmem(NPOP, 2, *TILE),
-            in_vmem(WORDS, *TILE),
+            in_vmem(WORDS + 1, *TILE),
             in_vmem(WORDS, *TILE),
             VMEM((groups,), jnp.int32),
         ],
         [
             in_vmem(NPOP + 1, ROWS, 2 * LANES),
-            in_vmem(NPOP + 1, *TILE),
+            in_vmem(NPOP + 1, ROWS, 2 * LANES),
             pltpu.SemaphoreType.DMA((3,)),
         ],
         name="pack",
@@ -625,21 +699,21 @@
     backward = [(i, (i - 1) % blocks) for i in range(blocks)]
     below = lax.ppermute(high, "blk", forward)
     above = lax.ppermute(low, "blk", backward)
-    inner, packed_inner, chosen = call(
+    inner, packed_inner, padded_inner, chosen, matrix = call(
         inner_kernel,
         (fine_v, solid_v, held(moved), held(early_inner), held(early_packed), held(slot)),
         [VMEM] * 6,
-        [*inner_shapes, in_vmem(2, groups, *TILE)],
+        [*inner_shapes, in_vmem((NPOP + 1) // 2 + 1, *TILE), in_vmem(4, groups, *TILE), VMEM((2 * LANES, LANES), jnp.bfloat16)],
         inner_shapes[:1],
         name="inner",
     )
 
     across = [exchange(packed_inner, s) for s in range(2, groups, 2)]
-    beside = exchange(packed_inner, 1)
+    beside = exchange(padded_inner, 1)
     edges, packed_edges = call(
         edge_kernel,
-        (held(moved), held(second), held(below), held(above), coarse_v, coarse_solid_v),
-        [VMEM] * 6,
+        (held(moved), held(second), held(below), held(above), held(matrix), coarse_v, coarse_solid_v),
+        [VMEM] * 7,
         [in_vmem(NPOP, 2, *TILE), in_vmem((NPOP + 1) // 4 + 1, *TILE)],
         name="edge",
     )
@@ -652,11 +726,19 @@
         name="write",
     )
     inner_parts = [beside, packed_inner, *across]
-    base = call(
+    base, ends = call(
         paste_kernel,
-        (held(edges), coarse_v, held(chosen), *map(held, inner_parts)),
-        [VMEM] * (3 + len(inner_parts)),
-        in_vmem(NPOP, 2, *TILE),
+        (
+            held(edges),
+            coarse_v,
+            coarse_solid_v,
+            held(chosen),
+            held(below),
+            held(above),
+            *map(held, inner_parts),
+        ),
+        [VMEM] * (6 + len(inner_parts)),
+        [in_vmem(NPOP, 2, *TILE), in_vmem(NPOP + 1, *TILE)],
         name="paste",
     )
     relayed = []
@@ -669,20 +751,20 @@
             name="split",
         )
         relayed += [exchange(half, 1) for half in halves]
+    middle = call(
+        coarse_kernel,
+        (left(fine_out), held(base), coarse_solid_v, held(chosen), *map(held, relayed)),
+        [pl.ANY] + [VMEM] * (3 + len(relayed)),
+        in_vmem(NPOP, 2, *TILE),
+        name="coarse",
+    )
     coarse_out = call(
         last_kernel,
-        (
-            coarse_v,
-            coarse_solid_v,
-            held(chosen),
-            held(below),
-            held(above),
-            held(base),
-            *map(held, edge_parts),
-            *map(held, relayed),
-        ),
-        [VMEM] * (6 + len(edge_parts) + len(relayed)),
+        (held(chosen), held(below), held(above), held(ends), held(middle), *map(held, edge_parts)),
+        [VMEM] * (5 + len(edge_parts)),
         jax.ShapeDtypeStruct(coarse_pops.shape, jnp.float32),
+        [in_vmem(*coarse_pops.shape), pltpu.SemaphoreType.DMA],
+        out_space=pl.ANY,
         name="last",
     )
     return fine_out, coarse_out

time: 15.7 us -> 15.6 us (level)
  waiting for transfers between devices: 0.96 us -> 0.63 us
    ppermute x7, waiting for transfers between devices: 0.61 us -> 0.33 us  [exchange(): lax.ppermute(array, 'grp', [(i, i ^ distance) for i in range(groups)])]
    ppermute x1, waiting for transfers between devices: 0.21 us -> 0.01 us  [per_device(): below = lax.ppermute(high, 'blk', forward)]
    pallas_call x8 -> x9, Pallas kernels: 4.25 us -> 4.3 us  [call(): pl.pallas_call(kernel, in_specs=[pl.BlockSpec(memory_space=s) for s in sp...]
  transfers between devices with their start and end apart: 9 -> 9, of which waited for: 4 -> 3; matrix products, arithmetic and copies ran while one was open for 0% -> 0% of each run, Pallas kernels for 13% -> 15%
where the time goes in v5:
time: 15.6 us; the launch traced here: 15.4 us
  starting transfers between devices  9.77 us (63%)
  Pallas kernels  4.3 us (28%)
  between operations  0.74 us (5%)
  waiting for transfers between devices  0.63 us (4%)
    pallas_call x9, Pallas kernels, call(): pl.pallas_call(kernel, in_specs=[pl.BlockSpec(memory_space=s) for s in sp...  4.3 us
    ppermute x7, starting transfers between devices, exchange(): lax.ppermute(array, 'grp', [(i, i ^ distance) for i in range(groups)])  4.25 us
    ppermute x1, starting transfers between devices, per_device(): below = lax.ppermute(high, 'blk', forward)  3.02 us
    ppermute x1, starting transfers between devices, per_device(): above = lax.ppermute(low, 'blk', backward)  2.49 us
    ppermute x7, waiting for transfers between devices, exchange(): lax.ppermute(array, 'grp', [(i, i ^ distance) for i in range(groups)])  0.33 us
  transfers between devices with their start and end apart: 9, of which 3 were waited for; matrix products, arithmetic and copies ran while one was open for 0% of the time, Pallas kernels for 15%

profile of v5, /device:TPU:0, one launch (start us, length us, event | category | flops | bytes accessed | tf_op | source)
XLA Modules:
  0.0 15.4 jit_solution(7744280870776285967)
XLA Ops:
  0.6 0.0 copy-start
  0.6 0.0 copy-start.2
  0.6 1.2 %pack.1 = (f32[20,2,8,128]{3,2,1,0:T(8,128)S(1)}, f32[19,2,8,128]{3,2,1,0:T(8,128)S(1)}, f32[13,8,128]{2,1,0:T(8,128)S(1)}, f32[12,8,128]{2,1,0:T(8,128)S(1)}, s32[4]{0:T(128)S(1)}) custom-call(f32[1,19,16,256]{3,2,1,0:T(8,128)} %fine.5, f32[1,16,256]{2,1,0:T(8,128)} %solid.7, f32[1,19,8,256]{3,2,1,0:T(8,128)} %coarse.6, f32[1,8,256]{2,1,0:T(8,128)} %solid.9, ...), custom_call_target="tpu_custom_call" | custom-call | bytes 1 | tf_op jit(solution)/shard_map/pack/pallas_call | solution.py:653
  1.8 3.0 %collective-permute-start = (f32[13,8,128]{2,1,0:T(8,128)S(1)}, f32[13,8,128]{2,1,0:T(8,128)S(1)}, u32[]{:S(2)}, u32[]{:S(2)}) collective-permute-start(f32[13,8,128]{2,1,0:T(8,128)S(1)} %get-tuple-element.28), channel_id=1, source_target_pairs={{0,1},{1,2},{2,3},{3,4},{4,5},{5,6},{6,7},{7,0},{8,9},{9,10},{10,1... | collective-permute-start | bytes 159752 | tf_op jit(solution)/shard_map/ppermute | solution.py:700
  4.9 0.0 copy-done
  4.9 0.0 copy-done.2
  4.9 0.6 %early.1 = (f32[19,2,16,128]{3,2,1,0:T(8,128)S(1)}, f32[10,8,128]{2,1,0:T(8,128)S(1)}, f32[12,8,128]{2,1,0:T(8,128)S(1)}) custom-call(f32[1,19,16,256]{3,2,1,0:T(8,128)S(1)} %copy-done, f32[1,16,256]{2,1,0:T(8,128)S(1)} %copy-done.2, f32[20,2,8,128]{3,2,1,0:T(8,128)S(1)} %get-tuple-element.21.moved, f32[12,8,128]{2,1,0:T(8,128)S(1)} %get-tuple-element.22.low), custom_call_target="tpu_custom_call" | custom-call | bytes 1 | tf_op jit(solution)/shard_map/early/pallas_call | solution.py:653
  5.5 2.5 %collective-permute-start.1 = (f32[12,8,128]{2,1,0:T(8,128)S(1)}, f32[12,8,128]{2,1,0:T(8,128)S(1)}, u32[]{:S(2)}, u32[]{:S(2)}) collective-permute-start(f32[12,8,128]{2,1,0:T(8,128)S(1)} %get-tuple-element.29), channel_id=1, source_target_pairs={{0,7},{1,0},{2,1},{3,2},{4,3},{5,4},{6,5},{7,6},{8,15},{9,8},{10,9... | collective-permute-start | bytes 147464 | tf_op jit(solution)/shard_map/ppermute | solution.py:701
  8.0 0.2 %inner.1 = (f32[19,2,16,128]{3,2,1,0:T(8,128)S(1)}, f32[10,8,128]{2,1,0:T(8,128)S(1)}, f32[11,8,128]{2,1,0:T(8,128)S(1)}, f32[4,4,8,128]{3,2,1,0:T(8,128)S(1)}, bf16[256,128]{1,0:T(8,128)(2,1)S(1)}) custom-call(f32[1,19,16,256]{3,2,1,0:T(8,128)S(1)} %copy-done, f32[1,16,256]{2,1,0:T(8,128)S(1)} %copy-done.2, f32[20,2,8,128]{3,2,1,0:T(8,128)S(1)} %get-tuple-element.21.moved, ...), custom_call_target="tpu_custom_call" | custom-call | bytes 1 | tf_op jit(solution)/shard_map/inner/pallas_call | solution.py:653
  8.2 0.1 collective-permute-start.2
  8.3 1.7 %collective-permute-start.3 = (f32[10,8,128]{2,1,0:T(8,128)S(1)}, f32[10,8,128]{2,1,0:T(8,128)S(1)}, u32[]{:S(2)}, u32[]{:S(2)}) collective-permute-start(f32[10,8,128]{2,1,0:T(8,128)S(1)} %get-tuple-element.34.refs_1_), channel_id=1, source_target_pairs={{0,16},{8,24},{16,0},{24,8},{1,17},{9,25},{17,1},{25,9},{2,18},{10... | collective-permute-start | bytes 122888 | tf_op jit(solution)/shard_map/ppermute | solution.py:635
  10.0 0.3 %collective-permute-done.1.above = f32[12,8,128]{2,1,0:T(8,128)S(1)} collective-permute-done((f32[12,8,128]{2,1,0:T(8,128)S(1)}, f32[12,8,128]{2,1,0:T(8,128)S(1)}, u32[]{:S(2)}, u32[]{:S(2)}) %collective-permute-start.1) | collective-permute-done | bytes 49184 | tf_op jit(solution)/shard_map/ppermute | solution.py:701
  10.3 0.0 collective-permute-done.below
  10.3 0.0 copy-done.1
  10.3 0.0 copy-done.3
  10.3 0.3 %edge.1 = (f32[19,2,8,128]{3,2,1,0:T(8,128)S(1)}, f32[6,8,128]{2,1,0:T(8,128)S(1)}) custom-call(f32[20,2,8,128]{3,2,1,0:T(8,128)S(1)} %get-tuple-element.21.moved, f32[19,2,8,128]{3,2,1,0:T(8,128)S(1)} %get-tuple-element.27.second, f32[13,8,128]{2,1,0:T(8,128)S(1)} %collective-permute-done.below, f32[12,8,128]{2,1,0:T(8,128)S(1)} %collective-permute-done.1.above, ...), custom_call_target="tpu_custom_call" | custom-call | bytes 1 | tf_op jit(solution)/shard_map/edge/pallas_call | solution.py:653
  10.6 0.1 collective-permute-start.8
  10.7 1.5 %collective-permute-start.7 = (f32[6,8,128]{2,1,0:T(8,128)S(1)}, f32[6,8,128]{2,1,0:T(8,128)S(1)}, u32[]{:S(2)}, u32[]{:S(2)}) collective-permute-start(f32[6,8,128]{2,1,0:T(8,128)S(1)} %get-tuple-element.39.refs_0_), channel_id=1, source_target_pairs={{0,16},{8,24},{16,0},{24,8},{1,17},{9,25},{17,1},{25,9},{2,18},{10... | collective-permute-start | bytes 73736 | tf_op jit(solution)/shard_map/ppermute | solution.py:635
  12.2 0.3 %collective-permute-start.6 = (f32[6,8,128]{2,1,0:T(8,128)S(1)}, f32[6,8,128]{2,1,0:T(8,128)S(1)}, u32[]{:S(2)}, u32[]{:S(2)}) collective-permute-start(f32[6,8,128]{2,1,0:T(8,128)S(1)} %get-tuple-element.39.refs_0_), channel_id=1, source_target_pairs={{0,8},{8,0},{16,24},{24,16},{1,9},{9,1},{17,25},{25,17},{2,10},{10... | collective-permute-start | bytes 73736 | tf_op jit(solution)/shard_map/ppermute | solution.py:635
  12.5 0.0 collective-permute-done.3.refs_2_.tiles
  12.6 0.0 collective-permute-done.2.refs_0_
  12.6 0.1 paste.1
  12.7 0.3 %collective-permute-start.4 = (f32[5,8,128]{2,1,0:T(8,128)S(1)}, f32[5,8,128]{2,1,0:T(8,128)S(1)}, u32[]{:S(2)}, u32[]{:S(2)}) collective-permute-start(f32[5,8,128]{2,1,0:T(8,128)S(1)} %get-tuple-element.37), channel_id=1, source_target_pairs={{0,8},{8,0},{16,24},{24,16},{1,9},{9,1},{17,25},{25,17},{2,10},{10... | collective-permute-start | bytes 61448 | tf_op jit(solution)/shard_map/ppermute | solution.py:635
  13.0 0.3 %collective-permute-start.5 = (f32[5,8,128]{2,1,0:T(8,128)S(1)}, f32[5,8,128]{2,1,0:T(8,128)S(1)}, u32[]{:S(2)}, u32[]{:S(2)}) collective-permute-start(f32[5,8,128]{2,1,0:T(8,128)S(1)} %get-tuple-element.38), channel_id=1, source_target_pairs={{0,8},{8,0},{16,24},{24,16},{1,9},{9,1},{17,25},{25,17},{2,10},{10... | collective-permute-start | bytes 61448 | tf_op jit(solution)/shard_map/ppermute | solution.py:635
  13.3 0.8 %write.1.after = f32[1,19,16,256]{3,2,1,0:T(8,128)} custom-call(f32[19,2,16,128]{3,2,1,0:T(8,128)S(1)} %get-tuple-element.26.inner, f32[19,2,8,128]{3,2,1,0:T(8,128)S(1)} %get-tuple-element.31.edges.after), custom_call_target="tpu_custom_call" | custom-call | bytes 1 | tf_op jit(solution)/shard_map/write/pallas_call | solution.py:653
  14.0 0.0 collective-permute-done.4.refs_0_
  14.0 0.1 collective-permute-done.5.refs_1_
  14.2 0.2 %coarse.7.middle = f32[19,2,8,128]{3,2,1,0:T(8,128)S(1)} custom-call(f32[1,19,16,256]{3,2,1,0:T(8,128)} %write.1.after, f32[19,2,8,128]{3,2,1,0:T(8,128)S(1)} %get-tuple-element.36.after.base, f32[1,8,256]{2,1,0:T(8,128)S(1)} %copy-done.3, f32[4,4,8,128]{3,2,1,0:T(8,128)S(1)} %get-tuple-element.32.chosen, f32[5,8,128]{2,1,0:T(8,128)S(1)} %collective-permute-done.4.refs_0_, ...), custom_call_target="tpu_custom_call" | custom-call | bytes 1 | tf_op jit(solution)/shard_map/coarse/pallas_call | solution.py:653
  14.4 0.0 collective-permute-done.8.refs_3_
  14.4 0.2 %collective-permute-done.7.refs_2_ = f32[6,8,128]{2,1,0:T(8,128)S(1)} collective-permute-done((f32[6,8,128]{2,1,0:T(8,128)S(1)}, f32[6,8,128]{2,1,0:T(8,128)S(1)}, u32[]{:S(2)}, u32[]{:S(2)}) %collective-permute-start.7) | collective-permute-done | bytes 24608 | tf_op jit(solution)/shard_map/ppermute | solution.py:635
  14.6 0.0 collective-permute-done.6.refs_1_
  14.6 0.8 %last.1 = f32[1,19,8,256]{3,2,1,0:T(8,128)} custom-call(f32[4,4,8,128]{3,2,1,0:T(8,128)S(1)} %get-tuple-element.32.chosen, f32[13,8,128]{2,1,0:T(8,128)S(1)} %collective-permute-done.below, f32[12,8,128]{2,1,0:T(8,128)S(1)} %collective-permute-done.1.above, f32[20,8,128]{2,1,0:T(8,128)S(1)} %get-tuple-element.35.base, f32[19,2,8,128]{3,2,1,0:T(8,128)S(1)} %coarse.7.middle, ...), custom_call_target="tpu_custom_call" | custom-call | bytes 1 | tf_op jit(solution)/shard_map/last/pallas_call | solution.py:653
  (3 shorter events, 0.0 us)
Async XLA Ops:
  0.6 4.2 %copy-start = (f32[1,19,16,256]{3,2,1,0:T(8,128)S(1)}, f32[1,19,16,256]{3,2,1,0:T(8,128)}, u32[]{:S(2)}) copy-start(f32[1,19,16,256]{3,2,1,0:T(8,128)} %fine.5) | copy-start | bytes 933892
  0.6 4.2 %copy-start.2 = (f32[1,16,256]{2,1,0:T(8,128)S(1)}, f32[1,16,256]{2,1,0:T(8,128)}, u32[]{:S(2)}) copy-start(f32[1,16,256]{2,1,0:T(8,128)} %solid.7) | copy-start | bytes 49156
  1.8 8.4 %collective-permute-start = (f32[13,8,128]{2,1,0:T(8,128)S(1)}, f32[13,8,128]{2,1,0:T(8,128)S(1)}, u32[]{:S(2)}, u32[]{:S(2)}) collective-permute-start(f32[13,8,128]{2,1,0:T(8,128)S(1)} %get-tuple-element.28), channel_id=1, source_target_pairs={{0,1},{1,2},{2,3},{3,4},{4,5},{5,6},{6,7},{7,0},{8,9},{9,10},{10,1... | collective-permute-start | bytes 159752 | tf_op jit(solution)/shard_map/ppermute | solution.py:700
  5.5 4.7 %collective-permute-start.1 = (f32[12,8,128]{2,1,0:T(8,128)S(1)}, f32[12,8,128]{2,1,0:T(8,128)S(1)}, u32[]{:S(2)}, u32[]{:S(2)}) collective-permute-start(f32[12,8,128]{2,1,0:T(8,128)S(1)} %get-tuple-element.29), channel_id=1, source_target_pairs={{0,7},{1,0},{2,1},{3,2},{4,3},{5,4},{6,5},{7,6},{8,15},{9,8},{10,9... | collective-permute-start | bytes 147464 | tf_op jit(solution)/shard_map/ppermute | solution.py:701
  8.0 2.3 %copy-start.1 = (f32[1,19,8,256]{3,2,1,0:T(8,128)S(1)}, f32[1,19,8,256]{3,2,1,0:T(8,128)}, u32[]{:S(2)}) copy-start(f32[1,19,8,256]{3,2,1,0:T(8,128)} %coarse.6) | copy-start | bytes 466948
  8.0 2.3 %copy-start.3 = (f32[1,8,256]{2,1,0:T(8,128)S(1)}, f32[1,8,256]{2,1,0:T(8,128)}, u32[]{:S(2)}) copy-start(f32[1,8,256]{2,1,0:T(8,128)} %solid.9) | copy-start | bytes 24580
  8.2 4.4 %collective-permute-start.2 = (f32[11,8,128]{2,1,0:T(8,128)S(1)}, f32[11,8,128]{2,1,0:T(8,128)S(1)}, u32[]{:S(2)}, u32[]{:S(2)}) collective-permute-start(f32[11,8,128]{2,1,0:T(8,128)S(1)} %get-tuple-element.33), channel_id=1, source_target_pairs={{0,8},{8,0},{16,24},{24,16},{1,9},{9,1},{17,25},{25,17},{2,10},{10... | collective-permute-start | bytes 135176 | tf_op jit(solution)/shard_map/ppermute | solution.py:635
  8.3 4.3 %collective-permute-start.3 = (f32[10,8,128]{2,1,0:T(8,128)S(1)}, f32[10,8,128]{2,1,0:T(8,128)S(1)}, u32[]{:S(2)}, u32[]{:S(2)}) collective-permute-start(f32[10,8,128]{2,1,0:T(8,128)S(1)} %get-tuple-element.34.refs_1_), channel_id=1, source_target_pairs={{0,16},{8,24},{16,0},{24,8},{1,17},{9,25},{17,1},{25,9},{2,18},{10... | collective-permute-start | bytes 122888 | tf_op jit(solution)/shard_map/ppermute | solution.py:635
  10.6 3.8 %collective-permute-start.8 = (f32[6,8,128]{2,1,0:T(8,128)S(1)}, f32[6,8,128]{2,1,0:T(8,128)S(1)}, u32[]{:S(2)}, u32[]{:S(2)}) collective-permute-start(f32[6,8,128]{2,1,0:T(8,128)S(1)} %get-tuple-element.39.refs_0_), channel_id=1, source_target_pairs={{0,24},{8,16},{16,8},{24,0},{1,25},{9,17},{17,9},{25,1},{2,26},{10... | collective-permute-start | bytes 73736 | tf_op jit(solution)/shard_map/ppermute | solution.py:635
  10.7 3.9 %collective-permute-start.7 = (f32[6,8,128]{2,1,0:T(8,128)S(1)}, f32[6,8,128]{2,1,0:T(8,128)S(1)}, u32[]{:S(2)}, u32[]{:S(2)}) collective-permute-start(f32[6,8,128]{2,1,0:T(8,128)S(1)} %get-tuple-element.39.refs_0_), channel_id=1, source_target_pairs={{0,16},{8,24},{16,0},{24,8},{1,17},{9,25},{17,1},{25,9},{2,18},{10... | collective-permute-start | bytes 73736 | tf_op jit(solution)/shard_map/ppermute | solution.py:635
  12.2 2.3 %collective-permute-start.6 = (f32[6,8,128]{2,1,0:T(8,128)S(1)}, f32[6,8,128]{2,1,0:T(8,128)S(1)}, u32[]{:S(2)}, u32[]{:S(2)}) collective-permute-start(f32[6,8,128]{2,1,0:T(8,128)S(1)} %get-tuple-element.39.refs_0_), channel_id=1, source_target_pairs={{0,8},{8,0},{16,24},{24,16},{1,9},{9,1},{17,25},{25,17},{2,10},{10... | collective-permute-start | bytes 73736 | tf_op jit(solution)/shard_map/ppermute | solution.py:635
  12.7 1.3 %collective-permute-start.4 = (f32[5,8,128]{2,1,0:T(8,128)S(1)}, f32[5,8,128]{2,1,0:T(8,128)S(1)}, u32[]{:S(2)}, u32[]{:S(2)}) collective-permute-start(f32[5,8,128]{2,1,0:T(8,128)S(1)} %get-tuple-element.37), channel_id=1, source_target_pairs={{0,8},{8,0},{16,24},{24,16},{1,9},{9,1},{17,25},{25,17},{2,10},{10... | collective-permute-start | bytes 61448 | tf_op jit(solution)/shard_map/ppermute | solution.py:635
  13.0 1.2 %collective-permute-start.5 = (f32[5,8,128]{2,1,0:T(8,128)S(1)}, f32[5,8,128]{2,1,0:T(8,128)S(1)}, u32[]{:S(2)}, u32[]{:S(2)}) collective-permute-start(f32[5,8,128]{2,1,0:T(8,128)S(1)} %get-tuple-element.38), channel_id=1, source_target_pairs={{0,8},{8,0},{16,24},{24,16},{1,9},{9,1},{17,25},{25,17},{2,10},{10... | collective-permute-start | bytes 61448 | tf_op jit(solution)/shard_map/ppermute | solution.py:635

commit v6 on v5

--- a/solution.py
+++ b/solution.py
@@ -178,6 +178,27 @@
     return [found[ROWS * k : ROWS * (k + 1)] for k in range(len(planes))]
 
 
+INNER_TILES = (NPOP + 1) // 2 - 2
+
+
+def fold(tiles):
+    out = list(tiles[:INNER_TILES])
+    for m in range(6):
+        extra, at = tiles[INNER_TILES + m // 3], 2 * (m % 3)
+        out[m] = pick(((0,), roll_rows(extra, -1 - at)), ((7,), roll_rows(extra, 5 - at)), (out[m],))
+    return out
+
+
+def unfold(tile, j):
+    if j < INNER_TILES:
+        return tile(j)
+    rows = []
+    for m in range(3):
+        v = tile(3 * (j - INNER_TILES) + m)
+        rows += [((1 + 2 * m,), roll_rows(v, 1 + 2 * m)), ((2 + 2 * m,), roll_rows(v, 2 * m - 5))]
+    return pick(*rows, (rows[-1][1],))
+
+
 def lower():
     return lane_ids() % BX < 8
 
@@ -214,8 +235,7 @@
 MOVING = len(FORWARD)
 
 PAIRS = (len(LEVEL) + 1) // 2
-FIRST_RIM = MOVING + PAIRS
-WORDS = FIRST_RIM + (MOVING + 1 + 3) // 4
+WORDS = MOVING + PAIRS
 
 
 def pick(*choices):
@@ -232,52 +252,45 @@
 def pack_message(message, first, second, rim, up):
     for k, i in enumerate(FORWARD if up else BACKWARD):
         f, s = [first(i, h) for h in range(2)], [second(i, h) for h in range(2)]
+        s = [v + roll_rows(v, -1) for v in s]
         if up:
             message[k] = pick(
                 ((7, 0), roll_rows(f[0], 1)),
                 ((1, 2), roll_rows(f[1], 3)),
-                ((3, 4), roll_rows(s[0], -2)),
-                (s[1],),
+                ((3,), roll_rows(s[0], -2)),
+                ((5,), s[1]),
+                ((4,), rim[k]),
+                (roll_rows(rim[k], -2),),
             )
         else:
             message[k] = pick(
                 ((3, 4), roll_rows(f[0], 3)),
                 ((5, 6), roll_rows(f[1], 5)),
-                ((7, 0), roll_rows(s[0], -2)),
-                (s[1],),
+                ((7,), roll_rows(s[0], -2)),
+                ((1,), s[1]),
+                ((0,), roll_rows(rim[k], -3)),
+                (roll_rows(rim[k], 3),),
             )
     for k in range(PAIRS):
         shared = []
         for i in (LEVEL + [NPOP])[2 * k : 2 * k + 2]:
             f = [first(i, h) for h in range(2)]
-            s = [second(i, h) for h in range(2)] if i < NPOP else f
             if up:
+                if i < NPOP:
+                    s = [roll_rows(second(i, 0), -3), roll_rows(second(i, 1), -1)]
+                else:
+                    s = [roll_rows(rim[MOVING], -1), roll_rows(rim[MOVING], 5)]
+                shared.append(pick(((7,), f[0]), ((1,), roll_rows(f[1], 2)), ((3,), s[0]), (s[1],)))
+            else:
+                if i < NPOP:
+                    s = [roll_rows(second(i, 0), -1), roll_rows(second(i, 1), 1)]
+                else:
+                    s = [roll_rows(rim[MOVING], -3), roll_rows(rim[MOVING], 3)]
                 shared.append(
-                    pick(
-                        ((7,), f[0]),
-                        ((1,), roll_rows(f[1], 2)),
-                        ((3,), roll_rows(s[0], -3)),
-                        (roll_rows(s[1], -1),),
-                    )
-                )
-            else:
-                shared.append(
-                    pick(
-                        ((4,), roll_rows(f[0], 4)),
-                        ((6,), roll_rows(f[1], -2)),
-                        ((0,), roll_rows(s[0], -1)),
-                        (roll_rows(s[1], 1),),
-                    )
+                    pick(((4,), roll_rows(f[0], 4)), ((6,), roll_rows(f[1], -2)), ((0,), s[0]), (s[1],))
                 )
         own_rows = (1, 3, 5, 7) if up else (0, 2, 4, 6)
         message[MOVING + k] = pick((own_rows, shared[0]), (roll_rows(shared[1], 1),))
-    for j in range(WORDS - FIRST_RIM):
-        tile = None
-        for k, v in enumerate(rim[4 * j : 4 * j + 4]):
-            v = roll_rows(v, k if up else -k)
-            at = k if up else 3 - k
-            tile = v if tile is None else jnp.where(row_ids() % 4 == at, v, tile)
-        message[FIRST_RIM + j] = tile
 
 
 def shared_tile(message, i):
@@ -286,8 +299,9 @@
 
 
 def rim_row(message, k, h, up):
-    row = 4 * (1 - h) + k % 4 if up else 4 * h + 3 - k % 4
-    return jnp.broadcast_to(message[FIRST_RIM + k // 4, pl.ds(row, 1), :], TILE)
+    index, row = (k, 0) if k < MOVING else (WORDS - 1, 1)
+    row = 4 + 2 * h if up else row + 2 * h
+    return jnp.broadcast_to(message[index, pl.ds(row, 1), :], TILE)
 
 
 def pack_kernel(fine, solid, coarse, coarse_solid, slot, moved, second, high, low, slot_out, strip, rim, sem):
@@ -377,8 +391,9 @@
         for i in range(NPOP)
     ]
     out = restrict(squeeze(sums, means())) + [None]
-    for j in range((NPOP + 1) // 2):
-        packed[j] = pair_up(out[2 * j], out[2 * j + 1])
+    pairs = [pair_up(out[2 * j], out[2 * j + 1]) for j in range((NPOP + 1) // 2)]
+    for j, tile in enumerate(fold(pairs)):
+        packed[j] = tile
 
 
 def starts_early():
@@ -445,6 +460,7 @@
         )
 
     twice = collide([middle(i) for i in range(NPOP)], middle(NPOP), TAU_FINE)
+    nothing = jnp.zeros(TILE, jnp.float32)
     both = [[], []]
     for h in range(2):
         for i in range(NPOP):
@@ -454,12 +470,14 @@
                 v = pick(
                     ((0, 1, 4, 5), v),
                     ((2, 3), roll_rows(mine, -3)),
+                    ((7,), nothing),
                     (roll_rows(below[FORWARD.index(i)], 3 - 2 * h),),
                 )
             elif cx < 0:
                 v = pick(
                     ((2, 3, 6, 7), v),
                     ((0, 1), roll_rows(mine, -1)),
+                    ((5,), nothing),
                     (roll_rows(above[BACKWARD.index(i)], -3 - 2 * h),),
                 )
             else:
@@ -488,7 +506,6 @@
     ]
     for j in range(len(pairs) // 2):
         packed[j] = pair_up(pairs[2 * j], pairs[2 * j + 1])
-    packed[len(pairs) // 2] = jnp.zeros(TILE, jnp.float32)
     for i in range(NPOP):
         for h in range(2):
             edges[i, h] = both[h][i]
@@ -532,7 +549,7 @@
         out[i, h] = tile
 
     paste_inner(
-        chosen, sources, lambda s, j: parts[s][j], lambda i, h: coarse[0, i, :, half_lanes(h)], write
+        chosen, sources, lambda s, j: unfold(lambda k: parts[s][k], j), lambda i, h: coarse[0, i, :, half_lanes(h)], write
     )
     for i in range(NPOP + 1):
         v = [coarse[0, i, :, half_lanes(h)] if i < NPOP else solid[0, :, half_lanes(h)] for h in range(2)]
@@ -556,9 +573,10 @@
     def write(i, h, tile):
         f[h][i] = tile
 
+    half = relayed[0].shape[0]
+
     def tile(s, j):
-        half, at = divmod(j, relayed[0].shape[0])
-        return relayed[s - 3 + half][at]
+        return unfold(lambda k: relayed[s - 3 + k // half][k % half], j)
 
     paste_inner(chosen, sources, tile, lambda i, h: base[i, h], write)
     f = move_in_planes([collide(f[h], solid[0, :, half_lanes(h)], TAU_COARSE) for h in range(2)])
@@ -686,7 +704,7 @@
     )
     fine_v, solid_v = held(fine_pops), held(fine_solid)
     coarse_v, coarse_solid_v = held(coarse_pops), held(coarse_solid)
-    inner_shapes = [in_vmem(NPOP, 2, 2 * ROWS, LANES), in_vmem((NPOP + 1) // 2, *TILE)]
+    inner_shapes = [in_vmem(NPOP, 2, 2 * ROWS, LANES), in_vmem(INNER_TILES, *TILE)]
     early_inner, early_packed, low = call(
         early_kernel,
         (fine_v, solid_v, held(moved), held(low)),
@@ -703,7 +721,7 @@
         inner_kernel,
         (fine_v, solid_v, held(moved), held(early_inner), held(early_packed), held(slot)),
         [VMEM] * 6,
-        [*inner_shapes, in_vmem((NPOP + 1) // 2 + 1, *TILE), in_vmem(4, groups, *TILE), VMEM((2 * LANES, LANES), jnp.bfloat16)],
+        [*inner_shapes, in_vmem(INNER_TILES + 1, *TILE), in_vmem(4, groups, *TILE), VMEM((2 * LANES, LANES), jnp.bfloat16)],
         inner_shapes[:1],
         name="inner",
     )
@@ -714,7 +732,7 @@
         edge_kernel,
         (held(moved), held(second), held(below), held(above), held(matrix), coarse_v, coarse_solid_v),
         [VMEM] * 7,
-        [in_vmem(NPOP, 2, *TILE), in_vmem((NPOP + 1) // 4 + 1, *TILE)],
+        [in_vmem(NPOP, 2, *TILE), in_vmem((NPOP + 1) // 4, *TILE)],
         name="edge",
     )
     edge_parts = [packed_edges] + [exchange(packed_edges, s) for s in others(groups)]

time: 15.6 us -> 15.4 us (0.987)
  waiting for transfers between devices: 0.63 us -> 0.38 us
    ppermute x1, waiting for transfers between devices: 0.3 us -> 0.1 us  [per_device(): above = lax.ppermute(low, 'blk', backward)]
  transfers between devices with their start and end apart: 9 -> 9, of which waited for: 3 -> 2; matrix products, arithmetic and copies ran while one was open for 0% -> 0% of each run, Pallas kernels for 15% -> 15%
where the time goes in v6:
time: 15.4 us; the launch traced here: 15.2 us
  starting transfers between devices  9.78 us (64%)
  Pallas kernels  4.31 us (28%)
  between operations  0.73 us (5%)
  waiting for transfers between devices  0.38 us (2%)
    pallas_call x9, Pallas kernels, call(): pl.pallas_call(kernel, in_specs=[pl.BlockSpec(memory_space=s) for s in sp...  4.31 us
    ppermute x7, starting transfers between devices, exchange(): lax.ppermute(array, 'grp', [(i, i ^ distance) for i in range(groups)])  4.27 us
    ppermute x1, starting transfers between devices, per_device(): below = lax.ppermute(high, 'blk', forward)  3.02 us
    ppermute x1, starting transfers between devices, per_device(): above = lax.ppermute(low, 'blk', backward)  2.49 us
  transfers between devices with their start and end apart: 9, of which 2 were waited for; matrix products, arithmetic and copies ran while one was open for 0% of the time, Pallas kernels for 15%

profile of v6, /device:TPU:0, one launch (start us, length us, event | category | flops | bytes accessed | tf_op | source)
XLA Modules:
  0.0 15.2 jit_solution(6584420809089542310)
XLA Ops:
  0.6 0.0 copy-start
  0.6 0.0 copy-start.2
  0.6 1.2 %pack.1 = (f32[20,2,8,128]{3,2,1,0:T(8,128)S(1)}, f32[19,2,8,128]{3,2,1,0:T(8,128)S(1)}, f32[11,8,128]{2,1,0:T(8,128)S(1)}, f32[10,8,128]{2,1,0:T(8,128)S(1)}, s32[4]{0:T(128)S(1)}) custom-call(f32[1,19,16,256]{3,2,1,0:T(8,128)} %fine.5, f32[1,16,256]{2,1,0:T(8,128)} %solid.7, f32[1,19,8,256]{3,2,1,0:T(8,128)} %coarse.6, f32[1,8,256]{2,1,0:T(8,128)} %solid.9, ...), custom_call_target="tpu_custom_call" | custom-call | bytes 1 | tf_op jit(solution)/shard_map/pack/pallas_call | solution.py:671
  1.8 3.0 %collective-permute-start = (f32[11,8,128]{2,1,0:T(8,128)S(1)}, f32[11,8,128]{2,1,0:T(8,128)S(1)}, u32[]{:S(2)}, u32[]{:S(2)}) collective-permute-start(f32[11,8,128]{2,1,0:T(8,128)S(1)} %get-tuple-element.28), channel_id=1, source_target_pairs={{0,1},{1,2},{2,3},{3,4},{4,5},{5,6},{6,7},{7,0},{8,9},{9,10},{10,1... | collective-permute-start | bytes 135176 | tf_op jit(solution)/shard_map/ppermute | solution.py:718
  4.9 0.0 copy-done
  4.9 0.0 copy-done.2
  4.9 0.6 %early.1 = (f32[19,2,16,128]{3,2,1,0:T(8,128)S(1)}, f32[8,8,128]{2,1,0:T(8,128)S(1)}, f32[10,8,128]{2,1,0:T(8,128)S(1)}) custom-call(f32[1,19,16,256]{3,2,1,0:T(8,128)S(1)} %copy-done, f32[1,16,256]{2,1,0:T(8,128)S(1)} %copy-done.2, f32[20,2,8,128]{3,2,1,0:T(8,128)S(1)} %get-tuple-element.21.moved, f32[10,8,128]{2,1,0:T(8,128)S(1)} %get-tuple-element.22.low), custom_call_target="tpu_custom_call" | custom-call | bytes 1 | tf_op jit(solution)/shard_map/early/pallas_call | solution.py:671
  5.5 2.5 %collective-permute-start.1 = (f32[10,8,128]{2,1,0:T(8,128)S(1)}, f32[10,8,128]{2,1,0:T(8,128)S(1)}, u32[]{:S(2)}, u32[]{:S(2)}) collective-permute-start(f32[10,8,128]{2,1,0:T(8,128)S(1)} %get-tuple-element.29), channel_id=1, source_target_pairs={{0,7},{1,0},{2,1},{3,2},{4,3},{5,4},{6,5},{7,6},{8,15},{9,8},{10,9... | collective-permute-start | bytes 122888 | tf_op jit(solution)/shard_map/ppermute | solution.py:719
  8.0 0.2 %inner.1 = (f32[19,2,16,128]{3,2,1,0:T(8,128)S(1)}, f32[8,8,128]{2,1,0:T(8,128)S(1)}, f32[9,8,128]{2,1,0:T(8,128)S(1)}, f32[4,4,8,128]{3,2,1,0:T(8,128)S(1)}, bf16[256,128]{1,0:T(8,128)(2,1)S(1)}) custom-call(f32[1,19,16,256]{3,2,1,0:T(8,128)S(1)} %copy-done, f32[1,16,256]{2,1,0:T(8,128)S(1)} %copy-done.2, f32[20,2,8,128]{3,2,1,0:T(8,128)S(1)} %get-tuple-element.21.moved, ...), custom_call_target="tpu_custom_call" | custom-call | bytes 1 | tf_op jit(solution)/shard_map/inner/pallas_call | solution.py:671
  8.2 0.1 collective-permute-start.2
  8.3 1.7 %collective-permute-start.3 = (f32[8,8,128]{2,1,0:T(8,128)S(1)}, f32[8,8,128]{2,1,0:T(8,128)S(1)}, u32[]{:S(2)}, u32[]{:S(2)}) collective-permute-start(f32[8,8,128]{2,1,0:T(8,128)S(1)} %get-tuple-element.34.refs_1_), channel_id=1, source_target_pairs={{0,16},{8,24},{16,0},{24,8},{1,17},{9,25},{17,1},{25,9},{2,18},{10... | collective-permute-start | bytes 98312 | tf_op jit(solution)/shard_map/ppermute | solution.py:653
  10.0 0.1 collective-permute-done.1.above
  10.1 0.0 collective-permute-done.below
  10.1 0.0 copy-done.1
  10.1 0.0 copy-done.3
  10.1 0.3 %edge.1 = (f32[19,2,8,128]{3,2,1,0:T(8,128)S(1)}, f32[5,8,128]{2,1,0:T(8,128)S(1)}) custom-call(f32[20,2,8,128]{3,2,1,0:T(8,128)S(1)} %get-tuple-element.21.moved, f32[19,2,8,128]{3,2,1,0:T(8,128)S(1)} %get-tuple-element.27.second, f32[11,8,128]{2,1,0:T(8,128)S(1)} %collective-permute-done.below, f32[10,8,128]{2,1,0:T(8,128)S(1)} %collective-permute-done.1.above, ...), custom_call_target="tpu_custom_call" | custom-call | bytes 1 | tf_op jit(solution)/shard_map/edge/pallas_call | solution.py:671
  10.4 0.2 collective-permute-start.8
  10.6 1.6 %collective-permute-start.7 = (f32[5,8,128]{2,1,0:T(8,128)S(1)}, f32[5,8,128]{2,1,0:T(8,128)S(1)}, u32[]{:S(2)}, u32[]{:S(2)}) collective-permute-start(f32[5,8,128]{2,1,0:T(8,128)S(1)} %get-tuple-element.39.refs_0_), channel_id=1, source_target_pairs={{0,16},{8,24},{16,0},{24,8},{1,17},{9,25},{17,1},{25,9},{2,18},{10... | collective-permute-start | bytes 61448 | tf_op jit(solution)/shard_map/ppermute | solution.py:653
  12.2 0.2 %collective-permute-start.6 = (f32[5,8,128]{2,1,0:T(8,128)S(1)}, f32[5,8,128]{2,1,0:T(8,128)S(1)}, u32[]{:S(2)}, u32[]{:S(2)}) collective-permute-start(f32[5,8,128]{2,1,0:T(8,128)S(1)} %get-tuple-element.39.refs_0_), channel_id=1, source_target_pairs={{0,8},{8,0},{16,24},{24,16},{1,9},{9,1},{17,25},{25,17},{2,10},{10... | collective-permute-start | bytes 61448 | tf_op jit(solution)/shard_map/ppermute | solution.py:653
  12.4 0.0 collective-permute-done.3.refs_2_.tiles
  12.4 0.0 collective-permute-done.2.refs_0_
  12.4 0.1 paste.1
  12.5 0.4 %collective-permute-start.4 = (f32[4,8,128]{2,1,0:T(8,128)S(1)}, f32[4,8,128]{2,1,0:T(8,128)S(1)}, u32[]{:S(2)}, u32[]{:S(2)}) collective-permute-start(f32[4,8,128]{2,1,0:T(8,128)S(1)} %get-tuple-element.37), channel_id=1, source_target_pairs={{0,8},{8,0},{16,24},{24,16},{1,9},{9,1},{17,25},{25,17},{2,10},{10... | collective-permute-start | bytes 49160 | tf_op jit(solution)/shard_map/ppermute | solution.py:653
  12.9 0.2 %collective-permute-start.5 = (f32[4,8,128]{2,1,0:T(8,128)S(1)}, f32[4,8,128]{2,1,0:T(8,128)S(1)}, u32[]{:S(2)}, u32[]{:S(2)}) collective-permute-start(f32[4,8,128]{2,1,0:T(8,128)S(1)} %get-tuple-element.38), channel_id=1, source_target_pairs={{0,8},{8,0},{16,24},{24,16},{1,9},{9,1},{17,25},{25,17},{2,10},{10... | collective-permute-start | bytes 49160 | tf_op jit(solution)/shard_map/ppermute | solution.py:653
  13.1 0.8 %write.1.after = f32[1,19,16,256]{3,2,1,0:T(8,128)} custom-call(f32[19,2,16,128]{3,2,1,0:T(8,128)S(1)} %get-tuple-element.26.inner, f32[19,2,8,128]{3,2,1,0:T(8,128)S(1)} %get-tuple-element.31.edges.after), custom_call_target="tpu_custom_call" | custom-call | bytes 1 | tf_op jit(solution)/shard_map/write/pallas_call | solution.py:671
  13.8 0.0 collective-permute-done.4.refs_0_
  13.8 0.3 %collective-permute-done.5.refs_1_ = f32[4,8,128]{2,1,0:T(8,128)S(1)} collective-permute-done((f32[4,8,128]{2,1,0:T(8,128)S(1)}, f32[4,8,128]{2,1,0:T(8,128)S(1)}, u32[]{:S(2)}, u32[]{:S(2)}) %collective-permute-start.5) | collective-permute-done | bytes 16416 | tf_op jit(solution)/shard_map/ppermute | solution.py:653
  14.1 0.2 %coarse.7.middle = f32[19,2,8,128]{3,2,1,0:T(8,128)S(1)} custom-call(f32[1,19,16,256]{3,2,1,0:T(8,128)} %write.1.after, f32[19,2,8,128]{3,2,1,0:T(8,128)S(1)} %get-tuple-element.36.after.base, f32[1,8,256]{2,1,0:T(8,128)S(1)} %copy-done.3, f32[4,4,8,128]{3,2,1,0:T(8,128)S(1)} %get-tuple-element.32.chosen, f32[4,8,128]{2,1,0:T(8,128)S(1)} %collective-permute-done.4.refs_0_, ...), custom_call_target="tpu_custom_call" | custom-call | bytes 1 | tf_op jit(solution)/shard_map/coarse/pallas_call | solution.py:671
  14.3 0.0 collective-permute-done.8.refs_3_
  14.4 0.0 collective-permute-done.7.refs_2_
  14.4 0.0 collective-permute-done.6.refs_1_
  14.4 0.8 %last.1 = f32[1,19,8,256]{3,2,1,0:T(8,128)} custom-call(f32[4,4,8,128]{3,2,1,0:T(8,128)S(1)} %get-tuple-element.32.chosen, f32[11,8,128]{2,1,0:T(8,128)S(1)} %collective-permute-done.below, f32[10,8,128]{2,1,0:T(8,128)S(1)} %collective-permute-done.1.above, f32[20,8,128]{2,1,0:T(8,128)S(1)} %get-tuple-element.35.base, f32[19,2,8,128]{3,2,1,0:T(8,128)S(1)} %coarse.7.middle, ...), custom_call_target="tpu_custom_call" | custom-call | bytes 1 | tf_op jit(solution)/shard_map/last/pallas_call | solution.py:671
  (3 shorter events, 0.0 us)
Async XLA Ops:
  0.6 4.2 %copy-start = (f32[1,19,16,256]{3,2,1,0:T(8,128)S(1)}, f32[1,19,16,256]{3,2,1,0:T(8,128)}, u32[]{:S(2)}) copy-start(f32[1,19,16,256]{3,2,1,0:T(8,128)} %fine.5) | copy-start | bytes 933892
  0.6 4.2 %copy-start.2 = (f32[1,16,256]{2,1,0:T(8,128)S(1)}, f32[1,16,256]{2,1,0:T(8,128)}, u32[]{:S(2)}) copy-start(f32[1,16,256]{2,1,0:T(8,128)} %solid.7) | copy-start | bytes 49156
  1.8 8.2 %collective-permute-start = (f32[11,8,128]{2,1,0:T(8,128)S(1)}, f32[11,8,128]{2,1,0:T(8,128)S(1)}, u32[]{:S(2)}, u32[]{:S(2)}) collective-permute-start(f32[11,8,128]{2,1,0:T(8,128)S(1)} %get-tuple-element.28), channel_id=1, source_target_pairs={{0,1},{1,2},{2,3},{3,4},{4,5},{5,6},{6,7},{7,0},{8,9},{9,10},{10,1... | collective-permute-start | bytes 135176 | tf_op jit(solution)/shard_map/ppermute | solution.py:718
  5.5 4.5 %collective-permute-start.1 = (f32[10,8,128]{2,1,0:T(8,128)S(1)}, f32[10,8,128]{2,1,0:T(8,128)S(1)}, u32[]{:S(2)}, u32[]{:S(2)}) collective-permute-start(f32[10,8,128]{2,1,0:T(8,128)S(1)} %get-tuple-element.29), channel_id=1, source_target_pairs={{0,7},{1,0},{2,1},{3,2},{4,3},{5,4},{6,5},{7,6},{8,15},{9,8},{10,9... | collective-permute-start | bytes 122888 | tf_op jit(solution)/shard_map/ppermute | solution.py:719
  8.0 2.1 %copy-start.1 = (f32[1,19,8,256]{3,2,1,0:T(8,128)S(1)}, f32[1,19,8,256]{3,2,1,0:T(8,128)}, u32[]{:S(2)}) copy-start(f32[1,19,8,256]{3,2,1,0:T(8,128)} %coarse.6) | copy-start | bytes 466948
  8.0 2.1 %copy-start.3 = (f32[1,8,256]{2,1,0:T(8,128)S(1)}, f32[1,8,256]{2,1,0:T(8,128)}, u32[]{:S(2)}) copy-start(f32[1,8,256]{2,1,0:T(8,128)} %solid.9) | copy-start | bytes 24580
  8.2 4.2 %collective-permute-start.2 = (f32[9,8,128]{2,1,0:T(8,128)S(1)}, f32[9,8,128]{2,1,0:T(8,128)S(1)}, u32[]{:S(2)}, u32[]{:S(2)}) collective-permute-start(f32[9,8,128]{2,1,0:T(8,128)S(1)} %get-tuple-element.33), channel_id=1, source_target_pairs={{0,8},{8,0},{16,24},{24,16},{1,9},{9,1},{17,25},{25,17},{2,10},{10... | collective-permute-start | bytes 110600 | tf_op jit(solution)/shard_map/ppermute | solution.py:653
  8.3 4.1 %collective-permute-start.3 = (f32[8,8,128]{2,1,0:T(8,128)S(1)}, f32[8,8,128]{2,1,0:T(8,128)S(1)}, u32[]{:S(2)}, u32[]{:S(2)}) collective-permute-start(f32[8,8,128]{2,1,0:T(8,128)S(1)} %get-tuple-element.34.refs_1_), channel_id=1, source_target_pairs={{0,16},{8,24},{16,0},{24,8},{1,17},{9,25},{17,1},{25,9},{2,18},{10... | collective-permute-start | bytes 98312 | tf_op jit(solution)/shard_map/ppermute | solution.py:653
  10.4 3.9 %collective-permute-start.8 = (f32[5,8,128]{2,1,0:T(8,128)S(1)}, f32[5,8,128]{2,1,0:T(8,128)S(1)}, u32[]{:S(2)}, u32[]{:S(2)}) collective-permute-start(f32[5,8,128]{2,1,0:T(8,128)S(1)} %get-tuple-element.39.refs_0_), channel_id=1, source_target_pairs={{0,24},{8,16},{16,8},{24,0},{1,25},{9,17},{17,9},{25,1},{2,26},{10... | collective-permute-start | bytes 61448 | tf_op jit(solution)/shard_map/ppermute | solution.py:653
  10.6 3.8 %collective-permute-start.7 = (f32[5,8,128]{2,1,0:T(8,128)S(1)}, f32[5,8,128]{2,1,0:T(8,128)S(1)}, u32[]{:S(2)}, u32[]{:S(2)}) collective-permute-start(f32[5,8,128]{2,1,0:T(8,128)S(1)} %get-tuple-element.39.refs_0_), channel_id=1, source_target_pairs={{0,16},{8,24},{16,0},{24,8},{1,17},{9,25},{17,1},{25,9},{2,18},{10... | collective-permute-start | bytes 61448 | tf_op jit(solution)/shard_map/ppermute | solution.py:653
  12.2 2.2 %collective-permute-start.6 = (f32[5,8,128]{2,1,0:T(8,128)S(1)}, f32[5,8,128]{2,1,0:T(8,128)S(1)}, u32[]{:S(2)}, u32[]{:S(2)}) collective-permute-start(f32[5,8,128]{2,1,0:T(8,128)S(1)} %get-tuple-element.39.refs_0_), channel_id=1, source_target_pairs={{0,8},{8,0},{16,24},{24,16},{1,9},{9,1},{17,25},{25,17},{2,10},{10... | collective-permute-start | bytes 61448 | tf_op jit(solution)/shard_map/ppermute | solution.py:653
  12.5 1.3 %collective-permute-start.4 = (f32[4,8,128]{2,1,0:T(8,128)S(1)}, f32[4,8,128]{2,1,0:T(8,128)S(1)}, u32[]{:S(2)}, u32[]{:S(2)}) collective-permute-start(f32[4,8,128]{2,1,0:T(8,128)S(1)} %get-tuple-element.37), channel_id=1, source_target_pairs={{0,8},{8,0},{16,24},{24,16},{1,9},{9,1},{17,25},{25,17},{2,10},{10... | collective-permute-start | bytes 49160 | tf_op jit(solution)/shard_map/ppermute | solution.py:653
  12.9 1.2 %collective-permute-start.5 = (f32[4,8,128]{2,1,0:T(8,128)S(1)}, f32[4,8,128]{2,1,0:T(8,128)S(1)}, u32[]{:S(2)}, u32[]{:S(2)}) collective-permute-start(f32[4,8,128]{2,1,0:T(8,128)S(1)} %get-tuple-element.38), channel_id=1, source_target_pairs={{0,8},{8,0},{16,24},{24,16},{1,9},{9,1},{17,25},{25,17},{2,10},{10... | collective-permute-start | bytes 49160 | tf_op jit(solution)/shard_map/ppermute | solution.py:653

commit v7 on v6

--- a/solution.py
+++ b/solution.py
@@ -304,7 +304,7 @@
     return jnp.broadcast_to(message[index, pl.ds(row, 1), :], TILE)
 
 
-def pack_kernel(fine, solid, coarse, coarse_solid, slot, moved, second, high, low, slot_out, strip, rim, sem):
+def pack_kernel(fine, solid, coarse, coarse_solid, slot, moved, second, high, low, slot_out, strip, shade, rim, sem):
     planes = fine.shape[2]
     last = coarse.shape[2] - 1
 
@@ -315,17 +315,20 @@
         pltpu.make_async_copy(target, target, sem.at[which]).wait()
 
     ends = ((0, 0), (planes - 4, 4))
-    for half in (pl.ds(0, 10), pl.ds(10, 9)):
+    for half in (pl.ds(0, 7), pl.ds(7, 6), pl.ds(13, 6)):
         for first, row in ends:
             bring(fine.at[0, half, pl.ds(first, 4), :], strip.at[half, pl.ds(row, 4), :], 0)
-    for first, row in ends:
-        bring(solid.at[0, pl.ds(first, 4), :], strip.at[NPOP, pl.ds(row, 4), :], 0)
+    bring(solid.at[0], shade, 0)
     for plane, row in ((last, 0), (0, 3)):
         bring(coarse.at[0, :, pl.ds(plane, 1), :], rim.at[pl.ds(0, NPOP), pl.ds(row, 1), :], 1)
         bring(coarse_solid.at[0, pl.ds(plane, 1), :], rim.at[NPOP, pl.ds(row, 1), :], 1)
     bring(slot, slot_out, 2)
     arrive(strip, 0)
-    solids = [strip[NPOP, :, half_lanes(h)] for h in range(2)]
+    upper = row_ids() < 4
+    solids = [
+        jnp.where(upper, shade[pl.ds(0, ROWS), half_lanes(h)], shade[pl.ds(planes - ROWS, ROWS), half_lanes(h)])
+        for h in range(2)
+    ]
     once = move_in_planes(
         [collide([strip[i, :, half_lanes(h)] for i in range(NPOP)], solids[h], TAU_FINE) for h in range(2)]
     )
@@ -400,15 +403,7 @@
     return lax.axis_index("blk") == 0
 
 
-def early_kernel(fine, solid, moved, low, inner, packed, low_out, work):
-    low_out[...] = low[...]
-
-    @pl.when(starts_early())
-    def _():
-        inner_steps(fine, solid, moved, inner, packed, work)
-
-
-def inner_kernel(fine, solid, moved, early_inner, early_packed, slot, inner, packed, padded, chosen, matrix, work):
+def prepare(slot, chosen, matrix):
     groups = chosen.shape[1]
     matrix[...] = means()
     me = lax.axis_index("grp")
@@ -419,14 +414,29 @@
         for q in range(4):
             chosen[q, s] = jnp.where(lane_ids() * 0 + (4 * me + q) == code, 1.0, 0.0)
 
+
+def early_kernel(fine, solid, moved, slot, low, inner, packed, chosen, matrix, low_out, work):
+    low_out[...] = low[...]
+
     @pl.when(starts_early())
     def _():
-        inner[...] = early_inner[...]
-        packed[...] = early_packed[...]
+        inner_steps(fine, solid, moved, inner, packed, work)
+        prepare(slot, chosen, matrix)
+
+
+def inner_kernel(fine, solid, moved, slot, *refs):
+    *refs, padded, work = refs
+    done, (inner, packed, chosen, matrix) = refs[:4], refs[4:]
+
+    @pl.when(starts_early())
+    def _():
+        for source, target in zip(done, (inner, packed, chosen, matrix)):
+            target[...] = source[...]
 
     @pl.when(jnp.logical_not(starts_early()))
     def _():
         inner_steps(fine, solid, moved, inner, packed, work)
+        prepare(slot, chosen, matrix)
 
     size = packed.shape[0]
     padded[pl.ds(0, size)] = packed[...]
@@ -696,7 +706,8 @@
             VMEM((groups,), jnp.int32),
         ],
         [
-            in_vmem(NPOP + 1, ROWS, 2 * LANES),
+            in_vmem(NPOP + 2, ROWS, 2 * LANES),
+            in_vmem(*fine_solid.shape[1:]),
             in_vmem(NPOP + 1, ROWS, 2 * LANES),
             pltpu.SemaphoreType.DMA((3,)),
         ],
@@ -704,11 +715,17 @@
     )
     fine_v, solid_v = held(fine_pops), held(fine_solid)
     coarse_v, coarse_solid_v = held(coarse_pops), held(coarse_solid)
-    inner_shapes = [in_vmem(NPOP, 2, 2 * ROWS, LANES), in_vmem(INNER_TILES, *TILE)]
-    early_inner, early_packed, low = call(
+    inner_shapes = [
+        in_vmem(NPOP, 2, 2 * ROWS, LANES),
+        in_vmem(INNER_TILES, *TILE),
+        in_vmem(4, groups, *TILE),
+        VMEM((2 * LANES, LANES), jnp.bfloat16),
+    ]
+    inner_args = (fine_v, solid_v, held(moved), held(slot))
+    *done, low = call(
         early_kernel,
-        (fine_v, solid_v, held(moved), held(low)),
-        [VMEM] * 4,
+        (*inner_args, held(low)),
+        [VMEM] * 5,
         [*inner_shapes, in_vmem(WORDS, *TILE)],
         inner_shapes[:1],
         name="early",
@@ -717,11 +734,11 @@
     backward = [(i, (i - 1) % blocks) for i in range(blocks)]
     below = lax.ppermute(high, "blk", forward)
     above = lax.ppermute(low, "blk", backward)
-    inner, packed_inner, padded_inner, chosen, matrix = call(
+    inner, packed_inner, chosen, matrix, padded_inner = call(
         inner_kernel,
-        (fine_v, solid_v, held(moved), held(early_inner), held(early_packed), held(slot)),
-        [VMEM] * 6,
-        [*inner_shapes, in_vmem(INNER_TILES + 1, *TILE), in_vmem(4, groups, *TILE), VMEM((2 * LANES, LANES), jnp.bfloat16)],
+        (*inner_args, *map(held, done)),
+        [VMEM] * 8,
+        [*inner_shapes, in_vmem(INNER_TILES + 1, *TILE)],
         inner_shapes[:1],
         name="inner",
     )

time: 15.4 us -> 15.4 us (level)
  transfers between devices with their start and end apart: 9 -> 9, of which waited for: 2 -> 3; matrix products, arithmetic and copies ran while one was open for 0% -> 0% of each run, Pallas kernels for 15% -> 14%
where the time goes in v7:
time: 15.4 us; the launch traced here: 15.2 us
  starting transfers between devices  9.75 us (63%)
  Pallas kernels  4.18 us (27%)
  between operations  0.73 us (5%)
  waiting for transfers between devices  0.53 us (3%)
    ppermute x7, starting transfers between devices, exchange(): lax.ppermute(array, 'grp', [(i, i ^ distance) for i in range(groups)])  4.25 us
    pallas_call x9, Pallas kernels, call(): pl.pallas_call(kernel, in_specs=[pl.BlockSpec(memory_space=s) for s in sp...  4.18 us
    ppermute x1, starting transfers between devices, per_device(): below = lax.ppermute(high, 'blk', forward)  3.02 us
    ppermute x1, starting transfers between devices, per_device(): above = lax.ppermute(low, 'blk', backward)  2.48 us
  transfers between devices with their start and end apart: 9, of which 3 were waited for; matrix products, arithmetic and copies ran while one was open for 0% of the time, Pallas kernels for 14%

profile of v7, /device:TPU:0, one launch (start us, length us, event | category | flops | bytes accessed | tf_op | source)
XLA Modules:
  0.0 15.2 jit_solution(6707690216302713750)
XLA Ops:
  0.6 0.0 copy-start
  0.6 0.0 copy-start.2
  0.6 1.2 %pack.1 = (f32[20,2,8,128]{3,2,1,0:T(8,128)S(1)}, f32[19,2,8,128]{3,2,1,0:T(8,128)S(1)}, f32[11,8,128]{2,1,0:T(8,128)S(1)}, f32[10,8,128]{2,1,0:T(8,128)S(1)}, s32[4]{0:T(128)S(1)}) custom-call(f32[1,19,16,256]{3,2,1,0:T(8,128)} %fine.5, f32[1,16,256]{2,1,0:T(8,128)} %solid.7, f32[1,19,8,256]{3,2,1,0:T(8,128)} %coarse.6, f32[1,8,256]{2,1,0:T(8,128)} %solid.9, ...), custom_call_target="tpu_custom_call" | custom-call | bytes 1 | tf_op jit(solution)/shard_map/pack/pallas_call | solution.py:681
  1.8 3.0 %collective-permute-start = (f32[11,8,128]{2,1,0:T(8,128)S(1)}, f32[11,8,128]{2,1,0:T(8,128)S(1)}, u32[]{:S(2)}, u32[]{:S(2)}) collective-permute-start(f32[11,8,128]{2,1,0:T(8,128)S(1)} %get-tuple-element.32), channel_id=1, source_target_pairs={{0,1},{1,2},{2,3},{3,4},{4,5},{5,6},{6,7},{7,0},{8,9},{9,10},{10,1... | collective-permute-start | bytes 135176 | tf_op jit(solution)/shard_map/ppermute | solution.py:735
  4.9 0.0 copy-done
  4.9 0.0 copy-done.2
  4.9 0.7 %early.1 = (f32[19,2,16,128]{3,2,1,0:T(8,128)S(1)}, f32[8,8,128]{2,1,0:T(8,128)S(1)}, f32[4,4,8,128]{3,2,1,0:T(8,128)S(1)}, bf16[256,128]{1,0:T(8,128)(2,1)S(1)}, f32[10,8,128]{2,1,0:T(8,128)S(1)}) custom-call(f32[1,19,16,256]{3,2,1,0:T(8,128)S(1)} %copy-done, f32[1,16,256]{2,1,0:T(8,128)S(1)} %copy-done.2, f32[20,2,8,128]{3,2,1,0:T(8,128)S(1)} %get-tuple-element.23.moved, ...), custom_call_target="tpu_custom_call" | custom-call | bytes 1 | tf_op jit(solution)/shard_map/early/pallas_call | solution.py:681
  5.5 2.5 %collective-permute-start.1 = (f32[10,8,128]{2,1,0:T(8,128)S(1)}, f32[10,8,128]{2,1,0:T(8,128)S(1)}, u32[]{:S(2)}, u32[]{:S(2)}) collective-permute-start(f32[10,8,128]{2,1,0:T(8,128)S(1)} %get-tuple-element.33), channel_id=1, source_target_pairs={{0,7},{1,0},{2,1},{3,2},{4,3},{5,4},{6,5},{7,6},{8,15},{9,8},{10,9... | collective-permute-start | bytes 122888 | tf_op jit(solution)/shard_map/ppermute | solution.py:736
  8.0 0.0 copy-start.1
  8.1 0.1 collective-permute-start.2
  8.1 1.7 %collective-permute-start.3 = (f32[8,8,128]{2,1,0:T(8,128)S(1)}, f32[8,8,128]{2,1,0:T(8,128)S(1)}, u32[]{:S(2)}, u32[]{:S(2)}) collective-permute-start(f32[8,8,128]{2,1,0:T(8,128)S(1)} %get-tuple-element.38.refs_1_), channel_id=1, source_target_pairs={{0,16},{8,24},{16,0},{24,8},{1,17},{9,25},{17,1},{25,9},{2,18},{10... | collective-permute-start | bytes 98312 | tf_op jit(solution)/shard_map/ppermute | solution.py:663
  9.8 0.2 %collective-permute-done.1.above = f32[10,8,128]{2,1,0:T(8,128)S(1)} collective-permute-done((f32[10,8,128]{2,1,0:T(8,128)S(1)}, f32[10,8,128]{2,1,0:T(8,128)S(1)}, u32[]{:S(2)}, u32[]{:S(2)}) %collective-permute-start.1) | collective-permute-done | bytes 40992 | tf_op jit(solution)/shard_map/ppermute | solution.py:736
  10.1 0.0 collective-permute-done.below
  10.1 0.0 copy-done.1
  10.1 0.0 copy-done.3
  10.1 0.4 %edge.1 = (f32[19,2,8,128]{3,2,1,0:T(8,128)S(1)}, f32[5,8,128]{2,1,0:T(8,128)S(1)}) custom-call(f32[20,2,8,128]{3,2,1,0:T(8,128)S(1)} %get-tuple-element.23.moved, f32[19,2,8,128]{3,2,1,0:T(8,128)S(1)} %get-tuple-element.31.second, f32[11,8,128]{2,1,0:T(8,128)S(1)} %collective-permute-done.below, f32[10,8,128]{2,1,0:T(8,128)S(1)} %collective-permute-done.1.above, ...), custom_call_target="tpu_custom_call" | custom-call | bytes 1 | tf_op jit(solution)/shard_map/edge/pallas_call | solution.py:681
  10.4 0.1 collective-permute-start.8
  10.5 1.6 %collective-permute-start.7 = (f32[5,8,128]{2,1,0:T(8,128)S(1)}, f32[5,8,128]{2,1,0:T(8,128)S(1)}, u32[]{:S(2)}, u32[]{:S(2)}) collective-permute-start(f32[5,8,128]{2,1,0:T(8,128)S(1)} %get-tuple-element.43.refs_0_), channel_id=1, source_target_pairs={{0,16},{8,24},{16,0},{24,8},{1,17},{9,25},{17,1},{25,9},{2,18},{10... | collective-permute-start | bytes 61448 | tf_op jit(solution)/shard_map/ppermute | solution.py:663
  12.1 0.3 %collective-permute-start.6 = (f32[5,8,128]{2,1,0:T(8,128)S(1)}, f32[5,8,128]{2,1,0:T(8,128)S(1)}, u32[]{:S(2)}, u32[]{:S(2)}) collective-permute-start(f32[5,8,128]{2,1,0:T(8,128)S(1)} %get-tuple-element.43.refs_0_), channel_id=1, source_target_pairs={{0,8},{8,0},{16,24},{24,16},{1,9},{9,1},{17,25},{25,17},{2,10},{10... | collective-permute-start | bytes 61448 | tf_op jit(solution)/shard_map/ppermute | solution.py:663
  12.4 0.0 collective-permute-done.3.refs_2_.tiles
  12.4 0.0 collective-permute-done.2.refs_0_
  12.4 0.1 paste.1
  12.5 0.3 %collective-permute-start.4 = (f32[4,8,128]{2,1,0:T(8,128)S(1)}, f32[4,8,128]{2,1,0:T(8,128)S(1)}, u32[]{:S(2)}, u32[]{:S(2)}) collective-permute-start(f32[4,8,128]{2,1,0:T(8,128)S(1)} %get-tuple-element.41), channel_id=1, source_target_pairs={{0,8},{8,0},{16,24},{24,16},{1,9},{9,1},{17,25},{25,17},{2,10},{10... | collective-permute-start | bytes 49160 | tf_op jit(solution)/shard_map/ppermute | solution.py:663
  12.8 0.3 %collective-permute-start.5 = (f32[4,8,128]{2,1,0:T(8,128)S(1)}, f32[4,8,128]{2,1,0:T(8,128)S(1)}, u32[]{:S(2)}, u32[]{:S(2)}) collective-permute-start(f32[4,8,128]{2,1,0:T(8,128)S(1)} %get-tuple-element.42), channel_id=1, source_target_pairs={{0,8},{8,0},{16,24},{24,16},{1,9},{9,1},{17,25},{25,17},{2,10},{10... | collective-permute-start | bytes 49160 | tf_op jit(solution)/shard_map/ppermute | solution.py:663
  13.1 0.8 %write.1.after = f32[1,19,16,256]{3,2,1,0:T(8,128)} custom-call(f32[19,2,16,128]{3,2,1,0:T(8,128)S(1)} %get-tuple-element.30.inner, f32[19,2,8,128]{3,2,1,0:T(8,128)S(1)} %get-tuple-element.35.edges.after), custom_call_target="tpu_custom_call" | custom-call | bytes 1 | tf_op jit(solution)/shard_map/write/pallas_call | solution.py:681
  13.8 0.0 collective-permute-done.4.refs_0_
  13.8 0.1 collective-permute-done.5.refs_1_
  14.0 0.2 %coarse.7.middle = f32[19,2,8,128]{3,2,1,0:T(8,128)S(1)} custom-call(f32[1,19,16,256]{3,2,1,0:T(8,128)} %write.1.after, f32[19,2,8,128]{3,2,1,0:T(8,128)S(1)} %get-tuple-element.40.after.base, f32[1,8,256]{2,1,0:T(8,128)S(1)} %copy-done.3, f32[4,4,8,128]{3,2,1,0:T(8,128)S(1)} %get-tuple-element.36.chosen, f32[4,8,128]{2,1,0:T(8,128)S(1)} %collective-permute-done.4.refs_0_, ...), custom_call_target="tpu_custom_call" | custom-call | bytes 1 | tf_op jit(solution)/shard_map/coarse/pallas_call | solution.py:681
  14.2 0.0 collective-permute-done.8.refs_3_
  14.2 0.1 collective-permute-done.7.refs_2_
  14.4 0.0 collective-permute-done.6.refs_1_
  14.4 0.8 %last.1 = f32[1,19,8,256]{3,2,1,0:T(8,128)} custom-call(f32[4,4,8,128]{3,2,1,0:T(8,128)S(1)} %get-tuple-element.36.chosen, f32[11,8,128]{2,1,0:T(8,128)S(1)} %collective-permute-done.below, f32[10,8,128]{2,1,0:T(8,128)S(1)} %collective-permute-done.1.above, f32[20,8,128]{2,1,0:T(8,128)S(1)} %get-tuple-element.39.base, f32[19,2,8,128]{3,2,1,0:T(8,128)S(1)} %coarse.7.middle, ...), custom_call_target="tpu_custom_call" | custom-call | bytes 1 | tf_op jit(solution)/shard_map/last/pallas_call | solution.py:681
  (3 shorter events, 0.0 us)
Async XLA Ops:
  0.6 4.2 %copy-start = (f32[1,19,16,256]{3,2,1,0:T(8,128)S(1)}, f32[1,19,16,256]{3,2,1,0:T(8,128)}, u32[]{:S(2)}) copy-start(f32[1,19,16,256]{3,2,1,0:T(8,128)} %fine.5) | copy-start | bytes 933892
  0.6 4.2 %copy-start.2 = (f32[1,16,256]{2,1,0:T(8,128)S(1)}, f32[1,16,256]{2,1,0:T(8,128)}, u32[]{:S(2)}) copy-start(f32[1,16,256]{2,1,0:T(8,128)} %solid.7) | copy-start | bytes 49156
  1.8 8.2 %collective-permute-start = (f32[11,8,128]{2,1,0:T(8,128)S(1)}, f32[11,8,128]{2,1,0:T(8,128)S(1)}, u32[]{:S(2)}, u32[]{:S(2)}) collective-permute-start(f32[11,8,128]{2,1,0:T(8,128)S(1)} %get-tuple-element.32), channel_id=1, source_target_pairs={{0,1},{1,2},{2,3},{3,4},{4,5},{5,6},{6,7},{7,0},{8,9},{9,10},{10,1... | collective-permute-start | bytes 135176 | tf_op jit(solution)/shard_map/ppermute | solution.py:735
  5.5 4.5 %collective-permute-start.1 = (f32[10,8,128]{2,1,0:T(8,128)S(1)}, f32[10,8,128]{2,1,0:T(8,128)S(1)}, u32[]{:S(2)}, u32[]{:S(2)}) collective-permute-start(f32[10,8,128]{2,1,0:T(8,128)S(1)} %get-tuple-element.33), channel_id=1, source_target_pairs={{0,7},{1,0},{2,1},{3,2},{4,3},{5,4},{6,5},{7,6},{8,15},{9,8},{10,9... | collective-permute-start | bytes 122888 | tf_op jit(solution)/shard_map/ppermute | solution.py:736
  8.0 2.1 %copy-start.1 = (f32[1,19,8,256]{3,2,1,0:T(8,128)S(1)}, f32[1,19,8,256]{3,2,1,0:T(8,128)}, u32[]{:S(2)}) copy-start(f32[1,19,8,256]{3,2,1,0:T(8,128)} %coarse.6) | copy-start | bytes 466948
  8.0 2.1 %copy-start.3 = (f32[1,8,256]{2,1,0:T(8,128)S(1)}, f32[1,8,256]{2,1,0:T(8,128)}, u32[]{:S(2)}) copy-start(f32[1,8,256]{2,1,0:T(8,128)} %solid.9) | copy-start | bytes 24580
  8.1 4.3 %collective-permute-start.2 = (f32[9,8,128]{2,1,0:T(8,128)S(1)}, f32[9,8,128]{2,1,0:T(8,128)S(1)}, u32[]{:S(2)}, u32[]{:S(2)}) collective-permute-start(f32[9,8,128]{2,1,0:T(8,128)S(1)} %get-tuple-element.37), channel_id=1, source_target_pairs={{0,8},{8,0},{16,24},{24,16},{1,9},{9,1},{17,25},{25,17},{2,10},{10... | collective-permute-start | bytes 110600 | tf_op jit(solution)/shard_map/ppermute | solution.py:663
  8.1 4.2 %collective-permute-start.3 = (f32[8,8,128]{2,1,0:T(8,128)S(1)}, f32[8,8,128]{2,1,0:T(8,128)S(1)}, u32[]{:S(2)}, u32[]{:S(2)}) collective-permute-start(f32[8,8,128]{2,1,0:T(8,128)S(1)} %get-tuple-element.38.refs_1_), channel_id=1, source_target_pairs={{0,16},{8,24},{16,0},{24,8},{1,17},{9,25},{17,1},{25,9},{2,18},{10... | collective-permute-start | bytes 98312 | tf_op jit(solution)/shard_map/ppermute | solution.py:663
  10.4 3.8 %collective-permute-start.8 = (f32[5,8,128]{2,1,0:T(8,128)S(1)}, f32[5,8,128]{2,1,0:T(8,128)S(1)}, u32[]{:S(2)}, u32[]{:S(2)}) collective-permute-start(f32[5,8,128]{2,1,0:T(8,128)S(1)} %get-tuple-element.43.refs_0_), channel_id=1, source_target_pairs={{0,24},{8,16},{16,8},{24,0},{1,25},{9,17},{17,9},{25,1},{2,26},{10... | collective-permute-start | bytes 61448 | tf_op jit(solution)/shard_map/ppermute | solution.py:663
  10.5 3.8 %collective-permute-start.7 = (f32[5,8,128]{2,1,0:T(8,128)S(1)}, f32[5,8,128]{2,1,0:T(8,128)S(1)}, u32[]{:S(2)}, u32[]{:S(2)}) collective-permute-start(f32[5,8,128]{2,1,0:T(8,128)S(1)} %get-tuple-element.43.refs_0_), channel_id=1, source_target_pairs={{0,16},{8,24},{16,0},{24,8},{1,17},{9,25},{17,1},{25,9},{2,18},{10... | collective-permute-start | bytes 61448 | tf_op jit(solution)/shard_map/ppermute | solution.py:663
  12.1 2.3 %collective-permute-start.6 = (f32[5,8,128]{2,1,0:T(8,128)S(1)}, f32[5,8,128]{2,1,0:T(8,128)S(1)}, u32[]{:S(2)}, u32[]{:S(2)}) collective-permute-start(f32[5,8,128]{2,1,0:T(8,128)S(1)} %get-tuple-element.43.refs_0_), channel_id=1, source_target_pairs={{0,8},{8,0},{16,24},{24,16},{1,9},{9,1},{17,25},{25,17},{2,10},{10... | collective-permute-start | bytes 61448 | tf_op jit(solution)/shard_map/ppermute | solution.py:663
  12.5 1.3 %collective-permute-start.4 = (f32[4,8,128]{2,1,0:T(8,128)S(1)}, f32[4,8,128]{2,1,0:T(8,128)S(1)}, u32[]{:S(2)}, u32[]{:S(2)}) collective-permute-start(f32[4,8,128]{2,1,0:T(8,128)S(1)} %get-tuple-element.41), channel_id=1, source_target_pairs={{0,8},{8,0},{16,24},{24,16},{1,9},{9,1},{17,25},{25,17},{2,10},{10... | collective-permute-start | bytes 49160 | tf_op jit(solution)/shard_map/ppermute | solution.py:663
  12.8 1.2 %collective-permute-start.5 = (f32[4,8,128]{2,1,0:T(8,128)S(1)}, f32[4,8,128]{2,1,0:T(8,128)S(1)}, u32[]{:S(2)}, u32[]{:S(2)}) collective-permute-start(f32[4,8,128]{2,1,0:T(8,128)S(1)} %get-tuple-element.42), channel_id=1, source_target_pairs={{0,8},{8,0},{16,24},{24,16},{1,9},{9,1},{17,25},{25,17},{2,10},{10... | collective-permute-start | bytes 49160 | tf_op jit(solution)/shard_map/ppermute | solution.py:663

commit v8 on v7

--- a/solution.py
+++ b/solution.py
@@ -304,7 +304,9 @@
     return jnp.broadcast_to(message[index, pl.ds(row, 1), :], TILE)
 
 
-def pack_kernel(fine, solid, coarse, coarse_solid, slot, moved, second, high, low, slot_out, strip, shade, rim, sem):
+def pack_kernel(
+    fine, solid, coarse, coarse_solid, slot, moved, second, high, low, center, shade, slot_out, strip, rim, sem
+):
     planes = fine.shape[2]
     last = coarse.shape[2] - 1
 
@@ -323,6 +325,8 @@
         bring(coarse.at[0, :, pl.ds(plane, 1), :], rim.at[pl.ds(0, NPOP), pl.ds(row, 1), :], 1)
         bring(coarse_solid.at[0, pl.ds(plane, 1), :], rim.at[NPOP, pl.ds(row, 1), :], 1)
     bring(slot, slot_out, 2)
+    for first, row in ((4, 4), (8, 0)):
+        bring(fine.at[0, :, pl.ds(first, 4), :], center.at[:, pl.ds(row, 4), :], 3)
     arrive(strip, 0)
     upper = row_ids() < 4
     solids = [
@@ -358,27 +362,29 @@
     pack_message(high, first_of, second_of, [outer[i] for i in FORWARD + [NPOP]], True)
     high[WORDS] = jnp.zeros(TILE, jnp.float32)
     pack_message(low, first_of, second_of, [outer[i] for i in BACKWARD + [NPOP]], False)
-
-
-def inner_steps(fine, solid, moved, inner, packed, work):
+    arrive(center, 3)
+
+
+def inner_steps(center, solid, moved, inner, packed, work):
     upper = row_ids() < 4
-
-    def middle(ref, h, *i):
-        at = half_lanes(h)
-        return jnp.where(upper, ref[(0, *i, pl.ds(ROWS, ROWS), at)], ref[(0, *i, pl.ds(0, ROWS), at)])
-
+    solids = [
+        [solid[pl.ds(ROWS * t, ROWS), half_lanes(h)] for h in range(2)] for t in range(2)
+    ]
     outer = [[moved[i, h] for i in range(NPOP)] for h in range(2)]
-    center = move_in_planes(
+    between = move_in_planes(
         [
-            collide([middle(fine, h, i) for i in range(NPOP)], middle(solid, h), TAU_FINE)
+            collide(
+                [center[i, :, half_lanes(h)] for i in range(NPOP)],
+                jnp.where(upper, solids[1][h], solids[0][h]),
+                TAU_FINE,
+            )
             for h in range(2)
         ]
     )
-    ring = move_along([merge(upper, outer, center), merge(upper, center, outer)])
+    ring = move_along([merge(upper, outer, between), merge(upper, between, outer)])
     for t in range(2):
         for h in range(2):
-            s = solid[0, pl.ds(ROWS * t, ROWS), half_lanes(h)]
-            ring[t][h] = collide(ring[t][h], s, TAU_FINE)
+            ring[t][h] = collide(ring[t][h], solids[t][h], TAU_FINE)
         ring[t] = move_in_planes(ring[t])
     ring = move_along(ring)
     for i in range(NPOP):
@@ -415,16 +421,16 @@
             chosen[q, s] = jnp.where(lane_ids() * 0 + (4 * me + q) == code, 1.0, 0.0)
 
 
-def early_kernel(fine, solid, moved, slot, low, inner, packed, chosen, matrix, low_out, work):
+def early_kernel(center, solid, moved, slot, low, inner, packed, chosen, matrix, low_out, work):
     low_out[...] = low[...]
 
     @pl.when(starts_early())
     def _():
-        inner_steps(fine, solid, moved, inner, packed, work)
+        inner_steps(center, solid, moved, inner, packed, work)
         prepare(slot, chosen, matrix)
 
 
-def inner_kernel(fine, solid, moved, slot, *refs):
+def inner_kernel(center, solid, moved, slot, *refs):
     *refs, padded, work = refs
     done, (inner, packed, chosen, matrix) = refs[:4], refs[4:]
 
@@ -435,7 +441,7 @@
 
     @pl.when(jnp.logical_not(starts_early()))
     def _():
-        inner_steps(fine, solid, moved, inner, packed, work)
+        inner_steps(center, solid, moved, inner, packed, work)
         prepare(slot, chosen, matrix)
 
     size = packed.shape[0]
@@ -694,7 +700,7 @@
 def per_device(fine_pops, fine_solid, coarse_pops, coarse_solid, coarse_slot):
     groups = lax.axis_size("grp")
     blocks = lax.axis_size("blk")
-    moved, second, high, low, slot = call(
+    moved, second, high, low, center, shade, slot = call(
         pack_kernel,
         tuple(map(left, (fine_pops, fine_solid, coarse_pops, coarse_solid, coarse_slot))),
         [pl.ANY] * 5,
@@ -703,17 +709,17 @@
             in_vmem(NPOP, 2, *TILE),
             in_vmem(WORDS + 1, *TILE),
             in_vmem(WORDS, *TILE),
+            in_vmem(NPOP, ROWS, 2 * LANES),
+            in_vmem(*fine_solid.shape[1:]),
             VMEM((groups,), jnp.int32),
         ],
         [
             in_vmem(NPOP + 2, ROWS, 2 * LANES),
-            in_vmem(*fine_solid.shape[1:]),
             in_vmem(NPOP + 1, ROWS, 2 * LANES),
-            pltpu.SemaphoreType.DMA((3,)),
+            pltpu.SemaphoreType.DMA((4,)),
         ],
         name="pack",
     )
-    fine_v, solid_v = held(fine_pops), held(fine_solid)
     coarse_v, coarse_solid_v = held(coarse_pops), held(coarse_solid)
     inner_shapes = [
         in_vmem(NPOP, 2, 2 * ROWS, LANES),
@@ -721,7 +727,7 @@
         in_vmem(4, groups, *TILE),
         VMEM((2 * LANES, LANES), jnp.bfloat16),
     ]
-    inner_args = (fine_v, solid_v, held(moved), held(slot))
+    inner_args = (held(center), held(shade), held(moved), held(slot))
     *done, low = call(
         early_kernel,
         (*inner_args, held(low)),

time: 15.4 us -> 15.3 us (level)
  no operation moved by 1% of the time
where the time goes in v8:
time: 15.3 us; the launch traced here: 15.1 us
  starting transfers between devices  9.7 us (63%)
  Pallas kernels  4.12 us (27%)
  between operations  0.72 us (5%)
  waiting for transfers between devices  0.59 us (4%)
    ppermute x7, starting transfers between devices, exchange(): lax.ppermute(array, 'grp', [(i, i ^ distance) for i in range(groups)])  4.2 us
    pallas_call x9, Pallas kernels, call(): pl.pallas_call(kernel, in_specs=[pl.BlockSpec(memory_space=s) for s in sp...  4.12 us
    ppermute x1, starting transfers between devices, per_device(): below = lax.ppermute(high, 'blk', forward)  3.02 us
    ppermute x1, starting transfers between devices, per_device(): above = lax.ppermute(low, 'blk', backward)  2.48 us
  transfers between devices with their start and end apart: 9, of which 3 were waited for; matrix products, arithmetic and copies ran while one was open for 0% of the time, Pallas kernels for 14%

profile of v8, /device:TPU:0, one launch (start us, length us, event | category | flops | bytes accessed | tf_op | source)
XLA Modules:
  0.0 15.1 jit_solution(17743647839233834305)
XLA Ops:
  0.6 1.2 %pack.1 = (f32[20,2,8,128]{3,2,1,0:T(8,128)S(1)}, f32[19,2,8,128]{3,2,1,0:T(8,128)S(1)}, f32[11,8,128]{2,1,0:T(8,128)S(1)}, f32[10,8,128]{2,1,0:T(8,128)S(1)}, f...) custom-call(f32[1,19,16,256]{3,2,1,0:T(8,128)} %fine.1, f32[1,16,256]{2,1,0:T(8,128)} %solid.3, ...), custom_call_target="tpu_custom_call" | custom-call | bytes 1 | tf_op jit(solution)/shard_map/pack/pallas_call | solution.py:687
  1.8 3.0 %collective-permute-start = (f32[11,8,128]{2,1,0:T(8,128)S(1)}, f32[11,8,128]{2,1,0:T(8,128)S(1)}, u32[]{:S(2)}, u32[]{:S(2)}) collective-permute-start(f32[11,8,128]{2,1,0:T(8,128)S(1)} %get-tuple-element.36), channel_id=1, source_target_pairs={{0,1},{1,2},{2,3},{3,4},{4,5},{5,6},{6,7},{7,0},{8,9},{9,10},{10,1... | collective-permute-start | bytes 135176 | tf_op jit(solution)/shard_map/ppermute | solution.py:741
  4.8 0.6 %early.1 = (f32[19,2,16,128]{3,2,1,0:T(8,128)S(1)}, f32[8,8,128]{2,1,0:T(8,128)S(1)}, f32[4,4,8,128]{3,2,1,0:T(8,128)S(1)}, bf16[256,128]{1,0:T(8,128)(2,1)S(1)}, f32[10,8,128]{2,1,0:T(8,128)S(1)}) custom-call(f32[19,8,256]{2,1,0:T(8,128)S(1)} %get-tuple-element.25.center, f32[16,256]{1,0:T(8,128)S(1)} %get-tuple-element.26.solid, ...), custom_call_target="tpu_custom_call" | custom-call | bytes 1 | tf_op jit(solution)/shard_map/early/pallas_call | solution.py:687
  5.5 2.5 %collective-permute-start.1 = (f32[10,8,128]{2,1,0:T(8,128)S(1)}, f32[10,8,128]{2,1,0:T(8,128)S(1)}, u32[]{:S(2)}, u32[]{:S(2)}) collective-permute-start(f32[10,8,128]{2,1,0:T(8,128)S(1)} %get-tuple-element.37), channel_id=1, source_target_pairs={{0,7},{1,0},{2,1},{3,2},{4,3},{5,4},{6,5},{7,6},{8,15},{9,8},{10,9... | collective-permute-start | bytes 122888 | tf_op jit(solution)/shard_map/ppermute | solution.py:742
  7.9 0.0 copy-start
  7.9 0.0 copy-start.1
  8.0 0.1 collective-permute-start.2
  8.1 1.6 %collective-permute-start.3 = (f32[8,8,128]{2,1,0:T(8,128)S(1)}, f32[8,8,128]{2,1,0:T(8,128)S(1)}, u32[]{:S(2)}, u32[]{:S(2)}) collective-permute-start(f32[8,8,128]{2,1,0:T(8,128)S(1)} %get-tuple-element.42.refs_1_), channel_id=1, source_target_pairs={{0,16},{8,24},{16,0},{24,8},{1,17},{9,25},{17,1},{25,9},{2,18},{10... | collective-permute-start | bytes 98312 | tf_op jit(solution)/shard_map/ppermute | solution.py:669
  9.7 0.3 %collective-permute-done.1.above = f32[10,8,128]{2,1,0:T(8,128)S(1)} collective-permute-done((f32[10,8,128]{2,1,0:T(8,128)S(1)}, f32[10,8,128]{2,1,0:T(8,128)S(1)}, u32[]{:S(2)}, u32[]{:S(2)}) %collective-permute-start.1) | collective-permute-done | bytes 40992 | tf_op jit(solution)/shard_map/ppermute | solution.py:742
  10.0 0.0 collective-permute-done.below
  10.0 0.0 copy-done
  10.0 0.0 copy-done.1
  10.0 0.3 %edge.1 = (f32[19,2,8,128]{3,2,1,0:T(8,128)S(1)}, f32[5,8,128]{2,1,0:T(8,128)S(1)}) custom-call(f32[20,2,8,128]{3,2,1,0:T(8,128)S(1)} %get-tuple-element.27.moved, f32[19,2,8,128]{3,2,1,0:T(8,128)S(1)} %get-tuple-element.35.second, f32[11,8,128]{2,1,0:T(8,128)S(1)} %collective-permute-done.below, f32[10,8,128]{2,1,0:T(8,128)S(1)} %collective-permute-done.1.above, ...), custom_call_target="tpu_custom_call" | custom-call | bytes 1 | tf_op jit(solution)/shard_map/edge/pallas_call | solution.py:687
  10.4 0.1 collective-permute-start.8
  10.4 1.6 %collective-permute-start.7 = (f32[5,8,128]{2,1,0:T(8,128)S(1)}, f32[5,8,128]{2,1,0:T(8,128)S(1)}, u32[]{:S(2)}, u32[]{:S(2)}) collective-permute-start(f32[5,8,128]{2,1,0:T(8,128)S(1)} %get-tuple-element.47.refs_0_), channel_id=1, source_target_pairs={{0,16},{8,24},{16,0},{24,8},{1,17},{9,25},{17,1},{25,9},{2,18},{10... | collective-permute-start | bytes 61448 | tf_op jit(solution)/shard_map/ppermute | solution.py:669
  12.0 0.3 %collective-permute-start.6 = (f32[5,8,128]{2,1,0:T(8,128)S(1)}, f32[5,8,128]{2,1,0:T(8,128)S(1)}, u32[]{:S(2)}, u32[]{:S(2)}) collective-permute-start(f32[5,8,128]{2,1,0:T(8,128)S(1)} %get-tuple-element.47.refs_0_), channel_id=1, source_target_pairs={{0,8},{8,0},{16,24},{24,16},{1,9},{9,1},{17,25},{25,17},{2,10},{10... | collective-permute-start | bytes 61448 | tf_op jit(solution)/shard_map/ppermute | solution.py:669
  12.3 0.0 collective-permute-done.3.refs_2_.tiles
  12.3 0.0 collective-permute-done.2.refs_0_
  12.3 0.1 paste.1
  12.4 0.3 %collective-permute-start.4 = (f32[4,8,128]{2,1,0:T(8,128)S(1)}, f32[4,8,128]{2,1,0:T(8,128)S(1)}, u32[]{:S(2)}, u32[]{:S(2)}) collective-permute-start(f32[4,8,128]{2,1,0:T(8,128)S(1)} %get-tuple-element.45), channel_id=1, source_target_pairs={{0,8},{8,0},{16,24},{24,16},{1,9},{9,1},{17,25},{25,17},{2,10},{10... | collective-permute-start | bytes 49160 | tf_op jit(solution)/shard_map/ppermute | solution.py:669
  12.7 0.3 %collective-permute-start.5 = (f32[4,8,128]{2,1,0:T(8,128)S(1)}, f32[4,8,128]{2,1,0:T(8,128)S(1)}, u32[]{:S(2)}, u32[]{:S(2)}) collective-permute-start(f32[4,8,128]{2,1,0:T(8,128)S(1)} %get-tuple-element.46), channel_id=1, source_target_pairs={{0,8},{8,0},{16,24},{24,16},{1,9},{9,1},{17,25},{25,17},{2,10},{10... | collective-permute-start | bytes 49160 | tf_op jit(solution)/shard_map/ppermute | solution.py:669
  13.0 0.8 %write.1.after = f32[1,19,16,256]{3,2,1,0:T(8,128)} custom-call(f32[19,2,16,128]{3,2,1,0:T(8,128)S(1)} %get-tuple-element.34.inner, f32[19,2,8,128]{3,2,1,0:T(8,128)S(1)} %get-tuple-element.39.edges.after), custom_call_target="tpu_custom_call" | custom-call | bytes 1 | tf_op jit(solution)/shard_map/write/pallas_call | solution.py:687
  13.8 0.0 collective-permute-done.4.refs_0_
  13.8 0.2 %collective-permute-done.5.refs_1_ = f32[4,8,128]{2,1,0:T(8,128)S(1)} collective-permute-done((f32[4,8,128]{2,1,0:T(8,128)S(1)}, f32[4,8,128]{2,1,0:T(8,128)S(1)}, u32[]{:S(2)}, u32[]{:S(2)}) %collective-permute-start.5) | collective-permute-done | bytes 16416 | tf_op jit(solution)/shard_map/ppermute | solution.py:669
  13.9 0.2 %coarse.7.middle = f32[19,2,8,128]{3,2,1,0:T(8,128)S(1)} custom-call(f32[1,19,16,256]{3,2,1,0:T(8,128)} %write.1.after, f32[19,2,8,128]{3,2,1,0:T(8,128)S(1)} %get-tuple-element.44.after.base, f32[1,8,256]{2,1,0:T(8,128)S(1)} %copy-done.1, f32[4,4,8,128]{3,2,1,0:T(8,128)S(1)} %get-tuple-element.40.chosen, f32[4,8,128]{2,1,0:T(8,128)S(1)} %collective-permute-done.4.refs_0_, ...), custom_call_target="tpu_custom_call" | custom-call | bytes 1 | tf_op jit(solution)/shard_map/coarse/pallas_call | solution.py:687
  14.2 0.0 collective-permute-done.8.refs_3_
  14.2 0.1 collective-permute-done.7.refs_2_
  14.3 0.0 collective-permute-done.6.refs_1_
  14.3 0.8 %last.1 = f32[1,19,8,256]{3,2,1,0:T(8,128)} custom-call(f32[4,4,8,128]{3,2,1,0:T(8,128)S(1)} %get-tuple-element.40.chosen, f32[11,8,128]{2,1,0:T(8,128)S(1)} %collective-permute-done.below, f32[10,8,128]{2,1,0:T(8,128)S(1)} %collective-permute-done.1.above, f32[20,8,128]{2,1,0:T(8,128)S(1)} %get-tuple-element.43.base, f32[19,2,8,128]{3,2,1,0:T(8,128)S(1)} %coarse.7.middle, ...), custom_call_target="tpu_custom_call" | custom-call | bytes 1 | tf_op jit(solution)/shard_map/last/pallas_call | solution.py:687
  (2 shorter events, 0.0 us)
Async XLA Ops:
  1.8 8.2 %collective-permute-start = (f32[11,8,128]{2,1,0:T(8,128)S(1)}, f32[11,8,128]{2,1,0:T(8,128)S(1)}, u32[]{:S(2)}, u32[]{:S(2)}) collective-permute-start(f32[11,8,128]{2,1,0:T(8,128)S(1)} %get-tuple-element.36), channel_id=1, source_target_pairs={{0,1},{1,2},{2,3},{3,4},{4,5},{5,6},{6,7},{7,0},{8,9},{9,10},{10,1... | collective-permute-start | bytes 135176 | tf_op jit(solution)/shard_map/ppermute | solution.py:741
  5.5 4.5 %collective-permute-start.1 = (f32[10,8,128]{2,1,0:T(8,128)S(1)}, f32[10,8,128]{2,1,0:T(8,128)S(1)}, u32[]{:S(2)}, u32[]{:S(2)}) collective-permute-start(f32[10,8,128]{2,1,0:T(8,128)S(1)} %get-tuple-element.37), channel_id=1, source_target_pairs={{0,7},{1,0},{2,1},{3,2},{4,3},{5,4},{6,5},{7,6},{8,15},{9,8},{10,9... | collective-permute-start | bytes 122888 | tf_op jit(solution)/shard_map/ppermute | solution.py:742
  7.9 2.1 %copy-start = (f32[1,19,8,256]{3,2,1,0:T(8,128)S(1)}, f32[1,19,8,256]{3,2,1,0:T(8,128)}, u32[]{:S(2)}) copy-start(f32[1,19,8,256]{3,2,1,0:T(8,128)} %coarse.6) | copy-start | bytes 466948
  7.9 2.1 %copy-start.1 = (f32[1,8,256]{2,1,0:T(8,128)S(1)}, f32[1,8,256]{2,1,0:T(8,128)}, u32[]{:S(2)}) copy-start(f32[1,8,256]{2,1,0:T(8,128)} %solid.5) | copy-start | bytes 24580
  8.0 4.3 %collective-permute-start.2 = (f32[9,8,128]{2,1,0:T(8,128)S(1)}, f32[9,8,128]{2,1,0:T(8,128)S(1)}, u32[]{:S(2)}, u32[]{:S(2)}) collective-permute-start(f32[9,8,128]{2,1,0:T(8,128)S(1)} %get-tuple-element.41), channel_id=1, source_target_pairs={{0,8},{8,0},{16,24},{24,16},{1,9},{9,1},{17,25},{25,17},{2,10},{10... | collective-permute-start | bytes 110600 | tf_op jit(solution)/shard_map/ppermute | solution.py:669
  8.1 4.2 %collective-permute-start.3 = (f32[8,8,128]{2,1,0:T(8,128)S(1)}, f32[8,8,128]{2,1,0:T(8,128)S(1)}, u32[]{:S(2)}, u32[]{:S(2)}) collective-permute-start(f32[8,8,128]{2,1,0:T(8,128)S(1)} %get-tuple-element.42.refs_1_), channel_id=1, source_target_pairs={{0,16},{8,24},{16,0},{24,8},{1,17},{9,25},{17,1},{25,9},{2,18},{10... | collective-permute-start | bytes 98312 | tf_op jit(solution)/shard_map/ppermute | solution.py:669
  10.4 3.8 %collective-permute-start.8 = (f32[5,8,128]{2,1,0:T(8,128)S(1)}, f32[5,8,128]{2,1,0:T(8,128)S(1)}, u32[]{:S(2)}, u32[]{:S(2)}) collective-permute-start(f32[5,8,128]{2,1,0:T(8,128)S(1)} %get-tuple-element.47.refs_0_), channel_id=1, source_target_pairs={{0,24},{8,16},{16,8},{24,0},{1,25},{9,17},{17,9},{25,1},{2,26},{10... | collective-permute-start | bytes 61448 | tf_op jit(solution)/shard_map/ppermute | solution.py:669
  10.4 3.8 %collective-permute-start.7 = (f32[5,8,128]{2,1,0:T(8,128)S(1)}, f32[5,8,128]{2,1,0:T(8,128)S(1)}, u32[]{:S(2)}, u32[]{:S(2)}) collective-permute-start(f32[5,8,128]{2,1,0:T(8,128)S(1)} %get-tuple-element.47.refs_0_), channel_id=1, source_target_pairs={{0,16},{8,24},{16,0},{24,8},{1,17},{9,25},{17,1},{25,9},{2,18},{10... | collective-permute-start | bytes 61448 | tf_op jit(solution)/shard_map/ppermute | solution.py:669
  12.0 2.3 %collective-permute-start.6 = (f32[5,8,128]{2,1,0:T(8,128)S(1)}, f32[5,8,128]{2,1,0:T(8,128)S(1)}, u32[]{:S(2)}, u32[]{:S(2)}) collective-permute-start(f32[5,8,128]{2,1,0:T(8,128)S(1)} %get-tuple-element.47.refs_0_), channel_id=1, source_target_pairs={{0,8},{8,0},{16,24},{24,16},{1,9},{9,1},{17,25},{25,17},{2,10},{10... | collective-permute-start | bytes 61448 | tf_op jit(solution)/shard_map/ppermute | solution.py:669
  12.4 1.3 %collective-permute-start.4 = (f32[4,8,128]{2,1,0:T(8,128)S(1)}, f32[4,8,128]{2,1,0:T(8,128)S(1)}, u32[]{:S(2)}, u32[]{:S(2)}) collective-permute-start(f32[4,8,128]{2,1,0:T(8,128)S(1)} %get-tuple-element.45), channel_id=1, source_target_pairs={{0,8},{8,0},{16,24},{24,16},{1,9},{9,1},{17,25},{25,17},{2,10},{10... | collective-permute-start | bytes 49160 | tf_op jit(solution)/shard_map/ppermute | solution.py:669
  12.7 1.2 %collective-permute-start.5 = (f32[4,8,128]{2,1,0:T(8,128)S(1)}, f32[4,8,128]{2,1,0:T(8,128)S(1)}, u32[]{:S(2)}, u32[]{:S(2)}) collective-permute-start(f32[4,8,128]{2,1,0:T(8,128)S(1)} %get-tuple-element.46), channel_id=1, source_target_pairs={{0,8},{8,0},{16,24},{24,16},{1,9},{9,1},{17,25},{25,17},{2,10},{10... | collective-permute-start | bytes 49160 | tf_op jit(solution)/shard_map/ppermute | solution.py:669

commit v9 on v8

--- a/solution.py
+++ b/solution.py
@@ -365,7 +365,7 @@
     arrive(center, 3)
 
 
-def inner_steps(center, solid, moved, inner, packed, work):
+def inner_steps(center, solid, moved, inner, packed):
     upper = row_ids() < 4
     solids = [
         [solid[pl.ds(ROWS * t, ROWS), half_lanes(h)] for h in range(2)] for t in range(2)
@@ -391,10 +391,9 @@
         for h in range(2):
             for t in range(2):
                 inner[i, h, pl.ds(ROWS * t, ROWS), :] = ring[t][h][i]
-                work[i, h, pl.ds(ROWS * t, ROWS), :] = ring[t][h][i]
     sums = [
         [
-            work[i, h, pl.ds(0, ROWS, stride=2), :] + work[i, h, pl.ds(1, ROWS, stride=2), :]
+            inner[i, h, pl.ds(0, ROWS, stride=2), :] + inner[i, h, pl.ds(1, ROWS, stride=2), :]
             for h in range(2)
         ]
         for i in range(NPOP)
@@ -421,17 +420,17 @@
             chosen[q, s] = jnp.where(lane_ids() * 0 + (4 * me + q) == code, 1.0, 0.0)
 
 
-def early_kernel(center, solid, moved, slot, low, inner, packed, chosen, matrix, low_out, work):
+def early_kernel(center, solid, moved, slot, low, inner, packed, chosen, matrix, low_out):
     low_out[...] = low[...]
 
     @pl.when(starts_early())
     def _():
-        inner_steps(center, solid, moved, inner, packed, work)
+        inner_steps(center, solid, moved, inner, packed)
         prepare(slot, chosen, matrix)
 
 
 def inner_kernel(center, solid, moved, slot, *refs):
-    *refs, padded, work = refs
+    *refs, padded = refs
     done, (inner, packed, chosen, matrix) = refs[:4], refs[4:]
 
     @pl.when(starts_early())
@@ -441,7 +440,7 @@
 
     @pl.when(jnp.logical_not(starts_early()))
     def _():
-        inner_steps(center, solid, moved, inner, packed, work)
+        inner_steps(center, solid, moved, inner, packed)
         prepare(slot, chosen, matrix)
 
     size = packed.shape[0]
@@ -733,7 +732,6 @@
         (*inner_args, held(low)),
         [VMEM] * 5,
         [*inner_shapes, in_vmem(WORDS, *TILE)],
-        inner_shapes[:1],
         name="early",
     )
     forward = [(i, (i + 1) % blocks) for i in range(blocks)]
@@ -745,7 +743,6 @@
         (*inner_args, *map(held, done)),
         [VMEM] * 8,
         [*inner_shapes, in_vmem(INNER_TILES + 1, *TILE)],
-        inner_shapes[:1],
         name="inner",
     )
 

time: 15.3 us -> 15.3 us (level)
  no operation moved by 1% of the time
where the time goes in v9:
time: 15.3 us; the launch traced here: 15.1 us
  starting transfers between devices  9.71 us (63%)
  Pallas kernels  4.12 us (27%)
  between operations  0.72 us (5%)
  waiting for transfers between devices  0.59 us (4%)
    ppermute x7, starting transfers between devices, exchange(): lax.ppermute(array, 'grp', [(i, i ^ distance) for i in range(groups)])  4.2 us
    pallas_call x9, Pallas kernels, call(): pl.pallas_call(kernel, in_specs=[pl.BlockSpec(memory_space=s) for s in sp...  4.12 us
    ppermute x1, starting transfers between devices, per_device(): below = lax.ppermute(high, 'blk', forward)  3.02 us
    ppermute x1, starting transfers between devices, per_device(): above = lax.ppermute(low, 'blk', backward)  2.48 us
  transfers between devices with their start and end apart: 9, of which 3 were waited for; matrix products, arithmetic and copies ran while one was open for 0% of the time, Pallas kernels for 14%

profile of v9, /device:TPU:0, one launch (start us, length us, event | category | flops | bytes accessed | tf_op | source)
XLA Modules:
  0.0 15.1 jit_solution(10951104371164169856)
XLA Ops:
  0.6 1.2 %pack.1 = (f32[20,2,8,128]{3,2,1,0:T(8,128)S(1)}, f32[19,2,8,128]{3,2,1,0:T(8,128)S(1)}, f32[11,8,128]{2,1,0:T(8,128)S(1)}, f32[10,8,128]{2,1,0:T(8,128)S(1)}, f...) custom-call(f32[1,19,16,256]{3,2,1,0:T(8,128)} %fine.1, f32[1,16,256]{2,1,0:T(8,128)} %solid.3, ...), custom_call_target="tpu_custom_call" | custom-call | bytes 1 | tf_op jit(solution)/shard_map/pack/pallas_call | solution.py:686
  1.8 3.0 %collective-permute-start = (f32[11,8,128]{2,1,0:T(8,128)S(1)}, f32[11,8,128]{2,1,0:T(8,128)S(1)}, u32[]{:S(2)}, u32[]{:S(2)}) collective-permute-start(f32[11,8,128]{2,1,0:T(8,128)S(1)} %get-tuple-element.36), channel_id=1, source_target_pairs={{0,1},{1,2},{2,3},{3,4},{4,5},{5,6},{6,7},{7,0},{8,9},{9,10},{10,1... | collective-permute-start | bytes 135176 | tf_op jit(solution)/shard_map/ppermute | solution.py:739
  4.8 0.6 %early.1 = (f32[19,2,16,128]{3,2,1,0:T(8,128)S(1)}, f32[8,8,128]{2,1,0:T(8,128)S(1)}, f32[4,4,8,128]{3,2,1,0:T(8,128)S(1)}, bf16[256,128]{1,0:T(8,128)(2,1)S(1)}, f32[10,8,128]{2,1,0:T(8,128)S(1)}) custom-call(f32[19,8,256]{2,1,0:T(8,128)S(1)} %get-tuple-element.25.center, f32[16,256]{1,0:T(8,128)S(1)} %get-tuple-element.26.solid, ...), custom_call_target="tpu_custom_call" | custom-call | bytes 1 | tf_op jit(solution)/shard_map/early/pallas_call | solution.py:686
  5.5 2.5 %collective-permute-start.1 = (f32[10,8,128]{2,1,0:T(8,128)S(1)}, f32[10,8,128]{2,1,0:T(8,128)S(1)}, u32[]{:S(2)}, u32[]{:S(2)}) collective-permute-start(f32[10,8,128]{2,1,0:T(8,128)S(1)} %get-tuple-element.37), channel_id=1, source_target_pairs={{0,7},{1,0},{2,1},{3,2},{4,3},{5,4},{6,5},{7,6},{8,15},{9,8},{10,9... | collective-permute-start | bytes 122888 | tf_op jit(solution)/shard_map/ppermute | solution.py:740
  7.9 0.0 copy-start
  7.9 0.0 copy-start.1
  8.0 0.1 collective-permute-start.2
  8.1 1.6 %collective-permute-start.3 = (f32[8,8,128]{2,1,0:T(8,128)S(1)}, f32[8,8,128]{2,1,0:T(8,128)S(1)}, u32[]{:S(2)}, u32[]{:S(2)}) collective-permute-start(f32[8,8,128]{2,1,0:T(8,128)S(1)} %get-tuple-element.42.refs_1_), channel_id=1, source_target_pairs={{0,16},{8,24},{16,0},{24,8},{1,17},{9,25},{17,1},{25,9},{2,18},{10... | collective-permute-start | bytes 98312 | tf_op jit(solution)/shard_map/ppermute | solution.py:668
  9.7 0.3 %collective-permute-done.1.above = f32[10,8,128]{2,1,0:T(8,128)S(1)} collective-permute-done((f32[10,8,128]{2,1,0:T(8,128)S(1)}, f32[10,8,128]{2,1,0:T(8,128)S(1)}, u32[]{:S(2)}, u32[]{:S(2)}) %collective-permute-start.1) | collective-permute-done | bytes 40992 | tf_op jit(solution)/shard_map/ppermute | solution.py:740
  10.0 0.0 collective-permute-done.below
  10.0 0.0 copy-done
  10.0 0.0 copy-done.1
  10.0 0.3 %edge.1 = (f32[19,2,8,128]{3,2,1,0:T(8,128)S(1)}, f32[5,8,128]{2,1,0:T(8,128)S(1)}) custom-call(f32[20,2,8,128]{3,2,1,0:T(8,128)S(1)} %get-tuple-element.27.moved, f32[19,2,8,128]{3,2,1,0:T(8,128)S(1)} %get-tuple-element.35.second, f32[11,8,128]{2,1,0:T(8,128)S(1)} %collective-permute-done.below, f32[10,8,128]{2,1,0:T(8,128)S(1)} %collective-permute-done.1.above, ...), custom_call_target="tpu_custom_call" | custom-call | bytes 1 | tf_op jit(solution)/shard_map/edge/pallas_call | solution.py:686
  10.4 0.1 collective-permute-start.8
  10.4 1.6 %collective-permute-start.7 = (f32[5,8,128]{2,1,0:T(8,128)S(1)}, f32[5,8,128]{2,1,0:T(8,128)S(1)}, u32[]{:S(2)}, u32[]{:S(2)}) collective-permute-start(f32[5,8,128]{2,1,0:T(8,128)S(1)} %get-tuple-element.47.refs_0_), channel_id=1, source_target_pairs={{0,16},{8,24},{16,0},{24,8},{1,17},{9,25},{17,1},{25,9},{2,18},{10... | collective-permute-start | bytes 61448 | tf_op jit(solution)/shard_map/ppermute | solution.py:668
  12.0 0.3 %collective-permute-start.6 = (f32[5,8,128]{2,1,0:T(8,128)S(1)}, f32[5,8,128]{2,1,0:T(8,128)S(1)}, u32[]{:S(2)}, u32[]{:S(2)}) collective-permute-start(f32[5,8,128]{2,1,0:T(8,128)S(1)} %get-tuple-element.47.refs_0_), channel_id=1, source_target_pairs={{0,8},{8,0},{16,24},{24,16},{1,9},{9,1},{17,25},{25,17},{2,10},{10... | collective-permute-start | bytes 61448 | tf_op jit(solution)/shard_map/ppermute | solution.py:668
  12.3 0.0 collective-permute-done.3.refs_2_.tiles
  12.3 0.0 collective-permute-done.2.refs_0_
  12.3 0.1 paste.1
  12.4 0.3 %collective-permute-start.4 = (f32[4,8,128]{2,1,0:T(8,128)S(1)}, f32[4,8,128]{2,1,0:T(8,128)S(1)}, u32[]{:S(2)}, u32[]{:S(2)}) collective-permute-start(f32[4,8,128]{2,1,0:T(8,128)S(1)} %get-tuple-element.45), channel_id=1, source_target_pairs={{0,8},{8,0},{16,24},{24,16},{1,9},{9,1},{17,25},{25,17},{2,10},{10... | collective-permute-start | bytes 49160 | tf_op jit(solution)/shard_map/ppermute | solution.py:668
  12.7 0.3 %collective-permute-start.5 = (f32[4,8,128]{2,1,0:T(8,128)S(1)}, f32[4,8,128]{2,1,0:T(8,128)S(1)}, u32[]{:S(2)}, u32[]{:S(2)}) collective-permute-start(f32[4,8,128]{2,1,0:T(8,128)S(1)} %get-tuple-element.46), channel_id=1, source_target_pairs={{0,8},{8,0},{16,24},{24,16},{1,9},{9,1},{17,25},{25,17},{2,10},{10... | collective-permute-start | bytes 49160 | tf_op jit(solution)/shard_map/ppermute | solution.py:668
  13.0 0.8 %write.1.after = f32[1,19,16,256]{3,2,1,0:T(8,128)} custom-call(f32[19,2,16,128]{3,2,1,0:T(8,128)S(1)} %get-tuple-element.34.inner, f32[19,2,8,128]{3,2,1,0:T(8,128)S(1)} %get-tuple-element.39.edges.after), custom_call_target="tpu_custom_call" | custom-call | bytes 1 | tf_op jit(solution)/shard_map/write/pallas_call | solution.py:686
  13.8 0.0 collective-permute-done.4.refs_0_
  13.8 0.2 %collective-permute-done.5.refs_1_ = f32[4,8,128]{2,1,0:T(8,128)S(1)} collective-permute-done((f32[4,8,128]{2,1,0:T(8,128)S(1)}, f32[4,8,128]{2,1,0:T(8,128)S(1)}, u32[]{:S(2)}, u32[]{:S(2)}) %collective-permute-start.5) | collective-permute-done | bytes 16416 | tf_op jit(solution)/shard_map/ppermute | solution.py:668
  13.9 0.2 %coarse.7.middle = f32[19,2,8,128]{3,2,1,0:T(8,128)S(1)} custom-call(f32[1,19,16,256]{3,2,1,0:T(8,128)} %write.1.after, f32[19,2,8,128]{3,2,1,0:T(8,128)S(1)} %get-tuple-element.44.after.base, f32[1,8,256]{2,1,0:T(8,128)S(1)} %copy-done.1, f32[4,4,8,128]{3,2,1,0:T(8,128)S(1)} %get-tuple-element.40.chosen, f32[4,8,128]{2,1,0:T(8,128)S(1)} %collective-permute-done.4.refs_0_, ...), custom_call_target="tpu_custom_call" | custom-call | bytes 1 | tf_op jit(solution)/shard_map/coarse/pallas_call | solution.py:686
  14.2 0.0 collective-permute-done.8.refs_3_
  14.2 0.1 collective-permute-done.7.refs_2_
  14.3 0.0 collective-permute-done.6.refs_1_
  14.3 0.8 %last.1 = f32[1,19,8,256]{3,2,1,0:T(8,128)} custom-call(f32[4,4,8,128]{3,2,1,0:T(8,128)S(1)} %get-tuple-element.40.chosen, f32[11,8,128]{2,1,0:T(8,128)S(1)} %collective-permute-done.below, f32[10,8,128]{2,1,0:T(8,128)S(1)} %collective-permute-done.1.above, f32[20,8,128]{2,1,0:T(8,128)S(1)} %get-tuple-element.43.base, f32[19,2,8,128]{3,2,1,0:T(8,128)S(1)} %coarse.7.middle, ...), custom_call_target="tpu_custom_call" | custom-call | bytes 1 | tf_op jit(solution)/shard_map/last/pallas_call | solution.py:686
  (2 shorter events, 0.0 us)
Async XLA Ops:
  1.8 8.2 %collective-permute-start = (f32[11,8,128]{2,1,0:T(8,128)S(1)}, f32[11,8,128]{2,1,0:T(8,128)S(1)}, u32[]{:S(2)}, u32[]{:S(2)}) collective-permute-start(f32[11,8,128]{2,1,0:T(8,128)S(1)} %get-tuple-element.36), channel_id=1, source_target_pairs={{0,1},{1,2},{2,3},{3,4},{4,5},{5,6},{6,7},{7,0},{8,9},{9,10},{10,1... | collective-permute-start | bytes 135176 | tf_op jit(solution)/shard_map/ppermute | solution.py:739
  5.5 4.5 %collective-permute-start.1 = (f32[10,8,128]{2,1,0:T(8,128)S(1)}, f32[10,8,128]{2,1,0:T(8,128)S(1)}, u32[]{:S(2)}, u32[]{:S(2)}) collective-permute-start(f32[10,8,128]{2,1,0:T(8,128)S(1)} %get-tuple-element.37), channel_id=1, source_target_pairs={{0,7},{1,0},{2,1},{3,2},{4,3},{5,4},{6,5},{7,6},{8,15},{9,8},{10,9... | collective-permute-start | bytes 122888 | tf_op jit(solution)/shard_map/ppermute | solution.py:740
  7.9 2.1 %copy-start = (f32[1,19,8,256]{3,2,1,0:T(8,128)S(1)}, f32[1,19,8,256]{3,2,1,0:T(8,128)}, u32[]{:S(2)}) copy-start(f32[1,19,8,256]{3,2,1,0:T(8,128)} %coarse.6) | copy-start | bytes 466948
  7.9 2.1 %copy-start.1 = (f32[1,8,256]{2,1,0:T(8,128)S(1)}, f32[1,8,256]{2,1,0:T(8,128)}, u32[]{:S(2)}) copy-start(f32[1,8,256]{2,1,0:T(8,128)} %solid.5) | copy-start | bytes 24580
  8.0 4.3 %collective-permute-start.2 = (f32[9,8,128]{2,1,0:T(8,128)S(1)}, f32[9,8,128]{2,1,0:T(8,128)S(1)}, u32[]{:S(2)}, u32[]{:S(2)}) collective-permute-start(f32[9,8,128]{2,1,0:T(8,128)S(1)} %get-tuple-element.41), channel_id=1, source_target_pairs={{0,8},{8,0},{16,24},{24,16},{1,9},{9,1},{17,25},{25,17},{2,10},{10... | collective-permute-start | bytes 110600 | tf_op jit(solution)/shard_map/ppermute | solution.py:668
  8.1 4.2 %collective-permute-start.3 = (f32[8,8,128]{2,1,0:T(8,128)S(1)}, f32[8,8,128]{2,1,0:T(8,128)S(1)}, u32[]{:S(2)}, u32[]{:S(2)}) collective-permute-start(f32[8,8,128]{2,1,0:T(8,128)S(1)} %get-tuple-element.42.refs_1_), channel_id=1, source_target_pairs={{0,16},{8,24},{16,0},{24,8},{1,17},{9,25},{17,1},{25,9},{2,18},{10... | collective-permute-start | bytes 98312 | tf_op jit(solution)/shard_map/ppermute | solution.py:668
  10.4 3.8 %collective-permute-start.8 = (f32[5,8,128]{2,1,0:T(8,128)S(1)}, f32[5,8,128]{2,1,0:T(8,128)S(1)}, u32[]{:S(2)}, u32[]{:S(2)}) collective-permute-start(f32[5,8,128]{2,1,0:T(8,128)S(1)} %get-tuple-element.47.refs_0_), channel_id=1, source_target_pairs={{0,24},{8,16},{16,8},{24,0},{1,25},{9,17},{17,9},{25,1},{2,26},{10... | collective-permute-start | bytes 61448 | tf_op jit(solution)/shard_map/ppermute | solution.py:668
  10.4 3.8 %collective-permute-start.7 = (f32[5,8,128]{2,1,0:T(8,128)S(1)}, f32[5,8,128]{2,1,0:T(8,128)S(1)}, u32[]{:S(2)}, u32[]{:S(2)}) collective-permute-start(f32[5,8,128]{2,1,0:T(8,128)S(1)} %get-tuple-element.47.refs_0_), channel_id=1, source_target_pairs={{0,16},{8,24},{16,0},{24,8},{1,17},{9,25},{17,1},{25,9},{2,18},{10... | collective-permute-start | bytes 61448 | tf_op jit(solution)/shard_map/ppermute | solution.py:668
  12.0 2.3 %collective-permute-start.6 = (f32[5,8,128]{2,1,0:T(8,128)S(1)}, f32[5,8,128]{2,1,0:T(8,128)S(1)}, u32[]{:S(2)}, u32[]{:S(2)}) collective-permute-start(f32[5,8,128]{2,1,0:T(8,128)S(1)} %get-tuple-element.47.refs_0_), channel_id=1, source_target_pairs={{0,8},{8,0},{16,24},{24,16},{1,9},{9,1},{17,25},{25,17},{2,10},{10... | collective-permute-start | bytes 61448 | tf_op jit(solution)/shard_map/ppermute | solution.py:668
  12.4 1.3 %collective-permute-start.4 = (f32[4,8,128]{2,1,0:T(8,128)S(1)}, f32[4,8,128]{2,1,0:T(8,128)S(1)}, u32[]{:S(2)}, u32[]{:S(2)}) collective-permute-start(f32[4,8,128]{2,1,0:T(8,128)S(1)} %get-tuple-element.45), channel_id=1, source_target_pairs={{0,8},{8,0},{16,24},{24,16},{1,9},{9,1},{17,25},{25,17},{2,10},{10... | collective-permute-start | bytes 49160 | tf_op jit(solution)/shard_map/ppermute | solution.py:668
  12.7 1.2 %collective-permute-start.5 = (f32[4,8,128]{2,1,0:T(8,128)S(1)}, f32[4,8,128]{2,1,0:T(8,128)S(1)}, u32[]{:S(2)}, u32[]{:S(2)}) collective-permute-start(f32[4,8,128]{2,1,0:T(8,128)S(1)} %get-tuple-element.46), channel_id=1, source_target_pairs={{0,8},{8,0},{16,24},{24,16},{1,9},{9,1},{17,25},{25,17},{2,10},{10... | collective-permute-start | bytes 49160 | tf_op jit(solution)/shard_map/ppermute | solution.py:668

commit v10 on v9

--- a/solution.py
+++ b/solution.py
@@ -783,7 +783,7 @@
     for part in across:
         halves = call(
             split_kernel,
-            (held(base), held(part)),
+            (held(edges), held(part)),
             [VMEM] * 2,
             [in_vmem(part.shape[0] // 2, *TILE)] * 2,
             name="split",

time: 15.3 us -> 15.3 us (level)
  transfers between devices with their start and end apart: 9 -> 9, of which waited for: 3 -> 2; matrix products, arithmetic and copies ran while one was open for 0% -> 0% of each run, Pallas kernels for 14% -> 14%
where the time goes in v10:
time: 15.3 us; the launch traced here: 15.1 us
  starting transfers between devices  9.64 us (63%)
  Pallas kernels  4.12 us (27%)
  between operations  0.72 us (5%)
  waiting for transfers between devices  0.66 us (4%)
    ppermute x7, starting transfers between devices, exchange(): lax.ppermute(array, 'grp', [(i, i ^ distance) for i in range(groups)])  4.14 us
    pallas_call x9, Pallas kernels, call(): pl.pallas_call(kernel, in_specs=[pl.BlockSpec(memory_space=s) for s in sp...  4.12 us
    ppermute x1, starting transfers between devices, per_device(): below = lax.ppermute(high, 'blk', forward)  3.02 us
    ppermute x1, starting transfers between devices, per_device(): above = lax.ppermute(low, 'blk', backward)  2.48 us
    ppermute x7, waiting for transfers between devices, exchange(): lax.ppermute(array, 'grp', [(i, i ^ distance) for i in range(groups)])  0.36 us
  transfers between devices with their start and end apart: 9, of which 2 were waited for; matrix products, arithmetic and copies ran while one was open for 0% of the time, Pallas kernels for 14%

profile of v10, /device:TPU:0, one launch (start us, length us, event | category | flops | bytes accessed | tf_op | source)
XLA Modules:
  0.0 15.1 jit_solution(8978376115604889587)
XLA Ops:
  0.6 1.2 %pack.1 = (f32[20,2,8,128]{3,2,1,0:T(8,128)S(1)}, f32[19,2,8,128]{3,2,1,0:T(8,128)S(1)}, f32[11,8,128]{2,1,0:T(8,128)S(1)}, f32[10,8,128]{2,1,0:T(8,128)S(1)}, f...) custom-call(f32[1,19,16,256]{3,2,1,0:T(8,128)} %fine.1, f32[1,16,256]{2,1,0:T(8,128)} %solid.3, ...), custom_call_target="tpu_custom_call" | custom-call | bytes 1 | tf_op jit(solution)/shard_map/pack/pallas_call | solution.py:686
  1.8 3.0 %collective-permute-start = (f32[11,8,128]{2,1,0:T(8,128)S(1)}, f32[11,8,128]{2,1,0:T(8,128)S(1)}, u32[]{:S(2)}, u32[]{:S(2)}) collective-permute-start(f32[11,8,128]{2,1,0:T(8,128)S(1)} %get-tuple-element.36), channel_id=1, source_target_pairs={{0,1},{1,2},{2,3},{3,4},{4,5},{5,6},{6,7},{7,0},{8,9},{9,10},{10,1... | collective-permute-start | bytes 135176 | tf_op jit(solution)/shard_map/ppermute | solution.py:739
  4.8 0.6 %early.1 = (f32[19,2,16,128]{3,2,1,0:T(8,128)S(1)}, f32[8,8,128]{2,1,0:T(8,128)S(1)}, f32[4,4,8,128]{3,2,1,0:T(8,128)S(1)}, bf16[256,128]{1,0:T(8,128)(2,1)S(1)}, f32[10,8,128]{2,1,0:T(8,128)S(1)}) custom-call(f32[19,8,256]{2,1,0:T(8,128)S(1)} %get-tuple-element.25.center, f32[16,256]{1,0:T(8,128)S(1)} %get-tuple-element.26.solid, ...), custom_call_target="tpu_custom_call" | custom-call | bytes 1 | tf_op jit(solution)/shard_map/early/pallas_call | solution.py:686
  5.5 2.5 %collective-permute-start.1 = (f32[10,8,128]{2,1,0:T(8,128)S(1)}, f32[10,8,128]{2,1,0:T(8,128)S(1)}, u32[]{:S(2)}, u32[]{:S(2)}) collective-permute-start(f32[10,8,128]{2,1,0:T(8,128)S(1)} %get-tuple-element.37), channel_id=1, source_target_pairs={{0,7},{1,0},{2,1},{3,2},{4,3},{5,4},{6,5},{7,6},{8,15},{9,8},{10,9... | collective-permute-start | bytes 122888 | tf_op jit(solution)/shard_map/ppermute | solution.py:740
  7.9 0.0 copy-start
  7.9 0.0 copy-start.1
  8.0 0.1 collective-permute-start.2
  8.1 1.6 %collective-permute-start.3 = (f32[8,8,128]{2,1,0:T(8,128)S(1)}, f32[8,8,128]{2,1,0:T(8,128)S(1)}, u32[]{:S(2)}, u32[]{:S(2)}) collective-permute-start(f32[8,8,128]{2,1,0:T(8,128)S(1)} %get-tuple-element.42.refs_1_), channel_id=1, source_target_pairs={{0,16},{8,24},{16,0},{24,8},{1,17},{9,25},{17,1},{25,9},{2,18},{10... | collective-permute-start | bytes 98312 | tf_op jit(solution)/shard_map/ppermute | solution.py:668
  9.7 0.3 %collective-permute-done.1.above = f32[10,8,128]{2,1,0:T(8,128)S(1)} collective-permute-done((f32[10,8,128]{2,1,0:T(8,128)S(1)}, f32[10,8,128]{2,1,0:T(8,128)S(1)}, u32[]{:S(2)}, u32[]{:S(2)}) %collective-permute-start.1) | collective-permute-done | bytes 40992 | tf_op jit(solution)/shard_map/ppermute | solution.py:740
  10.0 0.0 collective-permute-done.below
  10.0 0.0 copy-done
  10.0 0.0 copy-done.1
  10.0 0.3 %edge.1 = (f32[19,2,8,128]{3,2,1,0:T(8,128)S(1)}, f32[5,8,128]{2,1,0:T(8,128)S(1)}) custom-call(f32[20,2,8,128]{3,2,1,0:T(8,128)S(1)} %get-tuple-element.27.moved, f32[19,2,8,128]{3,2,1,0:T(8,128)S(1)} %get-tuple-element.35.second, f32[11,8,128]{2,1,0:T(8,128)S(1)} %collective-permute-done.below, f32[10,8,128]{2,1,0:T(8,128)S(1)} %collective-permute-done.1.above, ...), custom_call_target="tpu_custom_call" | custom-call | bytes 1 | tf_op jit(solution)/shard_map/edge/pallas_call | solution.py:686
  10.4 0.1 collective-permute-start.8
  10.4 1.6 %collective-permute-start.7 = (f32[5,8,128]{2,1,0:T(8,128)S(1)}, f32[5,8,128]{2,1,0:T(8,128)S(1)}, u32[]{:S(2)}, u32[]{:S(2)}) collective-permute-start(f32[5,8,128]{2,1,0:T(8,128)S(1)} %get-tuple-element.47.refs_0_), channel_id=1, source_target_pairs={{0,16},{8,24},{16,0},{24,8},{1,17},{9,25},{17,1},{25,9},{2,18},{10... | collective-permute-start | bytes 61448 | tf_op jit(solution)/shard_map/ppermute | solution.py:668
  12.0 0.3 %collective-permute-start.6 = (f32[5,8,128]{2,1,0:T(8,128)S(1)}, f32[5,8,128]{2,1,0:T(8,128)S(1)}, u32[]{:S(2)}, u32[]{:S(2)}) collective-permute-start(f32[5,8,128]{2,1,0:T(8,128)S(1)} %get-tuple-element.47.refs_0_), channel_id=1, source_target_pairs={{0,8},{8,0},{16,24},{24,16},{1,9},{9,1},{17,25},{25,17},{2,10},{10... | collective-permute-start | bytes 61448 | tf_op jit(solution)/shard_map/ppermute | solution.py:668
  12.3 0.0 collective-permute-done.3.refs_2_.tiles
  12.3 0.3 %collective-permute-start.4 = (f32[4,8,128]{2,1,0:T(8,128)S(1)}, f32[4,8,128]{2,1,0:T(8,128)S(1)}, u32[]{:S(2)}, u32[]{:S(2)}) collective-permute-start(f32[4,8,128]{2,1,0:T(8,128)S(1)} %get-tuple-element.45), channel_id=1, source_target_pairs={{0,8},{8,0},{16,24},{24,16},{1,9},{9,1},{17,25},{25,17},{2,10},{10... | collective-permute-start | bytes 49160 | tf_op jit(solution)/shard_map/ppermute | solution.py:668
  12.6 0.0 collective-permute-done.2.refs_0_
  12.6 0.3 %collective-permute-start.5 = (f32[4,8,128]{2,1,0:T(8,128)S(1)}, f32[4,8,128]{2,1,0:T(8,128)S(1)}, u32[]{:S(2)}, u32[]{:S(2)}) collective-permute-start(f32[4,8,128]{2,1,0:T(8,128)S(1)} %get-tuple-element.46), channel_id=1, source_target_pairs={{0,8},{8,0},{16,24},{24,16},{1,9},{9,1},{17,25},{25,17},{2,10},{10... | collective-permute-start | bytes 49160 | tf_op jit(solution)/shard_map/ppermute | solution.py:668
  12.8 0.8 %write.1.after = f32[1,19,16,256]{3,2,1,0:T(8,128)} custom-call(f32[19,2,16,128]{3,2,1,0:T(8,128)S(1)} %get-tuple-element.34.inner, f32[19,2,8,128]{3,2,1,0:T(8,128)S(1)} %get-tuple-element.39.edges.after), custom_call_target="tpu_custom_call" | custom-call | bytes 1 | tf_op jit(solution)/shard_map/write/pallas_call | solution.py:686
  13.6 0.1 paste.1
  13.7 0.0 collective-permute-done.4.refs_0_
  13.7 0.0 collective-permute-done.5.refs_1_
  13.7 0.2 %coarse.7.middle = f32[19,2,8,128]{3,2,1,0:T(8,128)S(1)} custom-call(f32[1,19,16,256]{3,2,1,0:T(8,128)} %write.1.after, f32[19,2,8,128]{3,2,1,0:T(8,128)S(1)} %get-tuple-element.44.base, f32[1,8,256]{2,1,0:T(8,128)S(1)} %copy-done.1, f32[4,4,8,128]{3,2,1,0:T(8,128)S(1)} %get-tuple-element.40.chosen, f32[4,8,128]{2,1,0:T(8,128)S(1)} %collective-permute-done.4.refs_0_, ...), custom_call_target="tpu_custom_call" | custom-call | bytes 1 | tf_op jit(solution)/shard_map/coarse/pallas_call | solution.py:686
  14.0 0.0 collective-permute-done.8.refs_3_
  14.0 0.3 %collective-permute-done.7.refs_2_ = f32[5,8,128]{2,1,0:T(8,128)S(1)} collective-permute-done((f32[5,8,128]{2,1,0:T(8,128)S(1)}, f32[5,8,128]{2,1,0:T(8,128)S(1)}, u32[]{:S(2)}, u32[]{:S(2)}) %collective-permute-start.7) | collective-permute-done | bytes 20512 | tf_op jit(solution)/shard_map/ppermute | solution.py:668
  14.3 0.0 collective-permute-done.6.refs_1_
  14.3 0.8 %last.1 = f32[1,19,8,256]{3,2,1,0:T(8,128)} custom-call(f32[4,4,8,128]{3,2,1,0:T(8,128)S(1)} %get-tuple-element.40.chosen, f32[11,8,128]{2,1,0:T(8,128)S(1)} %collective-permute-done.below, f32[10,8,128]{2,1,0:T(8,128)S(1)} %collective-permute-done.1.above, f32[20,8,128]{2,1,0:T(8,128)S(1)} %get-tuple-element.43.base, f32[19,2,8,128]{3,2,1,0:T(8,128)S(1)} %coarse.7.middle, ...), custom_call_target="tpu_custom_call" | custom-call | bytes 1 | tf_op jit(solution)/shard_map/last/pallas_call | solution.py:686
  (2 shorter events, 0.0 us)
Async XLA Ops:
  1.8 8.2 %collective-permute-start = (f32[11,8,128]{2,1,0:T(8,128)S(1)}, f32[11,8,128]{2,1,0:T(8,128)S(1)}, u32[]{:S(2)}, u32[]{:S(2)}) collective-permute-start(f32[11,8,128]{2,1,0:T(8,128)S(1)} %get-tuple-element.36), channel_id=1, source_target_pairs={{0,1},{1,2},{2,3},{3,4},{4,5},{5,6},{6,7},{7,0},{8,9},{9,10},{10,1... | collective-permute-start | bytes 135176 | tf_op jit(solution)/shard_map/ppermute | solution.py:739
  5.5 4.5 %collective-permute-start.1 = (f32[10,8,128]{2,1,0:T(8,128)S(1)}, f32[10,8,128]{2,1,0:T(8,128)S(1)}, u32[]{:S(2)}, u32[]{:S(2)}) collective-permute-start(f32[10,8,128]{2,1,0:T(8,128)S(1)} %get-tuple-element.37), channel_id=1, source_target_pairs={{0,7},{1,0},{2,1},{3,2},{4,3},{5,4},{6,5},{7,6},{8,15},{9,8},{10,9... | collective-permute-start | bytes 122888 | tf_op jit(solution)/shard_map/ppermute | solution.py:740
  7.9 2.1 %copy-start = (f32[1,19,8,256]{3,2,1,0:T(8,128)S(1)}, f32[1,19,8,256]{3,2,1,0:T(8,128)}, u32[]{:S(2)}) copy-start(f32[1,19,8,256]{3,2,1,0:T(8,128)} %coarse.6) | copy-start | bytes 466948
  7.9 2.1 %copy-start.1 = (f32[1,8,256]{2,1,0:T(8,128)S(1)}, f32[1,8,256]{2,1,0:T(8,128)}, u32[]{:S(2)}) copy-start(f32[1,8,256]{2,1,0:T(8,128)} %solid.5) | copy-start | bytes 24580
  8.0 4.6 %collective-permute-start.2 = (f32[9,8,128]{2,1,0:T(8,128)S(1)}, f32[9,8,128]{2,1,0:T(8,128)S(1)}, u32[]{:S(2)}, u32[]{:S(2)}) collective-permute-start(f32[9,8,128]{2,1,0:T(8,128)S(1)} %get-tuple-element.41), channel_id=1, source_target_pairs={{0,8},{8,0},{16,24},{24,16},{1,9},{9,1},{17,25},{25,17},{2,10},{10... | collective-permute-start | bytes 110600 | tf_op jit(solution)/shard_map/ppermute | solution.py:668
  8.1 4.2 %collective-permute-start.3 = (f32[8,8,128]{2,1,0:T(8,128)S(1)}, f32[8,8,128]{2,1,0:T(8,128)S(1)}, u32[]{:S(2)}, u32[]{:S(2)}) collective-permute-start(f32[8,8,128]{2,1,0:T(8,128)S(1)} %get-tuple-element.42.refs_1_), channel_id=1, source_target_pairs={{0,16},{8,24},{16,0},{24,8},{1,17},{9,25},{17,1},{25,9},{2,18},{10... | collective-permute-start | bytes 98312 | tf_op jit(solution)/shard_map/ppermute | solution.py:668
  10.4 3.6 %collective-permute-start.8 = (f32[5,8,128]{2,1,0:T(8,128)S(1)}, f32[5,8,128]{2,1,0:T(8,128)S(1)}, u32[]{:S(2)}, u32[]{:S(2)}) collective-permute-start(f32[5,8,128]{2,1,0:T(8,128)S(1)} %get-tuple-element.47.refs_0_), channel_id=1, source_target_pairs={{0,24},{8,16},{16,8},{24,0},{1,25},{9,17},{17,9},{25,1},{2,26},{10... | collective-permute-start | bytes 61448 | tf_op jit(solution)/shard_map/ppermute | solution.py:668
  10.4 3.8 %collective-permute-start.7 = (f32[5,8,128]{2,1,0:T(8,128)S(1)}, f32[5,8,128]{2,1,0:T(8,128)S(1)}, u32[]{:S(2)}, u32[]{:S(2)}) collective-permute-start(f32[5,8,128]{2,1,0:T(8,128)S(1)} %get-tuple-element.47.refs_0_), channel_id=1, source_target_pairs={{0,16},{8,24},{16,0},{24,8},{1,17},{9,25},{17,1},{25,9},{2,18},{10... | collective-permute-start | bytes 61448 | tf_op jit(solution)/shard_map/ppermute | solution.py:668
  12.0 2.3 %collective-permute-start.6 = (f32[5,8,128]{2,1,0:T(8,128)S(1)}, f32[5,8,128]{2,1,0:T(8,128)S(1)}, u32[]{:S(2)}, u32[]{:S(2)}) collective-permute-start(f32[5,8,128]{2,1,0:T(8,128)S(1)} %get-tuple-element.47.refs_0_), channel_id=1, source_target_pairs={{0,8},{8,0},{16,24},{24,16},{1,9},{9,1},{17,25},{25,17},{2,10},{10... | collective-permute-start | bytes 61448 | tf_op jit(solution)/shard_map/ppermute | solution.py:668
  12.3 1.4 %collective-permute-start.4 = (f32[4,8,128]{2,1,0:T(8,128)S(1)}, f32[4,8,128]{2,1,0:T(8,128)S(1)}, u32[]{:S(2)}, u32[]{:S(2)}) collective-permute-start(f32[4,8,128]{2,1,0:T(8,128)S(1)} %get-tuple-element.45), channel_id=1, source_target_pairs={{0,8},{8,0},{16,24},{24,16},{1,9},{9,1},{17,25},{25,17},{2,10},{10... | collective-permute-start | bytes 49160 | tf_op jit(solution)/shard_map/ppermute | solution.py:668
  12.6 1.2 %collective-permute-start.5 = (f32[4,8,128]{2,1,0:T(8,128)S(1)}, f32[4,8,128]{2,1,0:T(8,128)S(1)}, u32[]{:S(2)}, u32[]{:S(2)}) collective-permute-start(f32[4,8,128]{2,1,0:T(8,128)S(1)} %get-tuple-element.46), channel_id=1, source_target_pairs={{0,8},{8,0},{16,24},{24,16},{1,9},{9,1},{17,25},{25,17},{2,10},{10... | collective-permute-start | bytes 49160 | tf_op jit(solution)/shard_map/ppermute | solution.py:668

commit v11 on v10

--- a/solution.py
+++ b/solution.py
@@ -360,7 +360,6 @@
         return second[i, h]
 
     pack_message(high, first_of, second_of, [outer[i] for i in FORWARD + [NPOP]], True)
-    high[WORDS] = jnp.zeros(TILE, jnp.float32)
     pack_message(low, first_of, second_of, [outer[i] for i in BACKWARD + [NPOP]], False)
     arrive(center, 3)
 
@@ -706,7 +705,7 @@
         [
             in_vmem(NPOP + 1, 2, *TILE),
             in_vmem(NPOP, 2, *TILE),
-            in_vmem(WORDS + 1, *TILE),
+            in_vmem(WORDS, *TILE),
             in_vmem(WORDS, *TILE),
             in_vmem(NPOP, ROWS, 2 * LANES),
             in_vmem(*fine_solid.shape[1:]),

time: 15.3 us -> 15.3 us (level)
    ppermute x1, waiting for transfers between devices: 0.29 us -> 0.01 us  [per_device(): above = lax.ppermute(low, 'blk', backward)]
    ppermute x1, waiting for transfers between devices: 0.01 us -> 0.23 us  [per_device(): below = lax.ppermute(high, 'blk', forward)]
  transfers between devices with their start and end apart: 9 -> 9, of which waited for: 2 -> 3; matrix products, arithmetic and copies ran while one was open for 0% -> 0% of each run, Pallas kernels for 14% -> 14%
where the time goes in v11:
time: 15.3 us; the launch traced here: 15.1 us
  starting transfers between devices  9.64 us (63%)
  Pallas kernels  4.12 us (27%)
  between operations  0.71 us (5%)
  waiting for transfers between devices  0.61 us (4%)
    ppermute x7, starting transfers between devices, exchange(): lax.ppermute(array, 'grp', [(i, i ^ distance) for i in range(groups)])  4.14 us
    pallas_call x9, Pallas kernels, call(): pl.pallas_call(kernel, in_specs=[pl.BlockSpec(memory_space=s) for s in sp...  4.12 us
    ppermute x1, starting transfers between devices, per_device(): below = lax.ppermute(high, 'blk', forward)  3.02 us
    ppermute x1, starting transfers between devices, per_device(): above = lax.ppermute(low, 'blk', backward)  2.48 us
    ppermute x7, waiting for transfers between devices, exchange(): lax.ppermute(array, 'grp', [(i, i ^ distance) for i in range(groups)])  0.36 us
  transfers between devices with their start and end apart: 9, of which 3 were waited for; matrix products, arithmetic and copies ran while one was open for 0% of the time, Pallas kernels for 14%

profile of v11, /device:TPU:0, one launch (start us, length us, event | category | flops | bytes accessed | tf_op | source)
XLA Modules:
  0.0 15.1 jit_solution(15425641370961109432)
XLA Ops:
  0.6 1.2 %pack.1 = (f32[20,2,8,128]{3,2,1,0:T(8,128)S(1)}, f32[19,2,8,128]{3,2,1,0:T(8,128)S(1)}, f32[10,8,128]{2,1,0:T(8,128)S(1)}, f32[10,8,128]{2,1,0:T(8,128)S(1)}, f...) custom-call(f32[1,19,16,256]{3,2,1,0:T(8,128)} %fine.1, f32[1,16,256]{2,1,0:T(8,128)} %solid.3, ...), custom_call_target="tpu_custom_call" | custom-call | bytes 1 | tf_op jit(solution)/shard_map/pack/pallas_call | solution.py:685
  1.8 3.0 %collective-permute-start = (f32[10,8,128]{2,1,0:T(8,128)S(1)}, f32[10,8,128]{2,1,0:T(8,128)S(1)}, u32[]{:S(2)}, u32[]{:S(2)}) collective-permute-start(f32[10,8,128]{2,1,0:T(8,128)S(1)} %get-tuple-element.36), channel_id=1, source_target_pairs={{0,1},{1,2},{2,3},{3,4},{4,5},{5,6},{6,7},{7,0},{8,9},{9,10},{10,1... | collective-permute-start | bytes 122888 | tf_op jit(solution)/shard_map/ppermute | solution.py:738
  4.8 0.6 %early.1 = (f32[19,2,16,128]{3,2,1,0:T(8,128)S(1)}, f32[8,8,128]{2,1,0:T(8,128)S(1)}, f32[4,4,8,128]{3,2,1,0:T(8,128)S(1)}, bf16[256,128]{1,0:T(8,128)(2,1)S(1)}, f32[10,8,128]{2,1,0:T(8,128)S(1)}) custom-call(f32[19,8,256]{2,1,0:T(8,128)S(1)} %get-tuple-element.25.center, f32[16,256]{1,0:T(8,128)S(1)} %get-tuple-element.26.solid, ...), custom_call_target="tpu_custom_call" | custom-call | bytes 1 | tf_op jit(solution)/shard_map/early/pallas_call | solution.py:685
  5.5 2.5 %collective-permute-start.1 = (f32[10,8,128]{2,1,0:T(8,128)S(1)}, f32[10,8,128]{2,1,0:T(8,128)S(1)}, u32[]{:S(2)}, u32[]{:S(2)}) collective-permute-start(f32[10,8,128]{2,1,0:T(8,128)S(1)} %get-tuple-element.37), channel_id=1, source_target_pairs={{0,7},{1,0},{2,1},{3,2},{4,3},{5,4},{6,5},{7,6},{8,15},{9,8},{10,9... | collective-permute-start | bytes 122888 | tf_op jit(solution)/shard_map/ppermute | solution.py:739
  7.9 0.0 copy-start
  7.9 0.0 copy-start.1
  8.0 0.1 collective-permute-start.2
  8.1 1.6 %collective-permute-start.3 = (f32[8,8,128]{2,1,0:T(8,128)S(1)}, f32[8,8,128]{2,1,0:T(8,128)S(1)}, u32[]{:S(2)}, u32[]{:S(2)}) collective-permute-start(f32[8,8,128]{2,1,0:T(8,128)S(1)} %get-tuple-element.42.refs_1_), channel_id=1, source_target_pairs={{0,16},{8,24},{16,0},{24,8},{1,17},{9,25},{17,1},{25,9},{2,18},{10... | collective-permute-start | bytes 98312 | tf_op jit(solution)/shard_map/ppermute | solution.py:667
  9.7 0.2 %collective-permute-done.below = f32[10,8,128]{2,1,0:T(8,128)S(1)} collective-permute-done((f32[10,8,128]{2,1,0:T(8,128)S(1)}, f32[10,8,128]{2,1,0:T(8,128)S(1)}, u32[]{:S(2)}, u32[]{:S(2)}) %collective-permute-start) | collective-permute-done | bytes 40992 | tf_op jit(solution)/shard_map/ppermute | solution.py:738
  9.9 0.0 collective-permute-done.1.above
  9.9 0.0 copy-done
  10.0 0.0 copy-done.1
  10.0 0.3 %edge.1 = (f32[19,2,8,128]{3,2,1,0:T(8,128)S(1)}, f32[5,8,128]{2,1,0:T(8,128)S(1)}) custom-call(f32[20,2,8,128]{3,2,1,0:T(8,128)S(1)} %get-tuple-element.27.moved, f32[19,2,8,128]{3,2,1,0:T(8,128)S(1)} %get-tuple-element.35.second, f32[10,8,128]{2,1,0:T(8,128)S(1)} %collective-permute-done.below, f32[10,8,128]{2,1,0:T(8,128)S(1)} %collective-permute-done.1.above, ...), custom_call_target="tpu_custom_call" | custom-call | bytes 1 | tf_op jit(solution)/shard_map/edge/pallas_call | solution.py:685
  10.3 0.1 collective-permute-start.8
  10.4 1.6 %collective-permute-start.7 = (f32[5,8,128]{2,1,0:T(8,128)S(1)}, f32[5,8,128]{2,1,0:T(8,128)S(1)}, u32[]{:S(2)}, u32[]{:S(2)}) collective-permute-start(f32[5,8,128]{2,1,0:T(8,128)S(1)} %get-tuple-element.47.refs_0_), channel_id=1, source_target_pairs={{0,16},{8,24},{16,0},{24,8},{1,17},{9,25},{17,1},{25,9},{2,18},{10... | collective-permute-start | bytes 61448 | tf_op jit(solution)/shard_map/ppermute | solution.py:667
  12.0 0.2 %collective-permute-start.6 = (f32[5,8,128]{2,1,0:T(8,128)S(1)}, f32[5,8,128]{2,1,0:T(8,128)S(1)}, u32[]{:S(2)}, u32[]{:S(2)}) collective-permute-start(f32[5,8,128]{2,1,0:T(8,128)S(1)} %get-tuple-element.47.refs_0_), channel_id=1, source_target_pairs={{0,8},{8,0},{16,24},{24,16},{1,9},{9,1},{17,25},{25,17},{2,10},{10... | collective-permute-start | bytes 61448 | tf_op jit(solution)/shard_map/ppermute | solution.py:667
  12.2 0.0 collective-permute-done.3.refs_2_.tiles
  12.2 0.3 %collective-permute-start.4 = (f32[4,8,128]{2,1,0:T(8,128)S(1)}, f32[4,8,128]{2,1,0:T(8,128)S(1)}, u32[]{:S(2)}, u32[]{:S(2)}) collective-permute-start(f32[4,8,128]{2,1,0:T(8,128)S(1)} %get-tuple-element.45), channel_id=1, source_target_pairs={{0,8},{8,0},{16,24},{24,16},{1,9},{9,1},{17,25},{25,17},{2,10},{10... | collective-permute-start | bytes 49160 | tf_op jit(solution)/shard_map/ppermute | solution.py:667
  12.5 0.0 collective-permute-done.2.refs_0_
  12.5 0.2 %collective-permute-start.5 = (f32[4,8,128]{2,1,0:T(8,128)S(1)}, f32[4,8,128]{2,1,0:T(8,128)S(1)}, u32[]{:S(2)}, u32[]{:S(2)}) collective-permute-start(f32[4,8,128]{2,1,0:T(8,128)S(1)} %get-tuple-element.46), channel_id=1, source_target_pairs={{0,8},{8,0},{16,24},{24,16},{1,9},{9,1},{17,25},{25,17},{2,10},{10... | collective-permute-start | bytes 49160 | tf_op jit(solution)/shard_map/ppermute | solution.py:667
  12.8 0.8 %write.1.after = f32[1,19,16,256]{3,2,1,0:T(8,128)} custom-call(f32[19,2,16,128]{3,2,1,0:T(8,128)S(1)} %get-tuple-element.34.inner, f32[19,2,8,128]{3,2,1,0:T(8,128)S(1)} %get-tuple-element.39.edges.after), custom_call_target="tpu_custom_call" | custom-call | bytes 1 | tf_op jit(solution)/shard_map/write/pallas_call | solution.py:685
  13.5 0.1 paste.1
  13.6 0.0 collective-permute-done.4.refs_0_
  13.6 0.1 collective-permute-done.5.refs_1_
  13.7 0.2 %coarse.7.middle = f32[19,2,8,128]{3,2,1,0:T(8,128)S(1)} custom-call(f32[1,19,16,256]{3,2,1,0:T(8,128)} %write.1.after, f32[19,2,8,128]{3,2,1,0:T(8,128)S(1)} %get-tuple-element.44.base, f32[1,8,256]{2,1,0:T(8,128)S(1)} %copy-done.1, f32[4,4,8,128]{3,2,1,0:T(8,128)S(1)} %get-tuple-element.40.chosen, f32[4,8,128]{2,1,0:T(8,128)S(1)} %collective-permute-done.4.refs_0_, ...), custom_call_target="tpu_custom_call" | custom-call | bytes 1 | tf_op jit(solution)/shard_map/coarse/pallas_call | solution.py:685
  13.9 0.0 collective-permute-done.8.refs_3_
  13.9 0.3 %collective-permute-done.7.refs_2_ = f32[5,8,128]{2,1,0:T(8,128)S(1)} collective-permute-done((f32[5,8,128]{2,1,0:T(8,128)S(1)}, f32[5,8,128]{2,1,0:T(8,128)S(1)}, u32[]{:S(2)}, u32[]{:S(2)}) %collective-permute-start.7) | collective-permute-done | bytes 20512 | tf_op jit(solution)/shard_map/ppermute | solution.py:667
  14.2 0.0 collective-permute-done.6.refs_1_
  14.2 0.8 %last.1 = f32[1,19,8,256]{3,2,1,0:T(8,128)} custom-call(f32[4,4,8,128]{3,2,1,0:T(8,128)S(1)} %get-tuple-element.40.chosen, f32[10,8,128]{2,1,0:T(8,128)S(1)} %collective-permute-done.below, f32[10,8,128]{2,1,0:T(8,128)S(1)} %collective-permute-done.1.above, f32[20,8,128]{2,1,0:T(8,128)S(1)} %get-tuple-element.43.base, f32[19,2,8,128]{3,2,1,0:T(8,128)S(1)} %coarse.7.middle, ...), custom_call_target="tpu_custom_call" | custom-call | bytes 1 | tf_op jit(solution)/shard_map/last/pallas_call | solution.py:685
  (2 shorter events, 0.0 us)
Async XLA Ops:
  1.8 8.1 %collective-permute-start = (f32[10,8,128]{2,1,0:T(8,128)S(1)}, f32[10,8,128]{2,1,0:T(8,128)S(1)}, u32[]{:S(2)}, u32[]{:S(2)}) collective-permute-start(f32[10,8,128]{2,1,0:T(8,128)S(1)} %get-tuple-element.36), channel_id=1, source_target_pairs={{0,1},{1,2},{2,3},{3,4},{4,5},{5,6},{6,7},{7,0},{8,9},{9,10},{10,1... | collective-permute-start | bytes 122888 | tf_op jit(solution)/shard_map/ppermute | solution.py:738
  5.5 4.5 %collective-permute-start.1 = (f32[10,8,128]{2,1,0:T(8,128)S(1)}, f32[10,8,128]{2,1,0:T(8,128)S(1)}, u32[]{:S(2)}, u32[]{:S(2)}) collective-permute-start(f32[10,8,128]{2,1,0:T(8,128)S(1)} %get-tuple-element.37), channel_id=1, source_target_pairs={{0,7},{1,0},{2,1},{3,2},{4,3},{5,4},{6,5},{7,6},{8,15},{9,8},{10,9... | collective-permute-start | bytes 122888 | tf_op jit(solution)/shard_map/ppermute | solution.py:739
  7.9 2.0 %copy-start = (f32[1,19,8,256]{3,2,1,0:T(8,128)S(1)}, f32[1,19,8,256]{3,2,1,0:T(8,128)}, u32[]{:S(2)}) copy-start(f32[1,19,8,256]{3,2,1,0:T(8,128)} %coarse.6) | copy-start | bytes 466948
  7.9 2.0 %copy-start.1 = (f32[1,8,256]{2,1,0:T(8,128)S(1)}, f32[1,8,256]{2,1,0:T(8,128)}, u32[]{:S(2)}) copy-start(f32[1,8,256]{2,1,0:T(8,128)} %solid.5) | copy-start | bytes 24580
  8.0 4.5 %collective-permute-start.2 = (f32[9,8,128]{2,1,0:T(8,128)S(1)}, f32[9,8,128]{2,1,0:T(8,128)S(1)}, u32[]{:S(2)}, u32[]{:S(2)}) collective-permute-start(f32[9,8,128]{2,1,0:T(8,128)S(1)} %get-tuple-element.41), channel_id=1, source_target_pairs={{0,8},{8,0},{16,24},{24,16},{1,9},{9,1},{17,25},{25,17},{2,10},{10... | collective-permute-start | bytes 110600 | tf_op jit(solution)/shard_map/ppermute | solution.py:667
  8.1 4.2 %collective-permute-start.3 = (f32[8,8,128]{2,1,0:T(8,128)S(1)}, f32[8,8,128]{2,1,0:T(8,128)S(1)}, u32[]{:S(2)}, u32[]{:S(2)}) collective-permute-start(f32[8,8,128]{2,1,0:T(8,128)S(1)} %get-tuple-element.42.refs_1_), channel_id=1, source_target_pairs={{0,16},{8,24},{16,0},{24,8},{1,17},{9,25},{17,1},{25,9},{2,18},{10... | collective-permute-start | bytes 98312 | tf_op jit(solution)/shard_map/ppermute | solution.py:667
  10.3 3.6 %collective-permute-start.8 = (f32[5,8,128]{2,1,0:T(8,128)S(1)}, f32[5,8,128]{2,1,0:T(8,128)S(1)}, u32[]{:S(2)}, u32[]{:S(2)}) collective-permute-start(f32[5,8,128]{2,1,0:T(8,128)S(1)} %get-tuple-element.47.refs_0_), channel_id=1, source_target_pairs={{0,24},{8,16},{16,8},{24,0},{1,25},{9,17},{17,9},{25,1},{2,26},{10... | collective-permute-start | bytes 61448 | tf_op jit(solution)/shard_map/ppermute | solution.py:667
  10.4 3.8 %collective-permute-start.7 = (f32[5,8,128]{2,1,0:T(8,128)S(1)}, f32[5,8,128]{2,1,0:T(8,128)S(1)}, u32[]{:S(2)}, u32[]{:S(2)}) collective-permute-start(f32[5,8,128]{2,1,0:T(8,128)S(1)} %get-tuple-element.47.refs_0_), channel_id=1, source_target_pairs={{0,16},{8,24},{16,0},{24,8},{1,17},{9,25},{17,1},{25,9},{2,18},{10... | collective-permute-start | bytes 61448 | tf_op jit(solution)/shard_map/ppermute | solution.py:667
  12.0 2.2 %collective-permute-start.6 = (f32[5,8,128]{2,1,0:T(8,128)S(1)}, f32[5,8,128]{2,1,0:T(8,128)S(1)}, u32[]{:S(2)}, u32[]{:S(2)}) collective-permute-start(f32[5,8,128]{2,1,0:T(8,128)S(1)} %get-tuple-element.47.refs_0_), channel_id=1, source_target_pairs={{0,8},{8,0},{16,24},{24,16},{1,9},{9,1},{17,25},{25,17},{2,10},{10... | collective-permute-start | bytes 61448 | tf_op jit(solution)/shard_map/ppermute | solution.py:667
  12.2 1.4 %collective-permute-start.4 = (f32[4,8,128]{2,1,0:T(8,128)S(1)}, f32[4,8,128]{2,1,0:T(8,128)S(1)}, u32[]{:S(2)}, u32[]{:S(2)}) collective-permute-start(f32[4,8,128]{2,1,0:T(8,128)S(1)} %get-tuple-element.45), channel_id=1, source_target_pairs={{0,8},{8,0},{16,24},{24,16},{1,9},{9,1},{17,25},{25,17},{2,10},{10... | collective-permute-start | bytes 49160 | tf_op jit(solution)/shard_map/ppermute | solution.py:667
  12.5 1.2 %collective-permute-start.5 = (f32[4,8,128]{2,1,0:T(8,128)S(1)}, f32[4,8,128]{2,1,0:T(8,128)S(1)}, u32[]{:S(2)}, u32[]{:S(2)}) collective-permute-start(f32[4,8,128]{2,1,0:T(8,128)S(1)} %get-tuple-element.46), channel_id=1, source_target_pairs={{0,8},{8,0},{16,24},{24,16},{1,9},{9,1},{17,25},{25,17},{2,10},{10... | collective-permute-start | bytes 49160 | tf_op jit(solution)/shard_map/ppermute | solution.py:667

commit v12 on v11

--- a/solution.py
+++ b/solution.py
@@ -599,7 +599,7 @@
             out[i, h] = f[h][i]
 
 
-CHUNKS = (0, 3, 6, 9, 12, 15, 17, NPOP)
+CHUNKS = (0, 1, 3, 5, 7, 9, 11, 13, 15, 17, 18, NPOP)
 
 
 def last_kernel(chosen, below, above, base, middle, *refs):

time: 15.3 us -> 15.2 us (level)
  no operation moved by 1% of the time
where the time goes in v12:
time: 15.2 us; the launch traced here: 15.1 us
  starting transfers between devices  9.64 us (63%)
  Pallas kernels  4.11 us (27%)
  between operations  0.71 us (5%)
  waiting for transfers between devices  0.61 us (4%)
    ppermute x7, starting transfers between devices, exchange(): lax.ppermute(array, 'grp', [(i, i ^ distance) for i in range(groups)])  4.14 us
    pallas_call x9, Pallas kernels, call(): pl.pallas_call(kernel, in_specs=[pl.BlockSpec(memory_space=s) for s in sp...  4.11 us
    ppermute x1, starting transfers between devices, per_device(): below = lax.ppermute(high, 'blk', forward)  3.02 us
    ppermute x1, starting transfers between devices, per_device(): above = lax.ppermute(low, 'blk', backward)  2.48 us
    ppermute x7, waiting for transfers between devices, exchange(): lax.ppermute(array, 'grp', [(i, i ^ distance) for i in range(groups)])  0.36 us
  transfers between devices with their start and end apart: 9, of which 3 were waited for; matrix products, arithmetic and copies ran while one was open for 0% of the time, Pallas kernels for 14%

profile of v12, /device:TPU:0, one launch (start us, length us, event | category | flops | bytes accessed | tf_op | source)
XLA Modules:
  0.0 15.1 jit_solution(97451276619703182)
XLA Ops:
  0.6 1.2 %pack.1 = (f32[20,2,8,128]{3,2,1,0:T(8,128)S(1)}, f32[19,2,8,128]{3,2,1,0:T(8,128)S(1)}, f32[10,8,128]{2,1,0:T(8,128)S(1)}, f32[10,8,128]{2,1,0:T(8,128)S(1)}, f...) custom-call(f32[1,19,16,256]{3,2,1,0:T(8,128)} %fine.1, f32[1,16,256]{2,1,0:T(8,128)} %solid.3, ...), custom_call_target="tpu_custom_call" | custom-call | bytes 1 | tf_op jit(solution)/shard_map/pack/pallas_call | solution.py:685
  1.8 3.0 %collective-permute-start = (f32[10,8,128]{2,1,0:T(8,128)S(1)}, f32[10,8,128]{2,1,0:T(8,128)S(1)}, u32[]{:S(2)}, u32[]{:S(2)}) collective-permute-start(f32[10,8,128]{2,1,0:T(8,128)S(1)} %get-tuple-element.36), channel_id=1, source_target_pairs={{0,1},{1,2},{2,3},{3,4},{4,5},{5,6},{6,7},{7,0},{8,9},{9,10},{10,1... | collective-permute-start | bytes 122888 | tf_op jit(solution)/shard_map/ppermute | solution.py:738
  4.8 0.6 %early.1 = (f32[19,2,16,128]{3,2,1,0:T(8,128)S(1)}, f32[8,8,128]{2,1,0:T(8,128)S(1)}, f32[4,4,8,128]{3,2,1,0:T(8,128)S(1)}, bf16[256,128]{1,0:T(8,128)(2,1)S(1)}, f32[10,8,128]{2,1,0:T(8,128)S(1)}) custom-call(f32[19,8,256]{2,1,0:T(8,128)S(1)} %get-tuple-element.25.center, f32[16,256]{1,0:T(8,128)S(1)} %get-tuple-element.26.solid, ...), custom_call_target="tpu_custom_call" | custom-call | bytes 1 | tf_op jit(solution)/shard_map/early/pallas_call | solution.py:685
  5.5 2.5 %collective-permute-start.1 = (f32[10,8,128]{2,1,0:T(8,128)S(1)}, f32[10,8,128]{2,1,0:T(8,128)S(1)}, u32[]{:S(2)}, u32[]{:S(2)}) collective-permute-start(f32[10,8,128]{2,1,0:T(8,128)S(1)} %get-tuple-element.37), channel_id=1, source_target_pairs={{0,7},{1,0},{2,1},{3,2},{4,3},{5,4},{6,5},{7,6},{8,15},{9,8},{10,9... | collective-permute-start | bytes 122888 | tf_op jit(solution)/shard_map/ppermute | solution.py:739
  7.9 0.0 copy-start
  7.9 0.0 copy-start.1
  8.0 0.1 collective-permute-start.2
  8.1 1.6 %collective-permute-start.3 = (f32[8,8,128]{2,1,0:T(8,128)S(1)}, f32[8,8,128]{2,1,0:T(8,128)S(1)}, u32[]{:S(2)}, u32[]{:S(2)}) collective-permute-start(f32[8,8,128]{2,1,0:T(8,128)S(1)} %get-tuple-element.42.refs_1_), channel_id=1, source_target_pairs={{0,16},{8,24},{16,0},{24,8},{1,17},{9,25},{17,1},{25,9},{2,18},{10... | collective-permute-start | bytes 98312 | tf_op jit(solution)/shard_map/ppermute | solution.py:667
  9.7 0.2 %collective-permute-done.below = f32[10,8,128]{2,1,0:T(8,128)S(1)} collective-permute-done((f32[10,8,128]{2,1,0:T(8,128)S(1)}, f32[10,8,128]{2,1,0:T(8,128)S(1)}, u32[]{:S(2)}, u32[]{:S(2)}) %collective-permute-start) | collective-permute-done | bytes 40992 | tf_op jit(solution)/shard_map/ppermute | solution.py:738
  9.9 0.0 collective-permute-done.1.above
  9.9 0.0 copy-done
  10.0 0.0 copy-done.1
  10.0 0.3 %edge.1 = (f32[19,2,8,128]{3,2,1,0:T(8,128)S(1)}, f32[5,8,128]{2,1,0:T(8,128)S(1)}) custom-call(f32[20,2,8,128]{3,2,1,0:T(8,128)S(1)} %get-tuple-element.27.moved, f32[19,2,8,128]{3,2,1,0:T(8,128)S(1)} %get-tuple-element.35.second, f32[10,8,128]{2,1,0:T(8,128)S(1)} %collective-permute-done.below, f32[10,8,128]{2,1,0:T(8,128)S(1)} %collective-permute-done.1.above, ...), custom_call_target="tpu_custom_call" | custom-call | bytes 1 | tf_op jit(solution)/shard_map/edge/pallas_call | solution.py:685
  10.3 0.1 collective-permute-start.8
  10.4 1.6 %collective-permute-start.7 = (f32[5,8,128]{2,1,0:T(8,128)S(1)}, f32[5,8,128]{2,1,0:T(8,128)S(1)}, u32[]{:S(2)}, u32[]{:S(2)}) collective-permute-start(f32[5,8,128]{2,1,0:T(8,128)S(1)} %get-tuple-element.47.refs_0_), channel_id=1, source_target_pairs={{0,16},{8,24},{16,0},{24,8},{1,17},{9,25},{17,1},{25,9},{2,18},{10... | collective-permute-start | bytes 61448 | tf_op jit(solution)/shard_map/ppermute | solution.py:667
  12.0 0.2 %collective-permute-start.6 = (f32[5,8,128]{2,1,0:T(8,128)S(1)}, f32[5,8,128]{2,1,0:T(8,128)S(1)}, u32[]{:S(2)}, u32[]{:S(2)}) collective-permute-start(f32[5,8,128]{2,1,0:T(8,128)S(1)} %get-tuple-element.47.refs_0_), channel_id=1, source_target_pairs={{0,8},{8,0},{16,24},{24,16},{1,9},{9,1},{17,25},{25,17},{2,10},{10... | collective-permute-start | bytes 61448 | tf_op jit(solution)/shard_map/ppermute | solution.py:667
  12.2 0.0 collective-permute-done.3.refs_2_.tiles
  12.2 0.3 %collective-permute-start.4 = (f32[4,8,128]{2,1,0:T(8,128)S(1)}, f32[4,8,128]{2,1,0:T(8,128)S(1)}, u32[]{:S(2)}, u32[]{:S(2)}) collective-permute-start(f32[4,8,128]{2,1,0:T(8,128)S(1)} %get-tuple-element.45), channel_id=1, source_target_pairs={{0,8},{8,0},{16,24},{24,16},{1,9},{9,1},{17,25},{25,17},{2,10},{10... | collective-permute-start | bytes 49160 | tf_op jit(solution)/shard_map/ppermute | solution.py:667
  12.5 0.0 collective-permute-done.2.refs_0_
  12.5 0.2 %collective-permute-start.5 = (f32[4,8,128]{2,1,0:T(8,128)S(1)}, f32[4,8,128]{2,1,0:T(8,128)S(1)}, u32[]{:S(2)}, u32[]{:S(2)}) collective-permute-start(f32[4,8,128]{2,1,0:T(8,128)S(1)} %get-tuple-element.46), channel_id=1, source_target_pairs={{0,8},{8,0},{16,24},{24,16},{1,9},{9,1},{17,25},{25,17},{2,10},{10... | collective-permute-start | bytes 49160 | tf_op jit(solution)/shard_map/ppermute | solution.py:667
  12.8 0.8 %write.1.after = f32[1,19,16,256]{3,2,1,0:T(8,128)} custom-call(f32[19,2,16,128]{3,2,1,0:T(8,128)S(1)} %get-tuple-element.34.inner, f32[19,2,8,128]{3,2,1,0:T(8,128)S(1)} %get-tuple-element.39.edges.after), custom_call_target="tpu_custom_call" | custom-call | bytes 1 | tf_op jit(solution)/shard_map/write/pallas_call | solution.py:685
  13.5 0.1 paste.1
  13.6 0.0 collective-permute-done.4.refs_0_
  13.6 0.1 collective-permute-done.5.refs_1_
  13.7 0.2 %coarse.7.middle = f32[19,2,8,128]{3,2,1,0:T(8,128)S(1)} custom-call(f32[1,19,16,256]{3,2,1,0:T(8,128)} %write.1.after, f32[19,2,8,128]{3,2,1,0:T(8,128)S(1)} %get-tuple-element.44.base, f32[1,8,256]{2,1,0:T(8,128)S(1)} %copy-done.1, f32[4,4,8,128]{3,2,1,0:T(8,128)S(1)} %get-tuple-element.40.chosen, f32[4,8,128]{2,1,0:T(8,128)S(1)} %collective-permute-done.4.refs_0_, ...), custom_call_target="tpu_custom_call" | custom-call | bytes 1 | tf_op jit(solution)/shard_map/coarse/pallas_call | solution.py:685
  13.9 0.0 collective-permute-done.8.refs_3_
  13.9 0.3 %collective-permute-done.7.refs_2_ = f32[5,8,128]{2,1,0:T(8,128)S(1)} collective-permute-done((f32[5,8,128]{2,1,0:T(8,128)S(1)}, f32[5,8,128]{2,1,0:T(8,128)S(1)}, u32[]{:S(2)}, u32[]{:S(2)}) %collective-permute-start.7) | collective-permute-done | bytes 20512 | tf_op jit(solution)/shard_map/ppermute | solution.py:667
  14.2 0.0 collective-permute-done.6.refs_1_
  14.2 0.8 %last.1 = f32[1,19,8,256]{3,2,1,0:T(8,128)} custom-call(f32[4,4,8,128]{3,2,1,0:T(8,128)S(1)} %get-tuple-element.40.chosen, f32[10,8,128]{2,1,0:T(8,128)S(1)} %collective-permute-done.below, f32[10,8,128]{2,1,0:T(8,128)S(1)} %collective-permute-done.1.above, f32[20,8,128]{2,1,0:T(8,128)S(1)} %get-tuple-element.43.base, f32[19,2,8,128]{3,2,1,0:T(8,128)S(1)} %coarse.7.middle, ...), custom_call_target="tpu_custom_call" | custom-call | bytes 1 | tf_op jit(solution)/shard_map/last/pallas_call | solution.py:685
  (2 shorter events, 0.0 us)
Async XLA Ops:
  1.8 8.1 %collective-permute-start = (f32[10,8,128]{2,1,0:T(8,128)S(1)}, f32[10,8,128]{2,1,0:T(8,128)S(1)}, u32[]{:S(2)}, u32[]{:S(2)}) collective-permute-start(f32[10,8,128]{2,1,0:T(8,128)S(1)} %get-tuple-element.36), channel_id=1, source_target_pairs={{0,1},{1,2},{2,3},{3,4},{4,5},{5,6},{6,7},{7,0},{8,9},{9,10},{10,1... | collective-permute-start | bytes 122888 | tf_op jit(solution)/shard_map/ppermute | solution.py:738
  5.5 4.5 %collective-permute-start.1 = (f32[10,8,128]{2,1,0:T(8,128)S(1)}, f32[10,8,128]{2,1,0:T(8,128)S(1)}, u32[]{:S(2)}, u32[]{:S(2)}) collective-permute-start(f32[10,8,128]{2,1,0:T(8,128)S(1)} %get-tuple-element.37), channel_id=1, source_target_pairs={{0,7},{1,0},{2,1},{3,2},{4,3},{5,4},{6,5},{7,6},{8,15},{9,8},{10,9... | collective-permute-start | bytes 122888 | tf_op jit(solution)/shard_map/ppermute | solution.py:739
  7.9 2.0 %copy-start = (f32[1,19,8,256]{3,2,1,0:T(8,128)S(1)}, f32[1,19,8,256]{3,2,1,0:T(8,128)}, u32[]{:S(2)}) copy-start(f32[1,19,8,256]{3,2,1,0:T(8,128)} %coarse.6) | copy-start | bytes 466948
  7.9 2.0 %copy-start.1 = (f32[1,8,256]{2,1,0:T(8,128)S(1)}, f32[1,8,256]{2,1,0:T(8,128)}, u32[]{:S(2)}) copy-start(f32[1,8,256]{2,1,0:T(8,128)} %solid.5) | copy-start | bytes 24580
  8.0 4.5 %collective-permute-start.2 = (f32[9,8,128]{2,1,0:T(8,128)S(1)}, f32[9,8,128]{2,1,0:T(8,128)S(1)}, u32[]{:S(2)}, u32[]{:S(2)}) collective-permute-start(f32[9,8,128]{2,1,0:T(8,128)S(1)} %get-tuple-element.41), channel_id=1, source_target_pairs={{0,8},{8,0},{16,24},{24,16},{1,9},{9,1},{17,25},{25,17},{2,10},{10... | collective-permute-start | bytes 110600 | tf_op jit(solution)/shard_map/ppermute | solution.py:667
  8.1 4.2 %collective-permute-start.3 = (f32[8,8,128]{2,1,0:T(8,128)S(1)}, f32[8,8,128]{2,1,0:T(8,128)S(1)}, u32[]{:S(2)}, u32[]{:S(2)}) collective-permute-start(f32[8,8,128]{2,1,0:T(8,128)S(1)} %get-tuple-element.42.refs_1_), channel_id=1, source_target_pairs={{0,16},{8,24},{16,0},{24,8},{1,17},{9,25},{17,1},{25,9},{2,18},{10... | collective-permute-start | bytes 98312 | tf_op jit(solution)/shard_map/ppermute | solution.py:667
  10.3 3.6 %collective-permute-start.8 = (f32[5,8,128]{2,1,0:T(8,128)S(1)}, f32[5,8,128]{2,1,0:T(8,128)S(1)}, u32[]{:S(2)}, u32[]{:S(2)}) collective-permute-start(f32[5,8,128]{2,1,0:T(8,128)S(1)} %get-tuple-element.47.refs_0_), channel_id=1, source_target_pairs={{0,24},{8,16},{16,8},{24,0},{1,25},{9,17},{17,9},{25,1},{2,26},{10... | collective-permute-start | bytes 61448 | tf_op jit(solution)/shard_map/ppermute | solution.py:667
  10.4 3.8 %collective-permute-start.7 = (f32[5,8,128]{2,1,0:T(8,128)S(1)}, f32[5,8,128]{2,1,0:T(8,128)S(1)}, u32[]{:S(2)}, u32[]{:S(2)}) collective-permute-start(f32[5,8,128]{2,1,0:T(8,128)S(1)} %get-tuple-element.47.refs_0_), channel_id=1, source_target_pairs={{0,16},{8,24},{16,0},{24,8},{1,17},{9,25},{17,1},{25,9},{2,18},{10... | collective-permute-start | bytes 61448 | tf_op jit(solution)/shard_map/ppermute | solution.py:667
  12.0 2.2 %collective-permute-start.6 = (f32[5,8,128]{2,1,0:T(8,128)S(1)}, f32[5,8,128]{2,1,0:T(8,128)S(1)}, u32[]{:S(2)}, u32[]{:S(2)}) collective-permute-start(f32[5,8,128]{2,1,0:T(8,128)S(1)} %get-tuple-element.47.refs_0_), channel_id=1, source_target_pairs={{0,8},{8,0},{16,24},{24,16},{1,9},{9,1},{17,25},{25,17},{2,10},{10... | collective-permute-start | bytes 61448 | tf_op jit(solution)/shard_map/ppermute | solution.py:667
  12.2 1.4 %collective-permute-start.4 = (f32[4,8,128]{2,1,0:T(8,128)S(1)}, f32[4,8,128]{2,1,0:T(8,128)S(1)}, u32[]{:S(2)}, u32[]{:S(2)}) collective-permute-start(f32[4,8,128]{2,1,0:T(8,128)S(1)} %get-tuple-element.45), channel_id=1, source_target_pairs={{0,8},{8,0},{16,24},{24,16},{1,9},{9,1},{17,25},{25,17},{2,10},{10... | collective-permute-start | bytes 49160 | tf_op jit(solution)/shard_map/ppermute | solution.py:667
  12.5 1.2 %collective-permute-start.5 = (f32[4,8,128]{2,1,0:T(8,128)S(1)}, f32[4,8,128]{2,1,0:T(8,128)S(1)}, u32[]{:S(2)}, u32[]{:S(2)}) collective-permute-start(f32[4,8,128]{2,1,0:T(8,128)S(1)} %get-tuple-element.46), channel_id=1, source_target_pairs={{0,8},{8,0},{16,24},{24,16},{1,9},{9,1},{17,25},{25,17},{2,10},{10... | collective-permute-start | bytes 49160 | tf_op jit(solution)/shard_map/ppermute | solution.py:667
